TPU v7x, 128 devices: a whole 4x4x4 slice. The times are simulated.
128 devices in a mesh: head: 8 (over y, core), qblk: 16 (over z, x).
Axes of the slice: x: 4, y: 4, z: 4, core: 2. Of those that a mesh axis runs over, the one named last changes fastest.
Arguments:
- q_absorbed: bfloat16 [4096, 128, 576], P('qblk', 'head'), may hold values from -64 to 64
- key_cache: bfloat16 [512, 704, 128], P('qblk'), may hold values from -8 to 8
- index_input: bfloat16 [4096, 1536], P('qblk'), may hold values from -6 to 6
- index_weight: bfloat16 [1536, 8192], P(None, 'head'), may hold values from -0.15625 to 0.15625
- head_weights: float32 [4096, 64], P('qblk', 'head'), may hold values from -0.24 to 0.24
- block_ids: int32 [32, 16], replicated, may hold values from 0 to 511, as said below
- block_counts: int32 [32], replicated, may hold values from 1 to 16, as said below
Outputs:
- weight_grad: float32 [1536, 8192], P(None, 'head')
- cross_entropy: float32 [4096], P(('qblk', 'head'))
Inputs may be any that keep to these rules, and one draw needn't show every extreme that they name: `block_ids`: row g holds 16 distinct block numbers; entry 0 is 480 + g and all others are smaller. Of one row's entries at most 3 lie in one run of 32 block numbers starting at a multiple of 32, and in every row some such run holds exactly 3. `block_counts`: in every draw, for some index of qblk all 2 of its query blocks use all 16 slots.
All inputs are finite; a program needn't handle non-finite values.
Results may differ from a plain program's by a relative error of at most 0.03.
The roundings to bfloat16 on the way count: a program that leaves them out, or rounds other values in their place, can miss the bound.
Values may be sent and summed in bfloat16 or wider, within the bound.
No kernel may reach another device: no remote copies, remote signals or barrier semaphores. Data moves between devices by JAX's collectives and lax.ppermute only.
A program may use at most 128 MiB of HBM per device.

v0:
```python
import jax
import jax.numpy as jnp
from jax import lax
from jax.sharding import PartitionSpec as P

H = 128
CAP1 = 3


score_scale = 192.0 ** (-0.5)
masked_value = -1e30


def loss_terms(target, logits, valid, total_queries):
    masked = jnp.where(valid, logits, masked_value)
    peak = jnp.max(masked, axis=1, keepdims=True)
    log_total = peak + jnp.log(jnp.sum(jnp.exp(masked - peak), axis=1, keepdims=True))
    log_probs = masked - log_total
    entropy = -jnp.sum(jnp.where(valid, target * log_probs, 0.0), axis=1)
    logit_grad = jnp.where(valid, jnp.exp(log_probs) - target, 0.0) / total_queries
    return (entropy, logit_grad)


def on_device(
    q_absorbed, key_cache, index_input, index_weight, head_weights, block_ids, block_counts
):
    query_count, local_heads, features = q_absorbed.shape
    shard_blocks, channels, block_len = key_cache.shape
    q_blocks = query_count // block_len
    total_blocks, listed = block_ids.shape
    owners = lax.axis_size("qblk")
    head_count = lax.axis_size("head")
    shard_index = lax.axis_index("qblk")
    head_index = lax.axis_index("head")
    capacity = q_blocks * CAP1
    index_heads = head_weights.shape[1]
    total_queries = total_blocks * block_len
    slot_iota = jnp.arange(listed, dtype=jnp.int32)
    owner_of = block_ids // shard_blocks
    earlier = (owner_of[:, :, None] == owner_of[:, None, :]) & (
        slot_iota[None, None, :] < slot_iota[None, :, None]
    )
    ranking = jnp.sum(earlier.astype(jnp.int32), axis=2)
    slot_of = (jnp.arange(total_blocks, dtype=jnp.int32) % q_blocks)[:, None] * CAP1 + ranking
    local_number = block_ids - shard_index * shard_blocks
    capacity_iota = jnp.arange(capacity, dtype=jnp.int32)
    matches = (owner_of == shard_index)[:, :, None] & (
        slot_of[:, :, None] == capacity_iota[None, None, :]
    )
    slot_table = jnp.where(matches, local_number[:, :, None], 0).reshape(
        owners, q_blocks * listed, capacity
    )
    slot_table = jnp.sum(slot_table, axis=1).reshape(-1)
    my_owner = lax.dynamic_slice_in_dim(owner_of, shard_index * q_blocks, q_blocks, 0)
    my_slot = lax.dynamic_slice_in_dim(slot_of, shard_index * q_blocks, q_blocks, 0)
    flat_index = (my_owner * capacity + my_slot).reshape(-1)
    outgoing = jnp.take(key_cache, slot_table, axis=0).reshape(
        owners, capacity, channels, block_len
    )
    arrived = lax.all_to_all(outgoing, "qblk", split_axis=0, concat_axis=0, tiled=True)
    blocks = jnp.take(arrived.reshape(owners * capacity, channels, block_len), flat_index, axis=0)
    blocks = blocks.reshape(q_blocks, listed, channels, block_len)
    counts_mine = lax.dynamic_slice_in_dim(block_counts, shard_index * q_blocks, q_blocks, 0)
    token_iota = jnp.arange(block_len, dtype=jnp.int32)
    valid = (slot_iota[None, None, :, None] < counts_mine[:, None, None, None]) & (
        (slot_iota[None, None, :, None] > 0)
        | (token_iota[None, None, None, :] <= token_iota[None, :, None, None])
    )
    index_query = jnp.dot(index_input, index_weight, preferred_element_type=jnp.float32).astype(
        jnp.bfloat16
    )
    index_query = index_query.reshape(query_count, index_heads, -1)
    target_tiles = []
    logit_tiles = []
    affinities = []
    for row_block in range(q_blocks):
        rows_start = row_block * block_len
        query_tile = q_absorbed[rows_start : rows_start + block_len]
        latent = blocks[row_block, :, :features, :]
        index_keys = blocks[row_block, :, features:, :]
        scores = (
            jnp.einsum("qhd,sdk->qhsk", query_tile, latent, preferred_element_type=jnp.float32)
            * score_scale
        )
        scores = jnp.where(valid[row_block][:, None], scores, masked_value)
        row_peak = jnp.max(scores, axis=(2, 3), keepdims=True)
        weights_exp = jnp.exp(scores - row_peak)
        attention = weights_exp / jnp.sum(weights_exp, axis=(2, 3), keepdims=True)
        target_tiles.append((jnp.sum(attention, axis=1) / H).reshape(block_len, listed * block_len))
        affinity = jnp.einsum(
            "qjd,sdk->qjsk",
            index_query[rows_start : rows_start + block_len],
            index_keys,
            preferred_element_type=jnp.float32,
        )
        affinities.append(affinity)
        logits = jnp.einsum(
            "qj,qjsk->qsk",
            head_weights[rows_start : rows_start + block_len],
            jnp.maximum(affinity, 0.0),
            precision=lax.Precision.HIGHEST,
        )
        logit_tiles.append(logits.reshape(block_len, listed * block_len))
    targets = jnp.concatenate(target_tiles, axis=0)
    logit_terms = jnp.concatenate(logit_tiles, axis=0)
    valid_flat = valid.reshape(query_count, listed * block_len)
    share = query_count // head_count
    target_all, logit_all = lax.psum((targets, logit_terms), "head")
    entropy_all, logit_grad = loss_terms(target_all, logit_all, valid_flat, total_queries)
    entropy = lax.dynamic_slice_in_dim(entropy_all, head_index * share, share, 0)
    query_grads = []
    for row_block in range(q_blocks):
        rows_start = row_block * block_len
        index_keys = blocks[row_block, :, features:, :]
        grad_tile = logit_grad[rows_start : rows_start + block_len].reshape(
            block_len, listed, block_len
        )
        head_rows = head_weights[rows_start : rows_start + block_len]
        affinity_grad = (
            grad_tile[:, None] * head_rows[:, :, None, None] * (affinities[row_block] > 0)
        ).astype(jnp.bfloat16)
        query_tile_grad = jnp.einsum(
            "qjsk,sdk->qjd", affinity_grad, index_keys, preferred_element_type=jnp.float32
        )
        query_grads.append(query_tile_grad.astype(jnp.bfloat16).reshape(block_len, -1))
    query_grad = jnp.concatenate(query_grads, axis=0)
    local_grad = jnp.einsum(
        "td,tc->dc", index_input, query_grad, preferred_element_type=jnp.float32
    )
    weight_grad = lax.psum(local_grad, "qblk")
    return (weight_grad, entropy)


def solution(mesh):
    placed = (
        P("qblk", "head", None),
        P("qblk", None, None),
        P("qblk", None),
        P(None, "head"),
        P("qblk", "head"),
        P(),
        P(),
    )
    return jax.shard_map(
        on_device,
        mesh=mesh,
        in_specs=placed,
        out_specs=(P(None, "head"), P(("qblk", "head"))),
        check_vma=False,
    )
```

profile of v0, /device:TPU:1, one launch (start us, length us, event | category | flops | bytes accessed | tf_op | source)
XLA Modules:
  0.0 649.3 jit_solution(17676481618783405078)
XLA Ops:
  10.1 11.1 %gather_fusion = bf16[96,704,128]{2,1,0:T(8,128)(2,1)} fusion(bf16[32,704,128]{2,1,0:T(8,128)(2,1)} %param.8, s32[1024]{0:T(1024)S(1)} %pad_clamp_fusion.1), kind=kCustom, calls=%fused_computation | custom fusion | bytes 34603392 | tf_op jit(solution)/shard_map/jit(_take)/gather | solution.py:57
  21.2 14.5 %broadcast_select_fusion = bf16[16,6,704,128]{3,2,1,0:T(8,128)(2,1)} fusion(bf16[16,6,704,128]{3,2,1,0:T(8,128)(2,1)} %bitcast.128, pred[16,6]{1,0:T(8,128)(4,1)S(1)} %copy.77), kind=kLoop, calls=%fused_computation.2 | loop fusion | flops 8650752 | bytes 34603104 | tf_op jit(solution)/shard_map/jit(_take)/select_n | solution.py:57
  35.6 8.5 %all-to-all-start = ((bf16[16,6,704,128]{3,2,1,0:T(8,128)(2,1)}), bf16[16,6,704,128]{3,2,1,0:T(8,128)(2,1)}, u32[]{:S(2)}, u32[]{:S(2)}) async-start(bf16[16,6,704,128]{3,2,1,0:T(8,128)(2,1)} %broadcast_select_fusion), calls=%async_computation | async-start | bytes 34603008 | tf_op jit(solution)/shard_map/all_to_all | solution.py:60
  49.0 2.1 copy.81
  51.2 2.1 convolution_convert_fusion
  55.6 245.3 %all-to-all-done = bf16[16,6,704,128]{3,2,1,0:T(8,128)(2,1)} async-done(((bf16[16,6,704,128]{3,2,1,0:T(8,128)(2,1)}), bf16[16,6,704,128]{3,2,1,0:T(8,128)(2,1)}, u32[]{:S(2)}, u32[]{:S(2)}) %all-to-all-start) | async-done | bytes 17301536 | tf_op jit(solution)/shard_map/all_to_all | solution.py:60
  300.9 9.7 %gather_fusion.1 = bf16[32,704,128]{2,1,0:T(8,128)(2,1)} fusion(bf16[96,704,128]{2,1,0:T(8,128)(2,1)} %bitcast.3, s32[1024]{0:T(1024)S(1)} %pad_clamp_fusion), kind=kCustom, calls=%fused_computation.1 | custom fusion | bytes 11534464 | tf_op jit(solution)/shard_map/jit(_take)/gather | solution.py:61
  310.6 3.4 broadcast_select_fusion.1
  314.6 11.6 %fusion.3 = (f32[128,16]{0,1:T(8,128)S(1)}, f32[16,128,128,16]{2,1,3,0:T(8,128)}) fusion(pred[128,16,128]{0,2,1:T(8,128)(4,1)S(1)} %copy.82, bf16[256,16,576]{0,2,1:T(8,128)(2,1)S(1)} %bitcast.144, bf16[2,16,704,128]{3,2,1,0:T(8,128)(2,1)S(1)} %broadcast_select_fusion.1), kind=kOutput, calls=%fused_computation.12 | convolution fusion | flops 4844419072 | bytes 21766144 | tf_op jit(solution)/shard_map/qhd,sdk->qhsk/dot_general | solution.py:82
  326.2 9.1 %fusion.1 = f32[128,16]{0,1:T(8,128)S(1)} fusion(f32[16,128,128,16]{2,1,3,0:T(8,128)} %get-tuple-element.31, f32[128,16]{0,1:T(8,128)S(1)} %get-tuple-element.30, pred[128,16,128]{0,2,1:T(8,128)(4,1)S(1)} %copy.82), kind=kLoop, calls=%fused_computation.10 | loop fusion | flops 16775168 | bytes 17055744 | tf_op jit(solution)/shard_map/reduce_sum | solution.py:88
  335.3 8.0 %divide_reduce_fusion = f32[128,16,128]{0,2,1:T(8,128)S(1)} fusion(f32[16,128,128,16]{2,1,3,0:T(8,128)} %get-tuple-element.31, f32[128,16]{0,1:T(8,128)S(1)} %fusion.1, f32[128,16]{0,1:T(8,128)S(1)} %get-tuple-element.30, pred[128,16,128]{0,2,1:T(8,128)(4,1)S(1)} %copy.82), kind=kLoop, calls=%fused_computation.7 | loop fusion | flops 20709376 | bytes 18104320 | tf_op jit(solution)/shard_map/reduce_sum | solution.py:89
  343.8 13.1 %fusion.2 = (f32[128,16]{0,1:T(8,128)S(1)}, f32[16,128,128,16]{2,1,3,0:T(8,128)}) fusion(pred[128,16,128]{0,2,1:T(8,128)(4,1)} %copy.81, bf16[256,16,576]{0,2,1:T(8,128)(2,1)} %param.7, bf16[2,16,704,128]{3,2,1,0:T(8,128)(2,1)} %copy-done.4), kind=kOutput, calls=%fused_computation.11 | convolution fusion | flops 4844419072 | bytes 21766144 | tf_op jit(solution)/shard_map/qhd,sdk->qhsk/dot_general | solution.py:82
  356.9 9.1 %fusion = f32[128,16]{0,1:T(8,128)S(1)} fusion(f32[16,128,128,16]{2,1,3,0:T(8,128)} %get-tuple-element.33, f32[128,16]{0,1:T(8,128)S(1)} %get-tuple-element.32, pred[128,16,128]{0,2,1:T(8,128)(4,1)S(1)} %copy-done.5), kind=kLoop, calls=%fused_computation.9 | loop fusion | flops 16775168 | bytes 17055744 | tf_op jit(solution)/shard_map/reduce_sum | solution.py:88
  366.0 8.0 %divide_reduce_fusion.1 = f32[128,16,128]{0,2,1:T(8,128)S(1)} fusion(f32[16,128,128,16]{2,1,3,0:T(8,128)} %get-tuple-element.33, f32[128,16]{0,1:T(8,128)S(1)} %fusion, f32[128,16]{0,1:T(8,128)S(1)} %get-tuple-element.32, pred[128,16,128]{0,2,1:T(8,128)(4,1)S(1)} %copy-done.5), kind=kLoop, calls=%fused_computation.8 | loop fusion | flops 20709376 | bytes 18104320 | tf_op jit(solution)/shard_map/reduce_sum | solution.py:89
  374.4 5.6 broadcast_maximum_fusion
  380.0 5.5 broadcast_maximum_fusion.1
  385.6 1.6 pad_maximum_fusion.1
  387.1 14.7 %fusion.4 = f32[128,1,16,128]{3,1,2,0:T(1,128)S(1)} fusion(f32[128,8,1,1]{1,2,3,0:T(1,128)S(1)} %copy.96, f32[128,8,16,128]{3,0,2,1:T(8,128)S(1)} %get-tuple-element.34), kind=kOutput, calls=%fused_computation.18 | convolution fusion | flops 25165824 | bytes 9441280 | tf_op jit(solution)/shard_map/qj,qjsk->qsk/dot_general | solution.py:97
  401.8 14.9 %fusion.6 = f32[128,1,16,128]{3,1,2,0:T(1,128)S(1)} fusion(f32[128,8,1,1]{1,2,3,0:T(1,128)S(1)} %copy.92, f32[128,8,16,128]{3,0,2,1:T(8,128)S(1)} %get-tuple-element.36), kind=kOutput, calls=%fused_computation.20 | convolution fusion | flops 25165824 | bytes 9441280 | tf_op jit(solution)/shard_map/qj,qjsk->qsk/dot_general | solution.py:97
  417.6 1.6 pad_maximum_fusion
  419.5 5.3 fusion.9
  424.8 4.9 fusion.8
  429.6 59.6 %all-reduce.6.cloned.1.call-done = (f32[256,2048]{1,0:T(8,128)}, f32[256,2048]{1,0:T(8,128)}) async-done(((f32[256,2048]{1,0:T(8,128)}, f32[256,2048]{1,0:T(8,128)}), (f32[256,2048]{1,0:T(8,128)}, f32[256,2048]{1,0:T(8,128)})) %all-reduce.6.cloned.1.call-update) | async-done | bytes 4194320 | tf_op jit(solution)/shard_map/psum | solution.py:108
  489.2 2.0 fusion.20
  491.2 2.2 exponential_reduce_fusion
  493.4 3.3 select_reduce_fusion
  496.8 1.6 fusion.49
  502.1 2.8 fusion.24
  504.9 2.8 fusion.23
  507.7 3.7 convolution_bitcast_fusion
  512.0 123.7 %all-reduce.4.cloned.1.call-done = f32[1536,1024]{0,1:T(8,128)} async-done(((f32[1536,1024]{0,1:T(8,128)}), f32[1536,1024]{0,1:T(8,128)}) %all-reduce.4.cloned.1.call-update) | async-done | bytes 6291472 | tf_op jit(solution)/shard_map/psum | solution.py:130
  635.7 6.6 %copy.89 = f32[1536,1024]{1,0:T(8,128)} copy(f32[1536,1024]{0,1:T(8,128)} %all-reduce.4.cloned.1.call-done) | data formatting | bytes 12582912
  (85 shorter events, 17.0 us)
Async XLA Ops:
  7.2 44.0 %copy-start = (bf16[1536,1024]{1,0:T(8,128)(2,1)S(1)}, bf16[1536,1024]{1,0:T(8,128)(2,1)}, u32[]{:S(2)}) copy-start(bf16[1536,1024]{1,0:T(8,128)(2,1)} %param.10) | copy-start | bytes 9437188
  35.6 8.6 %copy-start.10 = (s32[32]{0:T(128)S(1)}, s32[32]{0:T(128)}, u32[]{:S(2)}) copy-start(s32[32]{0:T(128)} %param.13) | copy-start | bytes 388
  35.6 15.5 %copy-start.9 = (f32[256,8]{0,1:T(8,128)S(1)}, f32[256,8]{0,1:T(8,128)}, u32[]{:S(2)}) copy-start(f32[256,8]{0,1:T(8,128)} %param.11) | copy-start | bytes 24580
  35.6 265.3 %all-to-all-start = ((bf16[16,6,704,128]{3,2,1,0:T(8,128)(2,1)}), bf16[16,6,704,128]{3,2,1,0:T(8,128)(2,1)}, u32[]{:S(2)}, u32[]{:S(2)}) async-start(bf16[16,6,704,128]{3,2,1,0:T(8,128)(2,1)} %broadcast_select_fusion), calls=%async_computation | async-start | bytes 34603008 | tf_op jit(solution)/shard_map/all_to_all | solution.py:60
  44.2 445.1 %all-reduce.6.cloned.1.call-start = ((), (), s32[]{:S(2)}) async-start(), calls=%async_computation.2 | async-start | bytes 8388608 | tf_op jit(solution)/shard_map/psum | solution.py:108
  44.9 0.8 copy-start.2
  310.6 3.9 slice-start
  310.6 4.0 slice-start.1
  314.6 11.6 %copy-start.4 = (bf16[2,16,704,128]{3,2,1,0:T(8,128)(2,1)}, bf16[2,16,704,128]{3,2,1,0:T(8,128)(2,1)S(1)}, u32[]{:S(2)}) copy-start(bf16[2,16,704,128]{3,2,1,0:T(8,128)(2,1)S(1)} %broadcast_select_fusion.1) | copy-start | bytes 17301508
  343.8 13.1 %copy-start.5 = (pred[128,16,128]{0,2,1:T(8,128)(4,1)S(1)}, pred[128,16,128]{0,2,1:T(8,128)(4,1)}, u32[]{:S(2)}) copy-start(pred[128,16,128]{0,2,1:T(8,128)(4,1)} %copy.81) | copy-start | bytes 786436
  366.0 8.4 %copy-start.6 = (bf16[16,8,8,128]{3,2,1,0:T(8,128)(2,1)S(1)}, bf16[16,8,8,128]{3,2,1,0:T(8,128)(2,1)}, u32[]{:S(2)}) copy-start(bf16[16,8,8,128]{3,2,1,0:T(8,128)(2,1)} %copy.109) | copy-start | bytes 786436
  374.4 5.6 copy-start.7
  419.2 216.5 %all-reduce.4.cloned.1.call-start = ((), (), s32[]{:S(2)}) async-start(), calls=%async_computation.1 | async-start | bytes 12582912 | tf_op jit(solution)/shard_map/psum | solution.py:130
  419.4 69.8 %copy-start.3 = (pred[2,128,16,128]{3,2,1,0:T(8,128)(4,1)S(1)}, pred[2,128,16,128]{3,2,1,0:T(8,128)(4,1)}, u32[]{:S(2)}) copy-start(pred[2,128,16,128]{3,2,1,0:T(8,128)(4,1)} %copy-done.2) | copy-start | bytes 1572868
  504.9 2.8 copy-start.8
  511.4 130.9 %copy-start.1 = (bf16[1536,1024]{1,0:T(8,128)(2,1)S(1)}, bf16[1536,1024]{1,0:T(8,128)(2,1)}, u32[]{:S(2)}) copy-start(bf16[1536,1024]{1,0:T(8,128)(2,1)} %param.10) | copy-start | bytes 9437188
Sparse Core Ops, SparseCore 0:
  419.3 69.8 all-reduce.5
  511.5 124.1 all-reduce.3
where the time goes:
time: 655 us; the launch traced here: 649 us
  waiting for transfers between devices  429 us (65%)
  matrix products  76.8 us (12%)
  other arithmetic  75.5 us (12%)
  local copies, waits for them, and re-layouts  45.1 us (7%)
  between operations  14.6 us (2%)
  starting transfers between devices  8.78 us (1%)
    all_to_all x1, waiting for transfers between devices, on_device(): lax.all_to_all(outgoing, 'qblk', split_axis=0, concat_axis=0, tiled=True)  245 us
    psum x1, waiting for transfers between devices, on_device(): weight_grad = lax.psum(local_grad, 'qblk')  124 us
    psum x1, waiting for transfers between devices, on_device(): target_all, logit_all = lax.psum((targets, logit_terms), 'head')  59.6 us
    dot_general x2, matrix products, on_device(): jnp.einsum('qj,qjsk->qsk', head_weights[rows_start:rows_start + block_len...  29.6 us
    dot_general x2, matrix products, on_device(): jnp.einsum('qhd,sdk->qhsk', query_tile, latent, preferred_element_type=jn...  24.7 us
    reduce_sum x2, other arithmetic, on_device(): attention = weights_exp / jnp.sum(weights_exp, axis=(2, 3), keepdims=True)  18.2 us
    reduce_sum x2, other arithmetic, on_device(): jnp.sum(attention, axis=1) / H  16 us
    select_n x2, other arithmetic, on_device(): jnp.take(key_cache, slot_table, axis=0)  14.5 us
  transfers between devices with their start and end apart: 3, of which 3 were waited for; matrix products, arithmetic and copies ran while one was open for 3% of the time, Pallas kernels for 0%

commit v1 on v0

v1 whole, which is shorter than its diff:
```python
import functools

import jax
import jax.numpy as jnp
from jax import lax
from jax.experimental import pallas as pl
from jax.experimental.pallas import tpu as pltpu
from jax.sharding import Mesh, PartitionSpec as P

BF16 = jnp.bfloat16
F32 = jnp.float32
I32 = jnp.int32

H = 128
DK = 576
ID = 128
CAP = 3
BLK = 128
SEL = 16
KEYS = SEL * BLK
NY = 4
NQ = 16
SHARD = 32
LATC = DK // NY
IDXC = ID // NY
PIECE = LATC + IDXC
OWNK = KEYS // NY
HALF_COLS = 1024
IQ_ROWS = HALF_COLS + 32
LG_ROWS = OWNK + 16
DQ = 1536
COLS = HALF_COLS // NQ
QUERIES = 4096

score_scale = 192.0 ** (-0.5)
exp2_scale = score_scale * 1.4426950408889634
masked_value = -1e30
VMEM_LIMIT = 56 * 1024 * 1024

ANY = pl.BlockSpec(memory_space=pl.ANY)
VMEM = pl.BlockSpec(memory_space=pltpu.VMEM)
SMEM = pl.BlockSpec(memory_space=pltpu.SMEM)


def call(kernel, out_shape, in_specs, out_specs, scratch=(), name=None):
    return pl.pallas_call(
        kernel,
        out_shape=out_shape,
        in_specs=in_specs,
        out_specs=out_specs,
        scratch_shapes=list(scratch),
        compiler_params=pltpu.CompilerParams(vmem_limit_bytes=VMEM_LIMIT),
        name=name,
    )


def shape(dims, dtype):
    return jax.ShapeDtypeStruct(dims, dtype)


def pick_outgoing_kernel(ids, meta, cache, out, sem):
    y, core, me = meta[0], meta[1], meta[2]
    lat = pl.multiple_of(y * LATC, 16)
    idx = pl.multiple_of(DK + y * IDXC, 16)

    def copies(block, dst, slot):
        return (
            pltpu.make_async_copy(
                cache.at[block, pl.ds(lat, LATC), :], out.at[dst, slot, pl.ds(0, LATC), :], sem.at[0]
            ),
            pltpu.make_async_copy(
                cache.at[block, pl.ds(idx, IDXC), :], out.at[dst, slot, pl.ds(LATC, IDXC), :], sem.at[1]
            ),
        )

    def per_dst(dst, total):
        count = jnp.int32(0)
        for s in range(SEL):
            block = ids[2 * dst + core, s]
            mine = lax.shift_right_logical(block, 5) == me

            @pl.when(mine)
            def _(block=block, count=count):
                for c in copies(block - me * SHARD, dst, jnp.minimum(count, CAP - 1)):
                    c.start()

            count = count + mine.astype(I32)
        return total + count

    total = lax.fori_loop(0, NQ, per_dst, jnp.int32(0))

    def wait(_, carry):
        for c in copies(0, 0, 0):
            c.wait()
        return carry

    lax.fori_loop(0, total, wait, 0)


def pick_listed_kernel(ids, meta, arrived, lat, idx, seen, sem):
    core, me = meta[1], meta[2]
    row = 2 * me + core
    for i in range(NQ):
        seen[i] = 0
    pending = []
    for s in range(SEL):
        owner = lax.shift_right_logical(ids[row, s], 5)
        rank = jnp.minimum(seen[owner], CAP - 1)
        seen[owner] = seen[owner] + 1
        pending.append(
            pltpu.make_async_copy(arrived.at[owner, rank, pl.ds(LATC, IDXC), :], idx.at[s], sem.at[0])
        )
        pending.append(
            pltpu.make_async_copy(arrived.at[owner, rank, pl.ds(0, LATC), :], lat.at[s], sem.at[1])
        )
        pending[-2].start()
        pending[-1].start()
    for c in pending:
        c.wait()


def index_query_kernel(meta, x, w, hw, mine, other):
    core = meta[1]
    for k in range(4):
        cols = HALF_COLS // 4
        part = jnp.dot(x[...], w[:, k * cols : (k + 1) * cols], preferred_element_type=F32)
        part = part.astype(BF16)
        low = part[:BLK].T
        high = part[BLK:].T
        rows = pl.ds(k * cols, cols)
        first = jnp.broadcast_to(core == 0, low.shape)
        mine[rows, :] = jnp.where(first, low, high)
        other[rows, :] = jnp.where(first, high, low)
    weights = hw[...]
    hi = weights.astype(BF16)
    rest = weights - hi.astype(F32)
    mid = rest.astype(BF16)
    lo = (rest - mid.astype(F32)).astype(BF16)
    ext = jnp.concatenate(
        [hi.astype(F32), mid.astype(F32), lo.astype(F32), jnp.zeros_like(weights)], axis=0
    )
    first = jnp.broadcast_to(core == 0, (32, BLK))
    tail = pl.ds(HALF_COLS, 32)
    mine[tail, :] = jnp.where(first, ext[:, :BLK], ext[:, BLK:]).astype(BF16)
    other[tail, :] = jnp.where(first, ext[:, BLK:], ext[:, :BLK]).astype(BF16)


def head_rows(iq):
    tail = iq[HALF_COLS:, :].astype(F32)
    return tail[0:8] + tail[8:16] + tail[16:24]


def logits_kernel(meta, i0, i1, i2, i3, *rest):
    iq_refs, (logits_ref, stats_ref, keys, total) = rest[:8], rest[8:]
    y, count = meta[0], meta[3]
    for s, piece in enumerate((i0, i1, i2, i3)):
        start = pl.multiple_of(lax.rem(y + NY - s, NY) * IDXC, IDXC)
        for j in range(4):
            keys[pl.ds(start, IDXC), j * BLK : (j + 1) * BLK] = piece[4 * y + j]
    keys_t = keys[...].T
    total[...] = jnp.zeros_like(total)
    for ref in iq_refs:
        rows = head_rows(ref)
        for p in range(4):
            a, b = 2 * p, 2 * p + 1
            pair = jnp.concatenate(
                [ref[a * ID : (a + 1) * ID, :], ref[b * ID : (b + 1) * ID, :]], axis=1
            )
            affinity = jnp.maximum(jnp.dot(keys_t, pair, preferred_element_type=F32), 0.0)
            total[...] += (
                affinity[:, :BLK] * rows[a : a + 1] + affinity[:, BLK:] * rows[b : b + 1]
            )
    key = lax.broadcasted_iota(I32, (OWNK, BLK), 0) + y * OWNK
    token = lax.broadcasted_iota(I32, (OWNK, BLK), 1)
    valid = (key < count * BLK) & ((key >= BLK) | (key <= token))
    masked = jnp.where(valid, total[...], masked_value)
    logits_ref[...] = masked
    peak = jnp.max(masked, axis=0, keepdims=True)
    mass = jnp.sum(jnp.exp(masked - peak), axis=0, keepdims=True)
    row = lax.broadcasted_iota(I32, (8, BLK), 0)
    stats_ref[...] = jnp.where(row == 0, peak, mass)


def target_kernel(
    meta, l0, l1, l2, l3, q_own, q_other, o0, o1, o2, o3, keys, keys_t, qa, qb, buf_a, buf_b, total, sems
):
    y, core, count = meta[0], meta[1], meta[3]
    copies = []
    for s, piece in enumerate((l0, l1, l2, l3)):
        start = pl.multiple_of(lax.rem(y + NY - s, NY) * LATC, LATC)
        for j in range(SEL):
            copies.append(
                pltpu.make_async_copy(
                    piece.at[j], keys.at[pl.ds(start, LATC), pl.ds(j * BLK, BLK)], sems.at[0]
                )
            )
    lanes = pl.multiple_of(core * BLK, BLK)
    queries = [
        pltpu.make_async_copy(q_own.at[:, :, pl.ds(lanes, BLK)], qa, sems.at[1]),
        pltpu.make_async_copy(q_other, qb, sems.at[2]),
    ]
    for c in copies + queries:
        c.start()
    for c in copies:
        c.wait()
    for j in range(SEL):
        keys_t[j * BLK : (j + 1) * BLK, :] = keys[:, j * BLK : (j + 1) * BLK].T
    total[...] = jnp.zeros_like(total)
    for c in queries:
        c.wait()

    chunk = 256
    token = lax.broadcasted_iota(I32, (BLK, 2 * BLK), 1) % BLK
    causal = lax.broadcasted_iota(I32, (BLK, 2 * BLK), 0) <= token

    def scores(p, buf):
        pair = jnp.concatenate([qa[p], qb[p]], axis=1)
        peak = jnp.full((8, 2 * BLK), masked_value, F32)
        for k in range(KEYS // chunk):
            part = jnp.dot(
                keys_t[k * chunk : (k + 1) * chunk, :], pair, preferred_element_type=F32
            )
            for j in range(chunk // BLK):
                slot = k * (chunk // BLK) + j
                tile = part[j * BLK : (j + 1) * BLK]
                if slot == 0:
                    tile = jnp.where(causal, tile, masked_value)
                else:
                    tile = jnp.where(slot < count, tile, masked_value)
                buf[slot * BLK : (slot + 1) * BLK, :] = tile
                peak = jnp.maximum(peak, jnp.max(tile.reshape(BLK // 8, 8, 2 * BLK), axis=0))
        return jnp.max(peak, axis=0, keepdims=True)

    def spread(buf, peak):
        shift = peak * exp2_scale
        mass = jnp.zeros((8, 2 * BLK), F32)
        for j in range(SEL):
            tile = jnp.exp2(buf[j * BLK : (j + 1) * BLK, :] * exp2_scale - shift)
            buf[j * BLK : (j + 1) * BLK, :] = tile
            mass = mass + jnp.sum(tile.reshape(BLK // 8, 8, 2 * BLK), axis=0)
        share = 1.0 / (jnp.sum(mass, axis=0, keepdims=True) * H)
        for j in range(SEL):
            tile = buf[j * BLK : (j + 1) * BLK, :] * share
            total[j * BLK : (j + 1) * BLK, :] += tile[:, :BLK] + tile[:, BLK:]

    def step(k, peak_a):
        peak_b = scores(2 * k + 1, buf_b)
        spread(buf_a, peak_a)
        peak_next = scores(2 * k + 2, buf_a)
        spread(buf_b, peak_b)
        return peak_next

    pairs = qa.shape[0]
    peak_a = lax.fori_loop(0, pairs // 2 - 1, step, scores(0, buf_a))
    peak_b = scores(pairs - 1, buf_b)
    spread(buf_a, peak_a)
    spread(buf_b, peak_b)
    for s, out in enumerate((o0, o1, o2, o3)):
        start = pl.multiple_of(lax.rem(y + s, NY) * OWNK, OWNK)
        out[...] = total[pl.ds(start, OWNK), :].astype(BF16)


def loss_kernel(t0, t1, t2, t3, logits, s0, s1, s2, s3, out):
    stats = [s[...] for s in (s0, s1, s2, s3)]
    peak = functools.reduce(jnp.maximum, [s[0:1] for s in stats])
    mass = functools.reduce(jnp.add, [s[1:2] * jnp.exp(s[0:1] - peak) for s in stats])
    log_total = peak + jnp.log(mass)
    target = t0[...].astype(F32) + t1[...].astype(F32) + t2[...].astype(F32) + t3[...].astype(F32)
    masked = logits[...]
    valid = masked > 0.5 * masked_value
    log_probs = masked - log_total
    entropy = -jnp.sum(jnp.where(valid, target * log_probs, 0.0), axis=0, keepdims=True)
    grad = jnp.where(valid, jnp.exp(log_probs) - target, 0.0) / QUERIES
    out[:OWNK, :] = grad.astype(BF16)
    hi = entropy.astype(BF16).astype(F32)
    mid = (entropy - hi).astype(BF16).astype(F32)
    lo = entropy - hi - mid
    row = lax.broadcasted_iota(I32, (16, BLK), 0)
    ext = jnp.where(row == 0, hi, jnp.where(row == 1, mid, jnp.where(row == 2, lo, 0.0)))
    out[OWNK:, :] = ext.astype(BF16)


def backward_kernel(
    meta, g0, g1, g2, g3, i0, i1, i2, i3, iq0, iq1, out, entropy_ref, keys, keys_t, grads
):
    y = meta[0]
    entropy = jnp.zeros((1, BLK), F32)
    for s, piece in enumerate((g0, g1, g2, g3)):
        start = pl.multiple_of(lax.rem(y + NY - s, NY) * OWNK, OWNK)
        grads[pl.ds(start, OWNK), :] = piece[:OWNK, :].astype(F32)
        tail = piece[OWNK:, :].astype(F32)
        entropy = entropy + tail[0:1] + tail[1:2] + tail[2:3]
    entropy_ref[...] = jnp.broadcast_to(entropy, (8, BLK))
    for s, piece in enumerate((i0, i1, i2, i3)):
        start = pl.multiple_of(lax.rem(y + NY - s, NY) * IDXC, IDXC)
        for j in range(SEL):
            keys[pl.ds(start, IDXC), j * BLK : (j + 1) * BLK] = piece[j]
    for j in range(SEL):
        keys_t[j * BLK : (j + 1) * BLK, :] = keys[:, j * BLK : (j + 1) * BLK].T
    chunk = 512
    for core, ref in enumerate((iq0, iq1)):
        rows = head_rows(ref)
        for p in range(4):
            a, b = 2 * p, 2 * p + 1
            pair = jnp.concatenate(
                [ref[a * ID : (a + 1) * ID, :], ref[b * ID : (b + 1) * ID, :]], axis=1
            )
            acc = jnp.zeros((ID, 2 * BLK), F32)
            for k in range(KEYS // chunk):
                span = slice(k * chunk, (k + 1) * chunk)
                affinity = jnp.dot(keys_t[span, :], pair, preferred_element_type=F32)
                grad = grads[span, :]
                scaled = jnp.concatenate([grad * rows[a : a + 1], grad * rows[b : b + 1]], axis=1)
                masked = jnp.where(affinity > 0, scaled, 0.0).astype(BF16)
                acc = acc + jnp.dot(keys[:, span], masked, preferred_element_type=F32)
            acc = acc.astype(BF16)
            for n, head in enumerate((a, b)):
                lanes = slice(n * BLK, (n + 1) * BLK)
                out[4 * head + core] = acc[:COLS, lanes]
                out[4 * head + 2 + core] = acc[COLS:, lanes]


def weight_kernel(meta, qg, xa, xb, out, lhs, acc):
    step = pl.program_id(0)
    chunk = xa.shape[0]

    @pl.when(step == 0)
    def _():
        for s in range(2 * NQ):
            lhs[s // 4, :, (s % 4) * BLK : (s % 4 + 1) * BLK] = qg[s]
        acc[...] = jnp.zeros_like(acc)

    left = lhs[step]
    acc[0] += jnp.dot(left, xa[...], preferred_element_type=F32)
    acc[1] += jnp.dot(left, xb[...], preferred_element_type=F32)

    @pl.when(step == pl.num_programs(0) - 1)
    def _():
        own_first = jnp.broadcast_to(meta[1] == 0, acc.shape[1:])
        half = acc.shape[2]
        out[:, :half] = jnp.where(own_first, acc[0], acc[1]).astype(BF16)
        out[:, half:] = jnp.where(own_first, acc[1], acc[0]).astype(BF16)


def finish_kernel(gathered, out):
    out[...] = gathered[...].astype(F32).T


def ring(shift):
    return [(i, (i + shift) % NY) for i in range(NY)]


SWAP = [(0, 1), (1, 0)]
SHIFTS = (1, 3, 2)


def around_y(array):
    moved = {s: lax.ppermute(array, "y", ring(s)) for s in SHIFTS}
    return (array, moved[1], moved[2], moved[3])


def on_device(
    q_absorbed, key_cache, index_input, index_weight, head_weights, block_ids, block_counts
):
    y, core = lax.axis_index("y"), lax.axis_index("c")
    me = lax.axis_index(("z", "x"))
    count = lax.dynamic_index_in_dim(block_counts, 2 * me + core, 0, keepdims=False)
    meta = jnp.stack([y, core, me, count]).astype(I32)

    outgoing = call(
        pick_outgoing_kernel,
        shape((NQ, CAP, PIECE, BLK), BF16),
        [SMEM, SMEM, ANY],
        ANY,
        [pltpu.SemaphoreType.DMA((2,))],
        "pick_outgoing",
    )(block_ids, meta, key_cache)
    arrived = lax.all_to_all(outgoing, ("z", "x"), split_axis=0, concat_axis=0, tiled=True)

    iq_own, iq_send = call(
        index_query_kernel,
        (shape((IQ_ROWS, BLK), BF16),) * 2,
        [SMEM, VMEM, VMEM, VMEM],
        (VMEM, VMEM),
        name="index_query",
    )(meta, index_input, index_weight, head_weights.T)
    iq_other = lax.ppermute(iq_send, "c", SWAP)
    first = core == 0
    iq_pair = jnp.stack(
        [jnp.where(first, iq_own, iq_other), jnp.where(first, iq_other, iq_own)]
    )
    iq_all = around_y(iq_pair)

    q_t = jnp.transpose(q_absorbed, (1, 2, 0))
    q_send = lax.dynamic_slice_in_dim(q_t, (1 - core) * BLK, BLK, 2)
    q_other = lax.ppermute(q_send, "c", SWAP)

    lat, idx = call(
        pick_listed_kernel,
        (shape((SEL, LATC, BLK), BF16), shape((SEL, IDXC, BLK), BF16)),
        [SMEM, SMEM, ANY],
        (ANY, ANY),
        [pltpu.SMEM((NQ,), I32), pltpu.SemaphoreType.DMA((2,))],
        "pick_listed",
    )(block_ids, meta, arrived)
    idx_all = around_y(idx)
    lat_all = around_y(lat)

    half = DQ // 2
    x_half = lax.dynamic_slice_in_dim(index_input, core * half, half, 1)
    x_half, _ = lax.optimization_barrier((x_half, arrived))
    x_own = lax.all_gather(x_half, ("z", "x"), axis=0, tiled=True)
    x_other = lax.ppermute(x_own, "c", SWAP)

    logits, stats = call(
        logits_kernel,
        (shape((OWNK, BLK), F32), shape((8, BLK), F32)),
        [SMEM] + [VMEM] * 12,
        (VMEM, VMEM),
        [pltpu.VMEM((ID, OWNK), BF16), pltpu.VMEM((OWNK, BLK), F32)],
        "index_logits",
    )(meta, *idx_all, *[a[n] for a in iq_all for n in range(2)])
    stats_all = around_y(stats)

    targets = call(
        target_kernel,
        (shape((OWNK, BLK), BF16),) * 4,
        [SMEM] + [ANY] * 6,
        (VMEM,) * 4,
        [
            pltpu.VMEM((DK, KEYS), BF16),
            pltpu.VMEM((KEYS, DK), BF16),
            pltpu.VMEM((16, DK, BLK), BF16),
            pltpu.VMEM((16, DK, BLK), BF16),
            pltpu.VMEM((KEYS, 2 * BLK), F32),
            pltpu.VMEM((KEYS, 2 * BLK), F32),
            pltpu.VMEM((KEYS, BLK), F32),
            pltpu.SemaphoreType.DMA((3,)),
        ],
        "attention_target",
    )(meta, *lat_all, q_t, q_other)
    arrived_targets = {s: lax.ppermute(targets[s], "y", ring(s)) for s in SHIFTS}

    grads = call(
        loss_kernel,
        shape((LG_ROWS, BLK), BF16),
        [VMEM] * 9,
        VMEM,
        name="loss",
    )(targets[0], arrived_targets[1], arrived_targets[2], arrived_targets[3], logits, *stats_all)
    grads_all = around_y(grads)

    query_grad, entropy = call(
        backward_kernel,
        (shape((2 * NQ, COLS, BLK), BF16), shape((8, BLK), F32)),
        [SMEM] + [VMEM] * 10,
        (VMEM, VMEM),
        [
            pltpu.VMEM((ID, KEYS), BF16),
            pltpu.VMEM((KEYS, ID), BF16),
            pltpu.VMEM((KEYS, BLK), F32),
        ],
        "index_backward",
    )(meta, *grads_all, *idx_all, iq_pair[0], iq_pair[1])
    entropy_other = lax.ppermute(entropy, "c", SWAP)
    entropy_both = jnp.where(
        first,
        jnp.concatenate([entropy[0], entropy_other[0]]),
        jnp.concatenate([entropy_other[0], entropy[0]]),
    )
    share = 2 * BLK // (2 * NY)
    entropy_mine = lax.dynamic_slice_in_dim(entropy_both, (2 * y + core) * share, share, 0)

    swapped = lax.all_to_all(query_grad, ("z", "x", "c"), split_axis=0, concat_axis=0, tiled=True)
    chunk = 512
    piece = pl.pallas_call(
        weight_kernel,
        grid=(QUERIES // chunk,),
        out_shape=shape((COLS, DQ), BF16),
        in_specs=[
            SMEM,
            pl.BlockSpec((2 * NQ, COLS, BLK), lambda i: (0, 0, 0)),
            pl.BlockSpec((chunk, half), lambda i: (i, 0)),
            pl.BlockSpec((chunk, half), lambda i: (i, 0)),
        ],
        out_specs=pl.BlockSpec((COLS, DQ), lambda i: (0, 0)),
        scratch_shapes=[
            pltpu.VMEM((QUERIES // chunk, COLS, chunk), BF16),
            pltpu.VMEM((2, COLS, half), F32),
        ],
        compiler_params=pltpu.CompilerParams(vmem_limit_bytes=VMEM_LIMIT),
        name="weight_piece",
    )(meta, swapped, x_own, x_other)
    gathered = lax.all_gather(piece, ("z", "x"), axis=0, tiled=True)
    weight_grad = pl.pallas_call(
        finish_kernel,
        grid=(6,),
        out_shape=shape((DQ, HALF_COLS), F32),
        in_specs=[pl.BlockSpec((HALF_COLS, 256), lambda i: (0, i))],
        out_specs=pl.BlockSpec((256, HALF_COLS), lambda i: (i, 0)),
        compiler_params=pltpu.CompilerParams(vmem_limit_bytes=VMEM_LIMIT),
        name="finish",
    )(gathered)
    return weight_grad, entropy_mine


def solution(mesh):
    fine = Mesh(mesh.devices.reshape(NY, 2, 4, 4), ("y", "c", "z", "x"))
    head, qblk = ("y", "c"), ("z", "x")
    placed = (
        P(qblk, head, None),
        P(qblk, None, None),
        P(qblk, None),
        P(None, head),
        P(qblk, head),
        P(),
        P(),
    )
    return jax.shard_map(
        on_device,
        mesh=fine,
        in_specs=placed,
        out_specs=(P(None, head), P(qblk + head)),
        check_vma=False,
    )
```

time: 655 us -> 408 us (0.62)
  waiting for transfers between devices: 429 us -> 175 us
  Pallas kernels: 0 us -> 96.2 us
  matrix products: 76.8 us -> 0 us
  other arithmetic: 75.5 us -> 2.36 us
  starting transfers between devices: 8.78 us -> 79.5 us
  local copies, waits for them, and re-layouts: 45.1 us -> 11.8 us
  blocking collectives: 0 us -> 25.7 us
    all_to_all x1, waiting for transfers between devices: 245 us -> 30.9 us  [on_device(): lax.all_to_all(outgoing, ('z', 'x'), split_axis=0, concat_axis=0, tiled=T...]
    psum x2 -> x0, waiting for transfers between devices: 183 us -> none  [the longest x1 124 us: on_device(): weight_grad = lax.psum(local_grad, 'qblk')]
    all_gather x0 -> x2, waiting for transfers between devices: none -> 104 us  [the longest x1 60.8 us: on_device(): x_own = lax.all_gather(x_half, ('z', 'x'), axis=0, tiled=True)]
    pallas_call x0 -> x9, Pallas kernels: none -> 96.2 us  [the longest x1 25.7 us: on_device(): call(target_kernel, (shape((OWNK, BLK), BF16),) * 4, [SMEM] + [ANY] * 6,...]
    dot_general x10 -> x0, matrix products: 76.8 us -> none  [the longest x2 29.6 us: on_device(): jnp.einsum('qj,qjsk->qsk', head_weights[rows_start:rows_start + block_len...]
    all_to_all x1, starting transfers between devices: 8.53 us -> 58 us  [on_device(): lax.all_to_all(outgoing, ('z', 'x'), split_axis=0, concat_axis=0, tiled=T...]
    ppermute x0 -> x22, waiting for transfers between devices: none -> 40.9 us  [the longest x15 37 us: around_y(): moved = {s: lax.ppermute(array, 'y', ring(s)) for s in SHIFTS}]
    reduce_sum x8 -> x0, other arithmetic: 40 us -> none  [the longest x2 18.2 us: on_device(): attention = weights_exp / jnp.sum(weights_exp, axis=(2, 3), keepdims=True)]
  transfers between devices with their start and end apart: 3 -> 25, of which waited for: 3 -> 13; matrix products, arithmetic and copies ran while one was open for 3% -> 2% of each run, Pallas kernels for 0% -> 16%
where the time goes in v1:
time: 408 us; the launch traced here: 405 us
  waiting for transfers between devices  175 us (43%)
  Pallas kernels  96.2 us (24%)
  starting transfers between devices  79.5 us (19%)
  blocking collectives  25.7 us (6%)
  between operations  14.3 us (4%)
  local copies, waits for them, and re-layouts  11.8 us (3%)
    all_gather x1, waiting for transfers between devices, on_device(): x_own = lax.all_gather(x_half, ('z', 'x'), axis=0, tiled=True)  60.8 us
    all_to_all x1, starting transfers between devices, on_device(): lax.all_to_all(outgoing, ('z', 'x'), split_axis=0, concat_axis=0, tiled=T...  58 us
    all_gather x1, waiting for transfers between devices, on_device(): gathered = lax.all_gather(piece, ('z', 'x'), axis=0, tiled=True)  42.7 us
    ppermute x15, waiting for transfers between devices, around_y(): moved = {s: lax.ppermute(array, 'y', ring(s)) for s in SHIFTS}  37 us
    all_to_all x1, waiting for transfers between devices, on_device(): lax.all_to_all(outgoing, ('z', 'x'), split_axis=0, concat_axis=0, tiled=T...  30.9 us
    pallas_call x1, Pallas kernels, on_device(): call(target_kernel, (shape((OWNK, BLK), BF16),) * 4, [SMEM] + [ANY] * 6,...  25.7 us
    all_to_all x1, blocking collectives, on_device(): lax.all_to_all(query_grad, ('z', 'x', 'c'), split_axis=0, concat_axis=0,...  25.7 us
    pallas_call x1, Pallas kernels, on_device(): call(pick_listed_kernel, (shape((SEL, LATC, BLK), BF16), shape((SEL, IDXC...  23.9 us
  transfers between devices with their start and end apart: 25, of which 13 were waited for; matrix products, arithmetic and copies ran while one was open for 2% of the time, Pallas kernels for 16%

profile of v1, /device:TPU:1, one launch (start us, length us, event | category | flops | bytes accessed | tf_op | source)
XLA Modules:
  0.0 405.2 jit_solution(6031133325329709606)
XLA Ops:
  7.2 1.4 copy.10.ids
  8.5 1.2 dynamic_slice.13
  9.8 1.3 pad_add_fusion.meta
  11.1 14.5 %pick_outgoing.1 = bf16[16,3,176,128]{3,2,1,0:T(8,128)(2,1)} custom-call(s32[32,16]{1,0:T(8,128)} %copy.10.ids, s32[4]{0:T(128)} %pad_add_fusion.meta, bf16[32,704,128]{2,1,0:T(8,128)(2,1)} %cache.1), custom_call_target="tpu_custom_call" | custom-call | tf_op jit(solution)/shard_map/pick_outgoing/pallas_call | solution.py:370
  25.6 58.0 %all-to-all-start = ((bf16[16,3,176,128]{3,2,1,0:T(8,128)(2,1)}), bf16[16,3,176,128]{3,2,1,0:T(8,128)(2,1)S(1)}, u32[]{:S(2)}, u32[]{:S(2)}) async-start(bf16[16,3,176,128]{3,2,1,0:T(8,128)(2,1)} %pick_outgoing.1), calls=%async_computation | async-start | bytes 4325376 | tf_op jit(solution)/shard_map/all_to_all | solution.py:378
  84.4 30.9 %all-to-all-done.arrived = bf16[16,3,176,128]{3,2,1,0:T(8,128)(2,1)S(1)} async-done(((bf16[16,3,176,128]{3,2,1,0:T(8,128)(2,1)}), bf16[16,3,176,128]{3,2,1,0:T(8,128)(2,1)S(1)}, u32[]{:S(2)}, u32[]{:S(2)}) %all-to-all-start) | async-done | bytes 2162720 | tf_op jit(solution)/shard_map/all_to_all | solution.py:378
  115.4 60.8 %all-gather.3.cloned.1.call-done.xa = bf16[4096,768]{1,0:T(8,128)(2,1)} async-done(((bf16[256,768]{1,0:T(8,128)(2,1)}), bf16[4096,768]{1,0:T(8,128)(2,1)}) %all-gather.3.cloned.1.call-update) | async-done | bytes 6291472 | tf_op jit(solution)/shard_map/all_gather | solution.py:412
  176.9 3.2 dynamic-slice_bitcast_fusion
  180.1 4.0 index_query.1
  184.6 3.0 collective-permute-done.10
  188.7 2.5 collective-permute-start.13
  191.8 23.9 %pick_listed.1 = (bf16[16,144,128]{2,1,0:T(8,128)(2,1)}, bf16[16,32,128]{2,1,0:T(8,128)(2,1)}) custom-call(s32[32,16]{1,0:T(8,128)} %copy.10.ids, s32[4]{0:T(128)} %pad_add_fusion.meta, bf16[16,3,176,128]{3,2,1,0:T(8,128)(2,1)} %copy-done), custom_call_target="tpu_custom_call" | custom-call | tf_op jit(solution)/shard_map/pick_listed/pallas_call | solution.py:398
  216.4 1.9 collective-permute-start.1
  219.0 2.0 collective-permute-start.2
  221.8 9.2 %collective-permute-done.l1 = bf16[16,144,128]{2,1,0:T(8,128)(2,1)S(1)} collective-permute-done((bf16[16,144,128]{2,1,0:T(8,128)(2,1)}, bf16[16,144,128]{2,1,0:T(8,128)(2,1)S(1)}, u32[]{:S(2)}, u32[]{:S(2)}) %collective-permute-start) | collective-permute-done | bytes 589856 | tf_op jit(solution)/shard_map/ppermute | solution.py:358
  231.1 12.8 %collective-permute-done.1.l2 = bf16[16,144,128]{2,1,0:T(8,128)(2,1)S(1)} collective-permute-done((bf16[16,144,128]{2,1,0:T(8,128)(2,1)}, bf16[16,144,128]{2,1,0:T(8,128)(2,1)S(1)}, u32[]{:S(2)}, u32[]{:S(2)}) %collective-permute-start.1) | collective-permute-done | bytes 589856 | tf_op jit(solution)/shard_map/ppermute | solution.py:358
  245.8 3.6 collective-permute-start.9
  249.5 25.7 %attention_target.1 = (bf16[512,128]{1,0:T(8,128)(2,1)}, bf16[512,128]{1,0:T(8,128)(2,1)}, bf16[512,128]{1,0:T(8,128)(2,1)}, bf16[512,128]{1,0:T(8,128)(2,1)}) custom-call(s32[4]{0:T(128)} %pad_add_fusion.meta, bf16[16,144,128]{2,1,0:T(8,128)(2,1)} %get-tuple-element.15.l0, bf16[16,144,128]{2,1,0:T(8,128)(2,1)} %copy-done.4, ...), custom_call_target="tpu_custom_call" | custom-call | tf_op jit(solution)/shard_map/attention_target/pallas_call | solution.py:425
  275.8 1.7 collective-permute-start.5
  277.5 1.3 collective-permute-start.6
  280.3 4.9 %index_logits.1 = (f32[512,128]{1,0:T(8,128)}, f32[8,128]{1,0:T(8,128)}) custom-call(s32[4]{0:T(128)} %pad_add_fusion.meta, bf16[16,32,128]{2,1,0:T(8,128)(2,1)} %get-tuple-element.20.i0, bf16[16,32,128]{2,1,0:T(8,128)(2,1)} %copy-done.7, bf16[16,32,128]{2,1,0:T(8,128)(2,1)} %copy-done.8, bf16[16,32,128]{2,1,0:T(8,128)(2,1)} %copy-done.9, ...), custom_call_target="tpu_custom_call" | custom-call | tf_op jit(solution)/shard_map/index_logits/pallas_call | solution.py:415
  285.4 3.7 collective-permute-done.14.s1
  289.6 3.6 collective-permute-done.15.s2
  293.2 2.7 collective-permute-done.16.s3
  296.6 2.0 loss.1.g0
  298.7 2.4 collective-permute-start.18
  301.4 4.1 collective-permute-done.17.g1
  306.8 6.1 %index_backward.1 = (bf16[32,64,128]{2,1,0:T(8,128)(2,1)}, f32[8,128]{1,0:T(8,128)}) custom-call(s32[4]{0:T(128)} %pad_add_fusion.meta, bf16[528,128]{1,0:T(8,128)(2,1)} %loss.1.g0, bf16[528,128]{1,0:T(8,128)(2,1)} %copy-done.10, bf16[528,128]{1,0:T(8,128)(2,1)} %copy-done.11, bf16[528,128]{1,0:T(8,128)(2,1)} %copy-done.12, ...), custom_call_target="tpu_custom_call" | custom-call | tf_op jit(solution)/shard_map/index_backward/pallas_call | solution.py:453
  312.9 25.7 %all_to_all.10.qg = bf16[32,64,128]{2,1,0:T(8,128)(2,1)} all-to-all(bf16[32,64,128]{2,1,0:T(8,128)(2,1)} %get-tuple-element.25), channel_id=1, replica_groups=mesh['y'=4,'c'=2,'z'=4,'x'=4] {'z','x','c'}, dimensions={0} | all-to-all | bytes 1048576 | tf_op jit(solution)/shard_map/all_to_all | solution.py:474
  338.6 8.9 %weight_piece.1 = bf16[64,1536]{1,0:T(8,128)(2,1)} custom-call(s32[4]{0:T(128)} %pad_add_fusion.meta, bf16[32,64,128]{2,1,0:T(8,128)(2,1)} %all_to_all.10.qg, bf16[4096,768]{1,0:T(8,128)(2,1)} %all-gather.3.cloned.1.call-done.xa, bf16[4096,768]{1,0:T(8,128)(2,1)} %collective-permute-done.20.xb), custom_call_target="tpu_custom_call" | custom-call | tf_op jit(solution)/shard_map/weight_piece/pallas_call | solution.py:476
  349.4 42.7 %all-gather.5.cloned.1.call-done.gathered = bf16[1024,1536]{1,0:T(8,128)(2,1)} async-done(((bf16[64,1536]{1,0:T(8,128)(2,1)}), bf16[1024,1536]{1,0:T(8,128)(2,1)}) %all-gather.5.cloned.1.call-update) | async-done | bytes 3145744 | tf_op jit(solution)/shard_map/all_gather | solution.py:494
  392.2 6.1 %finish.1 = f32[1536,1024]{1,0:T(8,128)} custom-call(bf16[1024,1536]{1,0:T(8,128)(2,1)} %all-gather.5.cloned.1.call-done.gathered), custom_call_target="tpu_custom_call" | custom-call | tf_op jit(solution)/shard_map/finish/pallas_call | solution.py:495
  (84 shorter events, 14.9 us)
Async XLA Ops:
  25.6 58.1 %copy-start.3 = (bf16[256,1536]{1,0:T(8,128)(2,1)S(1)}, bf16[256,1536]{1,0:T(8,128)(2,1)}, u32[]{:S(2)}) copy-start(bf16[256,1536]{1,0:T(8,128)(2,1)} %x.1) | copy-start | bytes 2359300
  25.6 89.7 %all-to-all-start = ((bf16[16,3,176,128]{3,2,1,0:T(8,128)(2,1)}), bf16[16,3,176,128]{3,2,1,0:T(8,128)(2,1)S(1)}, u32[]{:S(2)}, u32[]{:S(2)}) async-start(bf16[16,3,176,128]{3,2,1,0:T(8,128)(2,1)} %pick_outgoing.1), calls=%async_computation | async-start | bytes 4325376 | tf_op jit(solution)/shard_map/all_to_all | solution.py:378
  83.6 92.6 %all-gather.3.cloned.1.call-start = ((), (), s32[]{:S(2)}) async-start(), calls=%async_computation.2 | async-start | bytes 6684672 | tf_op jit(solution)/shard_map/all_gather | solution.py:412
  115.3 68.8 %copy-start = (bf16[16,3,176,128]{3,2,1,0:T(8,128)(2,1)}, bf16[16,3,176,128]{3,2,1,0:T(8,128)(2,1)S(1)}, u32[]{:S(2)}) copy-start(bf16[16,3,176,128]{3,2,1,0:T(8,128)(2,1)S(1)} %all-to-all-done.arrived) | copy-start | bytes 6488068
  115.3 276.9 %all-gather.5.cloned.1.call-start = ((), (), s32[]{:S(2)}) async-start(), calls=%async_computation.3 | async-start | bytes 3342336 | tf_op jit(solution)/shard_map/all_gather | solution.py:494
  176.2 162.4 %collective-permute-start.20 = (bf16[4096,768]{1,0:T(8,128)(2,1)}, bf16[4096,768]{1,0:T(8,128)(2,1)}, u32[]{:S(2)}, u32[]{:S(2)}) collective-permute-start(bf16[4096,768]{1,0:T(8,128)(2,1)} %all-gather.3.cloned.1.call-done.xa), channel_id=1, source_target_pairs={{0,16},{16,0},{1,17},{17,1},{2,18},{18,2},{3,19},{19,3},{4,20},{20... | collective-permute-start | bytes 18874376 | tf_op jit(solution)/shard_map/ppermute | solution.py:413
  180.1 38.9 %collective-permute-start.3 = (bf16[16,576,128]{2,1,0:T(8,128)(2,1)}, bf16[16,576,128]{2,1,0:T(8,128)(2,1)}, u32[]{:S(2)}, u32[]{:S(2)}) collective-permute-start(bf16[16,576,128]{2,1,0:T(8,128)(2,1)} %dynamic-slice_bitcast_fusion), channel_id=1, source_target_pairs={{0,16},{16,0},{1,17},{17,1},{2,18},{18,2},{3,19},{19,3},{4,20},{20... | collective-permute-start | bytes 7077896 | tf_op jit(solution)/shard_map/ppermute | solution.py:396
  184.1 3.5 collective-permute-start.10
  188.6 86.6 %copy-start.1 = (bf16[1056,128]{1,0:T(8,128)(2,1)}, bf16[1056,128]{1,0:T(8,128)(2,1)S(1)}, u32[]{:S(2)}) copy-start(bf16[1056,128]{1,0:T(8,128)(2,1)S(1)} %get-tuple-element.34.rest_1_.iq1) | copy-start | bytes 811012
  188.6 86.6 %copy-start.2 = (bf16[1056,128]{1,0:T(8,128)(2,1)}, bf16[1056,128]{1,0:T(8,128)(2,1)S(1)}, u32[]{:S(2)}) copy-start(bf16[1056,128]{1,0:T(8,128)(2,1)S(1)} %get-tuple-element.35.rest_0_.iq0) | copy-start | bytes 811012
  188.7 27.7 %collective-permute-start.13 = (bf16[2,1056,128]{2,1,0:T(8,128)(2,1)S(1)}, bf16[2,1056,128]{2,1,0:T(8,128)(2,1)S(1)}, u32[]{:S(2)}, u32[]{:S(2)}) collective-permute-start(bf16[2,1056,128]{2,1,0:T(8,128)(2,1)S(1)} %pad_maximum_fusion), channel_id=1, source_target_pairs={{0,96},{32,0},{64,32},{96,64},{1,97},{33,1},{65,33},{97,65},{2,98}... | collective-permute-start | bytes 1622024 | tf_op jit(solution)/shard_map/ppermute | solution.py:358
  191.2 27.1 %collective-permute-start.12 = (bf16[2,1056,128]{2,1,0:T(8,128)(2,1)S(1)}, bf16[2,1056,128]{2,1,0:T(8,128)(2,1)S(1)}, u32[]{:S(2)}, u32[]{:S(2)}) collective-permute-start(bf16[2,1056,128]{2,1,0:T(8,128)(2,1)S(1)} %pad_maximum_fusion), channel_id=1, source_target_pairs={{0,64},{32,96},{64,0},{96,32},{1,65},{33,97},{65,1},{97,33},{2,66}... | collective-permute-start | bytes 1622024 | tf_op jit(solution)/shard_map/ppermute | solution.py:358
  215.7 15.4 %collective-permute-start = (bf16[16,144,128]{2,1,0:T(8,128)(2,1)}, bf16[16,144,128]{2,1,0:T(8,128)(2,1)S(1)}, u32[]{:S(2)}, u32[]{:S(2)}) collective-permute-start(bf16[16,144,128]{2,1,0:T(8,128)(2,1)} %get-tuple-element.15.l0), channel_id=1, source_target_pairs={{0,32},{32,64},{64,96},{96,0},{1,33},{33,65},{65,97},{97,1},{2,34}... | collective-permute-start | bytes 1769480 | tf_op jit(solution)/shard_map/ppermute | solution.py:358
  216.4 27.5 %collective-permute-start.1 = (bf16[16,144,128]{2,1,0:T(8,128)(2,1)}, bf16[16,144,128]{2,1,0:T(8,128)(2,1)S(1)}, u32[]{:S(2)}, u32[]{:S(2)}) collective-permute-start(bf16[16,144,128]{2,1,0:T(8,128)(2,1)} %get-tuple-element.15.l0), channel_id=1, source_target_pairs={{0,64},{32,96},{64,0},{96,32},{1,65},{33,97},{65,1},{97,33},{2,66}... | collective-permute-start | bytes 1769480 | tf_op jit(solution)/shard_map/ppermute | solution.py:358
  218.3 56.9 %collective-permute-start.11 = (bf16[2,1056,128]{2,1,0:T(8,128)(2,1)S(1)}, bf16[2,1056,128]{2,1,0:T(8,128)(2,1)S(1)}, u32[]{:S(2)}, u32[]{:S(2)}) collective-permute-start(bf16[2,1056,128]{2,1,0:T(8,128)(2,1)S(1)} %pad_maximum_fusion), channel_id=1, source_target_pairs={{0,32},{32,64},{64,96},{96,0},{1,33},{33,65},{65,97},{97,1},{2,34}... | collective-permute-start | bytes 1622024 | tf_op jit(solution)/shard_map/ppermute | solution.py:358
  219.0 26.8 %collective-permute-start.2 = (bf16[16,144,128]{2,1,0:T(8,128)(2,1)}, bf16[16,144,128]{2,1,0:T(8,128)(2,1)S(1)}, u32[]{:S(2)}, u32[]{:S(2)}) collective-permute-start(bf16[16,144,128]{2,1,0:T(8,128)(2,1)} %get-tuple-element.15.l0), channel_id=1, source_target_pairs={{0,96},{32,0},{64,32},{96,64},{1,97},{33,1},{65,33},{97,65},{2,98}... | collective-permute-start | bytes 1769480 | tf_op jit(solution)/shard_map/ppermute | solution.py:358
  231.1 18.4 %copy-start.4 = (bf16[16,144,128]{2,1,0:T(8,128)(2,1)}, bf16[16,144,128]{2,1,0:T(8,128)(2,1)S(1)}, u32[]{:S(2)}) copy-start(bf16[16,144,128]{2,1,0:T(8,128)(2,1)S(1)} %collective-permute-done.l1) | copy-start | bytes 1769476
  231.1 44.7 %collective-permute-start.7 = (bf16[16,32,128]{2,1,0:T(8,128)(2,1)}, bf16[16,32,128]{2,1,0:T(8,128)(2,1)S(1)}, u32[]{:S(2)}, u32[]{:S(2)}) collective-permute-start(bf16[16,32,128]{2,1,0:T(8,128)(2,1)} %get-tuple-element.20.i0), channel_id=1, source_target_pairs={{0,32},{32,64},{64,96},{96,0},{1,33},{33,65},{65,97},{97,1},{2,34}... | collective-permute-start | bytes 393224 | tf_op jit(solution)/shard_map/ppermute | solution.py:358
  243.9 33.6 %collective-permute-start.8 = (bf16[16,32,128]{2,1,0:T(8,128)(2,1)}, bf16[16,32,128]{2,1,0:T(8,128)(2,1)S(1)}, u32[]{:S(2)}, u32[]{:S(2)}) collective-permute-start(bf16[16,32,128]{2,1,0:T(8,128)(2,1)} %get-tuple-element.20.i0), channel_id=1, source_target_pairs={{0,64},{32,96},{64,0},{96,32},{1,65},{33,97},{65,1},{97,33},{2,66}... | collective-permute-start | bytes 393224 | tf_op jit(solution)/shard_map/ppermute | solution.py:358
  245.8 33.8 %collective-permute-start.9 = (bf16[16,32,128]{2,1,0:T(8,128)(2,1)}, bf16[16,32,128]{2,1,0:T(8,128)(2,1)S(1)}, u32[]{:S(2)}, u32[]{:S(2)}) collective-permute-start(bf16[16,32,128]{2,1,0:T(8,128)(2,1)} %get-tuple-element.20.i0), channel_id=1, source_target_pairs={{0,96},{32,0},{64,32},{96,64},{1,97},{33,1},{65,33},{97,65},{2,98}... | collective-permute-start | bytes 393224 | tf_op jit(solution)/shard_map/ppermute | solution.py:358
  275.2 20.7 %collective-permute-start.4 = (bf16[512,128]{1,0:T(8,128)(2,1)}, bf16[512,128]{1,0:T(8,128)(2,1)S(1)}, u32[]{:S(2)}, u32[]{:S(2)}) collective-permute-start(bf16[512,128]{1,0:T(8,128)(2,1)} %get-tuple-element.17), channel_id=1, source_target_pairs={{0,32},{32,64},{64,96},{96,0},{1,33},{33,65},{65,97},{97,1},{2,34}... | collective-permute-start | bytes 393224 | tf_op jit(solution)/shard_map/ppermute | solution.py:442
  275.8 20.1 %collective-permute-start.5 = (bf16[512,128]{1,0:T(8,128)(2,1)}, bf16[512,128]{1,0:T(8,128)(2,1)S(1)}, u32[]{:S(2)}, u32[]{:S(2)}) collective-permute-start(bf16[512,128]{1,0:T(8,128)(2,1)} %get-tuple-element.18), channel_id=1, source_target_pairs={{0,64},{32,96},{64,0},{96,32},{1,65},{33,97},{65,1},{97,33},{2,66}... | collective-permute-start | bytes 393224 | tf_op jit(solution)/shard_map/ppermute | solution.py:442
  277.5 18.4 %collective-permute-start.6 = (bf16[512,128]{1,0:T(8,128)(2,1)}, bf16[512,128]{1,0:T(8,128)(2,1)S(1)}, u32[]{:S(2)}, u32[]{:S(2)}) collective-permute-start(bf16[512,128]{1,0:T(8,128)(2,1)} %get-tuple-element.19), channel_id=1, source_target_pairs={{0,96},{32,0},{64,32},{96,64},{1,97},{33,1},{65,33},{97,65},{2,98}... | collective-permute-start | bytes 393224 | tf_op jit(solution)/shard_map/ppermute | solution.py:442
  285.2 3.9 collective-permute-start.14
  289.0 6.9 %copy-start.16 = (f32[8,128]{1,0:T(8,128)}, f32[8,128]{1,0:T(8,128)S(1)}, u32[]{:S(2)}) copy-start(f32[8,128]{1,0:T(8,128)S(1)} %collective-permute-done.14.s1) | copy-start | bytes 12292
  289.0 4.2 %collective-permute-start.15 = (f32[8,128]{1,0:T(8,128)}, f32[8,128]{1,0:T(8,128)S(1)}, u32[]{:S(2)}, u32[]{:S(2)}) collective-permute-start(f32[8,128]{1,0:T(8,128)} %get-tuple-element.24.s0), channel_id=1, source_target_pairs={{0,64},{32,96},{64,0},{96,32},{1,65},{33,97},{65,1},{97,33},{2,66}... | collective-permute-start | bytes 12296 | tf_op jit(solution)/shard_map/ppermute | solution.py:358
  293.2 2.7 collective-permute-start.16
  298.7 6.7 %collective-permute-start.17 = (bf16[528,128]{1,0:T(8,128)(2,1)}, bf16[528,128]{1,0:T(8,128)(2,1)S(1)}, u32[]{:S(2)}, u32[]{:S(2)}) collective-permute-start(bf16[528,128]{1,0:T(8,128)(2,1)} %loss.1.g0), channel_id=1, source_target_pairs={{0,32},{32,64},{64,96},{96,0},{1,33},{33,65},{65,97},{97,1},{2,34}... | collective-permute-start | bytes 405512 | tf_op jit(solution)/shard_map/ppermute | solution.py:358
  298.7 6.7 %collective-permute-start.18 = (bf16[528,128]{1,0:T(8,128)(2,1)}, bf16[528,128]{1,0:T(8,128)(2,1)S(1)}, u32[]{:S(2)}, u32[]{:S(2)}) collective-permute-start(bf16[528,128]{1,0:T(8,128)(2,1)} %loss.1.g0), channel_id=1, source_target_pairs={{0,64},{32,96},{64,0},{96,32},{1,65},{33,97},{65,1},{97,33},{2,66}... | collective-permute-start | bytes 405512 | tf_op jit(solution)/shard_map/ppermute | solution.py:358
  301.1 5.0 %collective-permute-start.19 = (bf16[528,128]{1,0:T(8,128)(2,1)}, bf16[528,128]{1,0:T(8,128)(2,1)S(1)}, u32[]{:S(2)}, u32[]{:S(2)}) collective-permute-start(bf16[528,128]{1,0:T(8,128)(2,1)} %loss.1.g0), channel_id=1, source_target_pairs={{0,96},{32,0},{64,32},{96,64},{1,97},{33,1},{65,33},{97,65},{2,98}... | collective-permute-start | bytes 405512 | tf_op jit(solution)/shard_map/ppermute | solution.py:358
  338.6 8.9 %copy-start.19 = (f32[8,128]{1,0:T(8,128)S(1)}, f32[8,128]{1,0:T(8,128)}, u32[]{:S(2)}) copy-start(f32[8,128]{1,0:T(8,128)} %get-tuple-element.27) | copy-start | bytes 12292
  347.5 1.3 collective-permute-start.21
  (13 other events, 23.2 us)
Sparse Core Ops, SparseCore 0:
  115.4 60.7 all-gather.2
  347.6 44.5 all-gather.4

commit v2 on v1

--- a/solution.py
+++ b/solution.py
@@ -58,8 +58,17 @@
     return jax.ShapeDtypeStruct(dims, dtype)
 
 
-def pick_outgoing_kernel(ids, meta, cache, out, sem):
-    y, core, me = meta[0], meta[1], meta[2]
+def place():
+    return lax.axis_index("y"), lax.axis_index("c"), lax.axis_index(("z", "x"))
+
+
+def slots_in_use(counts):
+    _, core, me = place()
+    return counts[2 * me + core]
+
+
+def pick_outgoing_kernel(ids, cache, out, sem):
+    y, core, me = place()
     lat = pl.multiple_of(y * LATC, 16)
     idx = pl.multiple_of(DK + y * IDXC, 16)
 
@@ -76,7 +85,7 @@
     def per_dst(dst, total):
         count = jnp.int32(0)
         for s in range(SEL):
-            block = ids[2 * dst + core, s]
+            block = ids[s, 2 * dst + core]
             mine = lax.shift_right_logical(block, 5) == me
 
             @pl.when(mine)
@@ -97,14 +106,15 @@
     lax.fori_loop(0, total, wait, 0)
 
 
-def pick_listed_kernel(ids, meta, arrived, lat, idx, seen, sem):
-    core, me = meta[1], meta[2]
+def pick_listed_kernel(ids, arrived, *refs):
+    lat, idx, seen, sem = refs[-4:]
+    _, core, me = place()
     row = 2 * me + core
     for i in range(NQ):
         seen[i] = 0
     pending = []
     for s in range(SEL):
-        owner = lax.shift_right_logical(ids[row, s], 5)
+        owner = lax.shift_right_logical(ids[s, row], 5)
         rank = jnp.minimum(seen[owner], CAP - 1)
         seen[owner] = seen[owner] + 1
         pending.append(
@@ -119,8 +129,8 @@
         c.wait()
 
 
-def index_query_kernel(meta, x, w, hw, mine, other):
-    core = meta[1]
+def index_query_kernel(x, w, hw, mine, other):
+    core = lax.axis_index("c")
     for k in range(4):
         cols = HALF_COLS // 4
         part = jnp.dot(x[...], w[:, k * cols : (k + 1) * cols], preferred_element_type=F32)
@@ -145,22 +155,22 @@
     other[tail, :] = jnp.where(first, ext[:, BLK:], ext[:, :BLK]).astype(BF16)
 
 
-def head_rows(iq):
-    tail = iq[HALF_COLS:, :].astype(F32)
+def head_rows(tail):
+    tail = tail.astype(F32)
     return tail[0:8] + tail[8:16] + tail[16:24]
 
 
-def logits_kernel(meta, i0, i1, i2, i3, *rest):
-    iq_refs, (logits_ref, stats_ref, keys, total) = rest[:8], rest[8:]
-    y, count = meta[0], meta[3]
+def logits_kernel(counts, i0, i1, i2, i3, *rest):
+    iq_refs, (logits_ref, stats_ref, keys, total) = rest[:4], rest[4:]
+    y, count = lax.axis_index("y"), slots_in_use(counts)
     for s, piece in enumerate((i0, i1, i2, i3)):
         start = pl.multiple_of(lax.rem(y + NY - s, NY) * IDXC, IDXC)
         for j in range(4):
             keys[pl.ds(start, IDXC), j * BLK : (j + 1) * BLK] = piece[4 * y + j]
     keys_t = keys[...].T
     total[...] = jnp.zeros_like(total)
-    for ref in iq_refs:
-        rows = head_rows(ref)
+    for ref in [r.at[n] for r in iq_refs for n in range(2)]:
+        rows = head_rows(ref[HALF_COLS:, :])
         for p in range(4):
             a, b = 2 * p, 2 * p + 1
             pair = jnp.concatenate(
@@ -181,10 +191,25 @@
     stats_ref[...] = jnp.where(row == 0, peak, mass)
 
 
+def split_rows(row):
+    hi = row.astype(BF16).astype(F32)
+    mid = (row - hi).astype(BF16).astype(F32)
+    return hi, mid, row - hi - mid
+
+
+def tail_tile(rows):
+    at = lax.broadcasted_iota(I32, (16, BLK), 0)
+    tile = jnp.zeros((16, BLK), F32)
+    for n, row in enumerate(rows):
+        tile = jnp.where(at == n, row, tile)
+    return tile.astype(BF16)
+
+
 def target_kernel(
-    meta, l0, l1, l2, l3, q_own, q_other, o0, o1, o2, o3, keys, keys_t, qa, qb, buf_a, buf_b, total, sems
+    counts, stats, l0, l1, l2, l3, q_own, q_other, o0, o1, o2, o3, keys, keys_t, qa, qb, buf_a, buf_b, total, sems
 ):
-    y, core, count = meta[0], meta[1], meta[3]
+    y, core, _ = place()
+    count = slots_in_use(counts)
     copies = []
     for s, piece in enumerate((l0, l1, l2, l3)):
         start = pl.multiple_of(lax.rem(y + NY - s, NY) * LATC, LATC)
@@ -255,35 +280,35 @@
     peak_b = scores(pairs - 1, buf_b)
     spread(buf_a, peak_a)
     spread(buf_b, peak_b)
+    tail = tail_tile(split_rows(stats[0:1, :]) + split_rows(stats[1:2, :]))
     for s, out in enumerate((o0, o1, o2, o3)):
         start = pl.multiple_of(lax.rem(y + s, NY) * OWNK, OWNK)
-        out[...] = total[pl.ds(start, OWNK), :].astype(BF16)
-
-
-def loss_kernel(t0, t1, t2, t3, logits, s0, s1, s2, s3, out):
-    stats = [s[...] for s in (s0, s1, s2, s3)]
-    peak = functools.reduce(jnp.maximum, [s[0:1] for s in stats])
-    mass = functools.reduce(jnp.add, [s[1:2] * jnp.exp(s[0:1] - peak) for s in stats])
+        out[:OWNK, :] = total[pl.ds(start, OWNK), :].astype(BF16)
+        out[OWNK:, :] = tail
+
+
+def loss_kernel(t0, t1, t2, t3, logits, out):
+    pieces = (t0, t1, t2, t3)
+    tails = [t[OWNK:, :].astype(F32) for t in pieces]
+    peaks = [t[0:1] + t[1:2] + t[2:3] for t in tails]
+    masses = [t[3:4] + t[4:5] + t[5:6] for t in tails]
+    peak = functools.reduce(jnp.maximum, peaks)
+    mass = functools.reduce(jnp.add, [m * jnp.exp(p - peak) for m, p in zip(masses, peaks)])
     log_total = peak + jnp.log(mass)
-    target = t0[...].astype(F32) + t1[...].astype(F32) + t2[...].astype(F32) + t3[...].astype(F32)
+    target = functools.reduce(jnp.add, [t[:OWNK, :].astype(F32) for t in pieces])
     masked = logits[...]
     valid = masked > 0.5 * masked_value
     log_probs = masked - log_total
     entropy = -jnp.sum(jnp.where(valid, target * log_probs, 0.0), axis=0, keepdims=True)
     grad = jnp.where(valid, jnp.exp(log_probs) - target, 0.0) / QUERIES
     out[:OWNK, :] = grad.astype(BF16)
-    hi = entropy.astype(BF16).astype(F32)
-    mid = (entropy - hi).astype(BF16).astype(F32)
-    lo = entropy - hi - mid
-    row = lax.broadcasted_iota(I32, (16, BLK), 0)
-    ext = jnp.where(row == 0, hi, jnp.where(row == 1, mid, jnp.where(row == 2, lo, 0.0)))
-    out[OWNK:, :] = ext.astype(BF16)
+    out[OWNK:, :] = tail_tile(split_rows(entropy))
 
 
 def backward_kernel(
-    meta, g0, g1, g2, g3, i0, i1, i2, i3, iq0, iq1, out, entropy_ref, keys, keys_t, grads
+    g0, g1, g2, g3, i0, i1, i2, i3, iq, out, entropy_ref, keys, keys_t, grads
 ):
-    y = meta[0]
+    y = lax.axis_index("y")
     entropy = jnp.zeros((1, BLK), F32)
     for s, piece in enumerate((g0, g1, g2, g3)):
         start = pl.multiple_of(lax.rem(y + NY - s, NY) * OWNK, OWNK)
@@ -298,8 +323,9 @@
     for j in range(SEL):
         keys_t[j * BLK : (j + 1) * BLK, :] = keys[:, j * BLK : (j + 1) * BLK].T
     chunk = 512
-    for core, ref in enumerate((iq0, iq1)):
-        rows = head_rows(ref)
+    for core in range(2):
+        ref = iq.at[core]
+        rows = head_rows(ref[HALF_COLS:, :])
         for p in range(4):
             a, b = 2 * p, 2 * p + 1
             pair = jnp.concatenate(
@@ -320,7 +346,7 @@
                 out[4 * head + 2 + core] = acc[COLS:, lanes]
 
 
-def weight_kernel(meta, qg, xa, xb, out, lhs, acc):
+def weight_kernel(qg, xa, xb, out, lhs, acc):
     step = pl.program_id(0)
     chunk = xa.shape[0]
 
@@ -336,7 +362,7 @@
 
     @pl.when(step == pl.num_programs(0) - 1)
     def _():
-        own_first = jnp.broadcast_to(meta[1] == 0, acc.shape[1:])
+        own_first = jnp.broadcast_to(lax.axis_index("c") == 0, acc.shape[1:])
         half = acc.shape[2]
         out[:, :half] = jnp.where(own_first, acc[0], acc[1]).astype(BF16)
         out[:, half:] = jnp.where(own_first, acc[1], acc[0]).astype(BF16)
@@ -362,28 +388,26 @@
 def on_device(
     q_absorbed, key_cache, index_input, index_weight, head_weights, block_ids, block_counts
 ):
-    y, core = lax.axis_index("y"), lax.axis_index("c")
-    me = lax.axis_index(("z", "x"))
-    count = lax.dynamic_index_in_dim(block_counts, 2 * me + core, 0, keepdims=False)
-    meta = jnp.stack([y, core, me, count]).astype(I32)
+    y, core, _ = place()
+    ids = block_ids.T
 
     outgoing = call(
         pick_outgoing_kernel,
         shape((NQ, CAP, PIECE, BLK), BF16),
-        [SMEM, SMEM, ANY],
-        ANY,
+        [SMEM, ANY],
+        VMEM,
         [pltpu.SemaphoreType.DMA((2,))],
         "pick_outgoing",
-    )(block_ids, meta, key_cache)
+    )(ids, key_cache)
     arrived = lax.all_to_all(outgoing, ("z", "x"), split_axis=0, concat_axis=0, tiled=True)
 
     iq_own, iq_send = call(
         index_query_kernel,
         (shape((IQ_ROWS, BLK), BF16),) * 2,
-        [SMEM, VMEM, VMEM, VMEM],
+        [VMEM, VMEM, VMEM],
         (VMEM, VMEM),
         name="index_query",
-    )(meta, index_input, index_weight, head_weights.T)
+    )(index_input, index_weight, head_weights.T)
     iq_other = lax.ppermute(iq_send, "c", SWAP)
     first = core == 0
     iq_pair = jnp.stack(
@@ -398,34 +422,33 @@
     lat, idx = call(
         pick_listed_kernel,
         (shape((SEL, LATC, BLK), BF16), shape((SEL, IDXC, BLK), BF16)),
-        [SMEM, SMEM, ANY],
-        (ANY, ANY),
+        [SMEM] + [ANY] * 5,
+        (VMEM, VMEM),
         [pltpu.SMEM((NQ,), I32), pltpu.SemaphoreType.DMA((2,))],
         "pick_listed",
-    )(block_ids, meta, arrived)
+    )(ids, arrived, q_send, *iq_all[1:])
     idx_all = around_y(idx)
+    lat = lax.optimization_barrier((lat, *idx_all[1:]))[0]
     lat_all = around_y(lat)
 
     half = DQ // 2
     x_half = lax.dynamic_slice_in_dim(index_input, core * half, half, 1)
-    x_half, _ = lax.optimization_barrier((x_half, arrived))
+    x_half, _ = lax.optimization_barrier((x_half, idx))
     x_own = lax.all_gather(x_half, ("z", "x"), axis=0, tiled=True)
-    x_other = lax.ppermute(x_own, "c", SWAP)
 
     logits, stats = call(
         logits_kernel,
         (shape((OWNK, BLK), F32), shape((8, BLK), F32)),
-        [SMEM] + [VMEM] * 12,
+        [SMEM] + [VMEM] * 8,
         (VMEM, VMEM),
         [pltpu.VMEM((ID, OWNK), BF16), pltpu.VMEM((OWNK, BLK), F32)],
         "index_logits",
-    )(meta, *idx_all, *[a[n] for a in iq_all for n in range(2)])
-    stats_all = around_y(stats)
+    )(block_counts, *idx_all, *iq_all)
 
     targets = call(
         target_kernel,
-        (shape((OWNK, BLK), BF16),) * 4,
-        [SMEM] + [ANY] * 6,
+        (shape((LG_ROWS, BLK), BF16),) * 4,
+        [SMEM, VMEM] + [ANY] * 6,
         (VMEM,) * 4,
         [
             pltpu.VMEM((DK, KEYS), BF16),
@@ -438,22 +461,24 @@
             pltpu.SemaphoreType.DMA((3,)),
         ],
         "attention_target",
-    )(meta, *lat_all, q_t, q_other)
+    )(block_counts, stats, *lat_all, q_t, q_other)
+    x_own, _ = lax.optimization_barrier((x_own, targets[0]))
+    x_other = lax.ppermute(x_own, "c", SWAP)
     arrived_targets = {s: lax.ppermute(targets[s], "y", ring(s)) for s in SHIFTS}
 
     grads = call(
         loss_kernel,
         shape((LG_ROWS, BLK), BF16),
-        [VMEM] * 9,
+        [VMEM] * 5,
         VMEM,
         name="loss",
-    )(targets[0], arrived_targets[1], arrived_targets[2], arrived_targets[3], logits, *stats_all)
+    )(targets[0], arrived_targets[1], arrived_targets[2], arrived_targets[3], logits)
     grads_all = around_y(grads)
 
     query_grad, entropy = call(
         backward_kernel,
         (shape((2 * NQ, COLS, BLK), BF16), shape((8, BLK), F32)),
-        [SMEM] + [VMEM] * 10,
+        [VMEM] * 9,
         (VMEM, VMEM),
         [
             pltpu.VMEM((ID, KEYS), BF16),
@@ -461,7 +486,7 @@
             pltpu.VMEM((KEYS, BLK), F32),
         ],
         "index_backward",
-    )(meta, *grads_all, *idx_all, iq_pair[0], iq_pair[1])
+    )(*grads_all, *idx_all, iq_pair)
     entropy_other = lax.ppermute(entropy, "c", SWAP)
     entropy_both = jnp.where(
         first,
@@ -478,7 +503,6 @@
         grid=(QUERIES // chunk,),
         out_shape=shape((COLS, DQ), BF16),
         in_specs=[
-            SMEM,
             pl.BlockSpec((2 * NQ, COLS, BLK), lambda i: (0, 0, 0)),
             pl.BlockSpec((chunk, half), lambda i: (i, 0)),
             pl.BlockSpec((chunk, half), lambda i: (i, 0)),
@@ -490,7 +514,7 @@
         ],
         compiler_params=pltpu.CompilerParams(vmem_limit_bytes=VMEM_LIMIT),
         name="weight_piece",
-    )(meta, swapped, x_own, x_other)
+    )(swapped, x_own, x_other)
     gathered = lax.all_gather(piece, ("z", "x"), axis=0, tiled=True)
     weight_grad = pl.pallas_call(
         finish_kernel,

time: 408 us -> 248 us (0.61)
  waiting for transfers between devices: 175 us -> 101 us
  starting transfers between devices: 79.5 us -> 34.3 us
  Pallas kernels: 96.2 us -> 65.9 us
  blocking collectives: 25.7 us -> 20.2 us
    all_gather x1, waiting for transfers between devices: 60.8 us -> 0.02 us  [on_device(): x_own = lax.all_gather(x_half, ('z', 'x'), axis=0, tiled=True)]
    all_to_all x1, starting transfers between devices: 58 us -> 8.29 us  [on_device(): lax.all_to_all(outgoing, ('z', 'x'), split_axis=0, concat_axis=0, tiled=T...]
    all_to_all x1, waiting for transfers between devices: 30.9 us -> 0.01 us  [on_device(): lax.all_to_all(outgoing, ('z', 'x'), split_axis=0, concat_axis=0, tiled=T...]
    pallas_call x1, Pallas kernels: 23.9 us -> 2.84 us  [on_device(): call(pick_listed_kernel, (shape((SEL, LATC, BLK), BF16), shape((SEL, IDXC...]
    ppermute x15 -> x12, waiting for transfers between devices: 37 us -> 50.6 us  [around_y(): moved = {s: lax.ppermute(array, 'y', ring(s)) for s in SHIFTS}]
    pallas_call x4, Pallas kernels: 46.2 us -> 37 us  [the longest x1 25.9 us: on_device(): call(target_kernel, (shape((LG_ROWS, BLK), BF16),) * 4, [SMEM, VMEM] + [A...]
    ppermute x3, waiting for transfers between devices: 0.01 us -> 6.37 us  [on_device(): lax.ppermute(targets[s], 'y', ring(s))]
    all_to_all x1, blocking collectives: 25.7 us -> 20.2 us  [on_device(): lax.all_to_all(query_grad, ('z', 'x', 'c'), split_axis=0, concat_axis=0,...]
  transfers between devices with their start and end apart: 25 -> 22, of which waited for: 13 -> 14; matrix products, arithmetic and copies ran while one was open for 2% -> 2% of each run, Pallas kernels for 16% -> 17%
where the time goes in v2:
time: 248 us; the launch traced here: 247 us
  waiting for transfers between devices  101 us (41%)
  Pallas kernels  65.9 us (27%)
  starting transfers between devices  34.3 us (14%)
  blocking collectives  20.2 us (8%)
  between operations  14.2 us (6%)
  local copies, waits for them, and re-layouts  10.4 us (4%)
    ppermute x12, waiting for transfers between devices, around_y(): moved = {s: lax.ppermute(array, 'y', ring(s)) for s in SHIFTS}  50.6 us
    all_gather x1, waiting for transfers between devices, on_device(): gathered = lax.all_gather(piece, ('z', 'x'), axis=0, tiled=True)  41.8 us
    pallas_call x1, Pallas kernels, on_device(): call(target_kernel, (shape((LG_ROWS, BLK), BF16),) * 4, [SMEM, VMEM] + [A...  25.9 us
    all_to_all x1, blocking collectives, on_device(): lax.all_to_all(query_grad, ('z', 'x', 'c'), split_axis=0, concat_axis=0,...  20.2 us
    ppermute x12, starting transfers between devices, around_y(): moved = {s: lax.ppermute(array, 'y', ring(s)) for s in SHIFTS}  18 us
    pallas_call x1, Pallas kernels, on_device(): pl.pallas_call(weight_kernel, grid=(QUERIES // chunk,), out_shape=shape((...  8.83 us
    all_to_all x1, starting transfers between devices, on_device(): lax.all_to_all(outgoing, ('z', 'x'), split_axis=0, concat_axis=0, tiled=T...  8.29 us
    ppermute x3, waiting for transfers between devices, on_device(): lax.ppermute(targets[s], 'y', ring(s))  6.37 us
  transfers between devices with their start and end apart: 22, of which 14 were waited for; matrix products, arithmetic and copies ran while one was open for 2% of the time, Pallas kernels for 17%

profile of v2, /device:TPU:1, one launch (start us, length us, event | category | flops | bytes accessed | tf_op | source)
XLA Modules:
  0.0 247.1 jit_solution(12270563085025149610)
XLA Ops:
  7.2 5.0 %pick_outgoing.1 = bf16[16,3,176,128]{3,2,1,0:T(8,128)(2,1)} custom-call(s32[16,32]{1,0:T(8,128)} %bitcast.14, bf16[32,704,128]{2,1,0:T(8,128)(2,1)} %cache.1), custom_call_target="tpu_custom_call" | custom-call | tf_op jit(solution)/shard_map/pick_outgoing/pallas_call | solution.py:394
  12.2 8.3 %all-to-all-start = ((bf16[16,3,176,128]{3,2,1,0:T(8,128)(2,1)}), bf16[16,3,176,128]{3,2,1,0:T(8,128)(2,1)}, u32[]{:S(2)}, u32[]{:S(2)}) async-start(bf16[16,3,176,128]{3,2,1,0:T(8,128)(2,1)} %pick_outgoing.1), calls=%async_computation | async-start | bytes 4325376 | tf_op jit(solution)/shard_map/all_to_all | solution.py:402
  20.6 4.0 %index_query.1 = (bf16[1056,128]{1,0:T(8,128)(2,1)}, bf16[1056,128]{1,0:T(8,128)(2,1)}) custom-call(bf16[256,1536]{1,0:T(8,128)(2,1)} %x.1, bf16[1536,1024]{1,0:T(8,128)(2,1)} %w.1, f32[8,256]{1,0:T(8,128)} %bitcast.16), custom_call_target="tpu_custom_call" | custom-call | tf_op jit(solution)/shard_map/index_query/pallas_call | solution.py:404
  25.8 1.4 collective-permute-done
  29.6 2.6 %collective-permute-start.2 = (bf16[2,1056,128]{2,1,0:T(8,128)(2,1)S(1)}, bf16[2,1056,128]{2,1,0:T(8,128)(2,1)}, u32[]{:S(2)}, u32[]{:S(2)}) collective-permute-start(bf16[2,1056,128]{2,1,0:T(8,128)(2,1)S(1)} %pad_maximum_fusion.rest_0_.iq), channel_id=1, source_target_pairs={{0,64},{32,96},{64,0},{96,32},{1,65},{33,97},{65,1},{97,33},{2,66}... | collective-permute-start | bytes 1622024 | tf_op jit(solution)/shard_map/ppermute | solution.py:384
  34.1 3.2 %dynamic-slice_bitcast_fusion.refs_0_ = bf16[16,576,128]{2,1,0:T(8,128)(2,1)} fusion(bf16[256,16,576]{0,2,1:T(8,128)(2,1)} %param.7, s32[]{:T(128)S(6)} %select_n.29), kind=kLoop, calls=%fused_computation | loop fusion | bytes 4718596 | tf_op jit(solution)/shard_map/dynamic_slice | solution.py:419
  37.3 5.9 %collective-permute-done.1.refs_1_.rest_1_ = bf16[2,1056,128]{2,1,0:T(8,128)(2,1)S(1)} collective-permute-done((bf16[2,1056,128]{2,1,0:T(8,128)(2,1)S(1)}, bf16[2,1056,128]{2,1,0:T(8,128)(2,1)S(1)}, u32[]{:S(2)}, u32[]{:S(2)}) %collective-permute-start.1) | collective-permute-done | bytes 540704 | tf_op jit(solution)/shard_map/ppermute | solution.py:384
  43.3 12.7 %collective-permute-done.2.refs_2_.rest_2_ = bf16[2,1056,128]{2,1,0:T(8,128)(2,1)} collective-permute-done((bf16[2,1056,128]{2,1,0:T(8,128)(2,1)S(1)}, bf16[2,1056,128]{2,1,0:T(8,128)(2,1)}, u32[]{:S(2)}, u32[]{:S(2)}) %collective-permute-start.2) | collective-permute-done | bytes 540704 | tf_op jit(solution)/shard_map/ppermute | solution.py:384
  56.0 2.8 %pick_listed.1 = (bf16[16,144,128]{2,1,0:T(8,128)(2,1)}, bf16[16,32,128]{2,1,0:T(8,128)(2,1)}) custom-call(s32[16,32]{1,0:T(8,128)} %bitcast.15, bf16[16,3,176,128]{3,2,1,0:T(8,128)(2,1)} %all-to-all-done.arrived, bf16[16,576,128]{2,1,0:T(8,128)(2,1)} %dynamic-slice_bitcast_fusion.refs_0_, bf16[2,1056,128]{2,1,0:T(8,128)(2,1)} %copy-done.4, ...), custom_call_target="tpu_custom_call" | custom-call | tf_op jit(solution)/shard_map/pick_listed/pallas_call | solution.py:422
  61.2 2.1 collective-permute-start.5
  64.6 2.1 collective-permute-done.4.i1
  66.7 3.2 %collective-permute-done.5.i2 = bf16[16,32,128]{2,1,0:T(8,128)(2,1)S(1)} collective-permute-done((bf16[16,32,128]{2,1,0:T(8,128)(2,1)}, bf16[16,32,128]{2,1,0:T(8,128)(2,1)S(1)}, u32[]{:S(2)}, u32[]{:S(2)}) %collective-permute-start.5) | collective-permute-done | bytes 131104 | tf_op jit(solution)/shard_map/ppermute | solution.py:384
  69.9 1.8 collective-permute-start.7
  71.7 2.2 collective-permute-start.8
  74.2 4.9 %index_logits.1 = (f32[512,128]{1,0:T(8,128)}, f32[8,128]{1,0:T(8,128)}) custom-call(s32[32]{0:T(128)} %counts.3, bf16[16,32,128]{2,1,0:T(8,128)(2,1)} %get-tuple-element.19.i0, bf16[16,32,128]{2,1,0:T(8,128)(2,1)} %copy-done.9, bf16[16,32,128]{2,1,0:T(8,128)(2,1)} %copy-done.10, bf16[16,32,128]{2,1,0:T(8,128)(2,1)} %copy-done.11, ...), custom_call_target="tpu_custom_call" | custom-call | tf_op jit(solution)/shard_map/index_logits/pallas_call | solution.py:439
  79.1 6.3 %collective-permute-done.7.l1 = bf16[16,144,128]{2,1,0:T(8,128)(2,1)S(1)} collective-permute-done((bf16[16,144,128]{2,1,0:T(8,128)(2,1)}, bf16[16,144,128]{2,1,0:T(8,128)(2,1)S(1)}, u32[]{:S(2)}, u32[]{:S(2)}) %collective-permute-start.7) | collective-permute-done | bytes 589856 | tf_op jit(solution)/shard_map/ppermute | solution.py:384
  85.5 14.1 %collective-permute-done.8.l2 = bf16[16,144,128]{2,1,0:T(8,128)(2,1)S(1)} collective-permute-done((bf16[16,144,128]{2,1,0:T(8,128)(2,1)}, bf16[16,144,128]{2,1,0:T(8,128)(2,1)S(1)}, u32[]{:S(2)}, u32[]{:S(2)}) %collective-permute-start.8) | collective-permute-done | bytes 589856 | tf_op jit(solution)/shard_map/ppermute | solution.py:384
  100.6 25.9 %attention_target.1 = (bf16[528,128]{1,0:T(8,128)(2,1)}, bf16[528,128]{1,0:T(8,128)(2,1)}, bf16[528,128]{1,0:T(8,128)(2,1)}, bf16[528,128]{1,0:T(8,128)(2,1)}) custom-call(s32[32]{0:T(128)} %counts.3, f32[8,128]{1,0:T(8,128)} %get-tuple-element.20.stats, bf16[16,144,128]{2,1,0:T(8,128)(2,1)} %get-tuple-element.22.l0, bf16[16,144,128]{2,1,0:T(8,128)(2,1)} %copy-done.6, ...), custom_call_target="tpu_custom_call" | custom-call | tf_op jit(solution)/shard_map/attention_target/pallas_call | solution.py:448
  126.6 1.6 collective-permute-start.17
  128.8 2.1 collective-permute-start.12
  131.5 3.2 %collective-permute-done.11.t1 = bf16[528,128]{1,0:T(8,128)(2,1)S(1)} collective-permute-done((bf16[528,128]{1,0:T(8,128)(2,1)}, bf16[528,128]{1,0:T(8,128)(2,1)S(1)}, u32[]{:S(2)}, u32[]{:S(2)}) %collective-permute-start.11) | collective-permute-done | bytes 135200 | tf_op jit(solution)/shard_map/ppermute | solution.py:467
  134.7 2.9 %collective-permute-done.12.t2 = bf16[528,128]{1,0:T(8,128)(2,1)S(1)} collective-permute-done((bf16[528,128]{1,0:T(8,128)(2,1)}, bf16[528,128]{1,0:T(8,128)(2,1)S(1)}, u32[]{:S(2)}, u32[]{:S(2)}) %collective-permute-start.12) | collective-permute-done | bytes 135200 | tf_op jit(solution)/shard_map/ppermute | solution.py:467
  138.6 2.0 loss.1.g0
  141.9 2.9 %collective-permute-start.15 = (bf16[528,128]{1,0:T(8,128)(2,1)}, bf16[528,128]{1,0:T(8,128)(2,1)S(1)}, u32[]{:S(2)}, u32[]{:S(2)}) collective-permute-start(bf16[528,128]{1,0:T(8,128)(2,1)} %loss.1.g0), channel_id=1, source_target_pairs={{0,64},{32,96},{64,0},{96,32},{1,65},{33,97},{65,1},{97,33},{2,66}... | collective-permute-start | bytes 405512 | tf_op jit(solution)/shard_map/ppermute | solution.py:384
  144.8 1.9 collective-permute-done.14.g1
  146.7 4.4 %collective-permute-done.15.g2 = bf16[528,128]{1,0:T(8,128)(2,1)S(1)} collective-permute-done((bf16[528,128]{1,0:T(8,128)(2,1)}, bf16[528,128]{1,0:T(8,128)(2,1)S(1)}, u32[]{:S(2)}, u32[]{:S(2)}) %collective-permute-start.15) | collective-permute-done | bytes 135200 | tf_op jit(solution)/shard_map/ppermute | solution.py:384
  152.4 6.1 %index_backward.1 = (bf16[32,64,128]{2,1,0:T(8,128)(2,1)}, f32[8,128]{1,0:T(8,128)}) custom-call(bf16[528,128]{1,0:T(8,128)(2,1)} %loss.1.g0, bf16[528,128]{1,0:T(8,128)(2,1)} %copy-done.12, bf16[528,128]{1,0:T(8,128)(2,1)} %copy-done.14, bf16[528,128]{1,0:T(8,128)(2,1)} %copy-done.16, bf16[16,32,128]{2,1,0:T(8,128)(2,1)} %get-tuple-element.19.i0, ...), custom_call_target="tpu_custom_call" | custom-call | tf_op jit(solution)/shard_map/index_backward/pallas_call | solution.py:478
  158.6 20.2 %all_to_all.10.qg = bf16[32,64,128]{2,1,0:T(8,128)(2,1)} all-to-all(bf16[32,64,128]{2,1,0:T(8,128)(2,1)} %get-tuple-element.28), channel_id=1, replica_groups=mesh['y'=4,'c'=2,'z'=4,'x'=4] {'z','x','c'}, dimensions={0} | all-to-all | bytes 1048576 | tf_op jit(solution)/shard_map/all_to_all | solution.py:499
  178.8 2.7 %copy-done.1 = bf16[4096,768]{1,0:T(8,128)(2,1)} copy-done((bf16[4096,768]{1,0:T(8,128)(2,1)}, bf16[4096,768]{1,0:T(8,128)(2,1)S(1)}, u32[]{:S(2)}) %copy-start.1) | copy-done | bytes 6291480
  181.5 8.8 %weight_piece.1 = bf16[64,1536]{1,0:T(8,128)(2,1)} custom-call(bf16[32,64,128]{2,1,0:T(8,128)(2,1)} %all_to_all.10.qg, bf16[4096,768]{1,0:T(8,128)(2,1)} %all-gather.3.cloned.1.call-done.xa, bf16[4096,768]{1,0:T(8,128)(2,1)} %copy-done.1), custom_call_target="tpu_custom_call" | custom-call | tf_op jit(solution)/shard_map/weight_piece/pallas_call | solution.py:501
  192.3 41.8 %all-gather.5.cloned.1.call-done.gathered = bf16[1024,1536]{1,0:T(8,128)(2,1)} async-done(((bf16[64,1536]{1,0:T(8,128)(2,1)}), bf16[1024,1536]{1,0:T(8,128)(2,1)}) %all-gather.5.cloned.1.call-update) | async-done | bytes 3145744 | tf_op jit(solution)/shard_map/all_gather | solution.py:518
  234.2 6.1 %finish.1 = f32[1536,1024]{1,0:T(8,128)} custom-call(bf16[1024,1536]{1,0:T(8,128)(2,1)} %all-gather.5.cloned.1.call-done.gathered), custom_call_target="tpu_custom_call" | custom-call | tf_op jit(solution)/shard_map/finish/pallas_call | solution.py:519
  (70 shorter events, 17.4 us)
Async XLA Ops:
  12.2 43.8 %all-to-all-start = ((bf16[16,3,176,128]{3,2,1,0:T(8,128)(2,1)}), bf16[16,3,176,128]{3,2,1,0:T(8,128)(2,1)}, u32[]{:S(2)}, u32[]{:S(2)}) async-start(bf16[16,3,176,128]{3,2,1,0:T(8,128)(2,1)} %pick_outgoing.1), calls=%async_computation | async-start | bytes 4325376 | tf_op jit(solution)/shard_map/all_to_all | solution.py:402
  20.5 12.8 %copy-start.5 = (bf16[256,1536]{1,0:T(8,128)(2,1)S(1)}, bf16[256,1536]{1,0:T(8,128)(2,1)}, u32[]{:S(2)}) copy-start(bf16[256,1536]{1,0:T(8,128)(2,1)} %x.1) | copy-start | bytes 2359300
  20.5 106.1 %all-gather.3.cloned.1.call-start = ((), (), s32[]{:S(2)}) async-start(), calls=%async_computation.2 | async-start | bytes 6684672 | tf_op jit(solution)/shard_map/all_gather | solution.py:437
  24.6 2.7 %collective-permute-start = (bf16[1056,128]{1,0:T(8,128)(2,1)}, bf16[1056,128]{1,0:T(8,128)(2,1)S(1)}, u32[]{:S(2)}, u32[]{:S(2)}) collective-permute-start(bf16[1056,128]{1,0:T(8,128)(2,1)} %get-tuple-element.18), channel_id=1, source_target_pairs={{0,16},{16,0},{1,17},{17,1},{2,18},{18,2},{3,19},{19,3},{4,20},{20... | collective-permute-start | bytes 811016 | tf_op jit(solution)/shard_map/ppermute | solution.py:411
  28.3 30.6 %copy-start.2 = (bf16[2,1056,128]{2,1,0:T(8,128)(2,1)}, bf16[2,1056,128]{2,1,0:T(8,128)(2,1)S(1)}, u32[]{:S(2)}) copy-start(bf16[2,1056,128]{2,1,0:T(8,128)(2,1)S(1)} %pad_maximum_fusion.rest_0_.iq) | copy-start | bytes 1622020
  28.3 15.0 %collective-permute-start.1 = (bf16[2,1056,128]{2,1,0:T(8,128)(2,1)S(1)}, bf16[2,1056,128]{2,1,0:T(8,128)(2,1)S(1)}, u32[]{:S(2)}, u32[]{:S(2)}) collective-permute-start(bf16[2,1056,128]{2,1,0:T(8,128)(2,1)S(1)} %pad_maximum_fusion.rest_0_.iq), channel_id=1, source_target_pairs={{0,32},{32,64},{64,96},{96,0},{1,33},{33,65},{65,97},{97,1},{2,34}... | collective-permute-start | bytes 1622024 | tf_op jit(solution)/shard_map/ppermute | solution.py:384
  29.6 26.3 %collective-permute-start.2 = (bf16[2,1056,128]{2,1,0:T(8,128)(2,1)S(1)}, bf16[2,1056,128]{2,1,0:T(8,128)(2,1)}, u32[]{:S(2)}, u32[]{:S(2)}) collective-permute-start(bf16[2,1056,128]{2,1,0:T(8,128)(2,1)S(1)} %pad_maximum_fusion.rest_0_.iq), channel_id=1, source_target_pairs={{0,64},{32,96},{64,0},{96,32},{1,65},{33,97},{65,1},{97,33},{2,66}... | collective-permute-start | bytes 1622024 | tf_op jit(solution)/shard_map/ppermute | solution.py:384
  32.3 23.7 %collective-permute-start.3 = (bf16[2,1056,128]{2,1,0:T(8,128)(2,1)S(1)}, bf16[2,1056,128]{2,1,0:T(8,128)(2,1)}, u32[]{:S(2)}, u32[]{:S(2)}) collective-permute-start(bf16[2,1056,128]{2,1,0:T(8,128)(2,1)S(1)} %pad_maximum_fusion.rest_0_.iq), channel_id=1, source_target_pairs={{0,96},{32,0},{64,32},{96,64},{1,97},{33,1},{65,33},{97,65},{2,98}... | collective-permute-start | bytes 1622024 | tf_op jit(solution)/shard_map/ppermute | solution.py:384
  37.3 21.6 %copy-start = (bf16[16,576,128]{2,1,0:T(8,128)(2,1)S(1)}, bf16[16,576,128]{2,1,0:T(8,128)(2,1)}, u32[]{:S(2)}) copy-start(bf16[16,576,128]{2,1,0:T(8,128)(2,1)} %dynamic-slice_bitcast_fusion.refs_0_) | copy-start | bytes 7077892
  43.3 12.7 %copy-start.4 = (bf16[2,1056,128]{2,1,0:T(8,128)(2,1)}, bf16[2,1056,128]{2,1,0:T(8,128)(2,1)S(1)}, u32[]{:S(2)}) copy-start(bf16[2,1056,128]{2,1,0:T(8,128)(2,1)S(1)} %collective-permute-done.1.refs_1_.rest_1_) | copy-start | bytes 1622020
  58.9 175.3 %all-gather.5.cloned.1.call-start = ((), (), s32[]{:S(2)}) async-start(), calls=%async_computation.3 | async-start | bytes 3342336 | tf_op jit(solution)/shard_map/all_gather | solution.py:518
  58.9 20.2 %collective-permute-start.10 = (bf16[16,576,128]{2,1,0:T(8,128)(2,1)S(1)}, bf16[16,576,128]{2,1,0:T(8,128)(2,1)S(1)}, u32[]{:S(2)}, u32[]{:S(2)}) collective-permute-start(bf16[16,576,128]{2,1,0:T(8,128)(2,1)S(1)} %copy-done), channel_id=1, source_target_pairs={{0,16},{16,0},{1,17},{17,1},{2,18},{18,2},{3,19},{19,3},{4,20},{20... | collective-permute-start | bytes 7077896 | tf_op jit(solution)/shard_map/ppermute | solution.py:420
  60.2 6.5 %collective-permute-start.4 = (bf16[16,32,128]{2,1,0:T(8,128)(2,1)}, bf16[16,32,128]{2,1,0:T(8,128)(2,1)S(1)}, u32[]{:S(2)}, u32[]{:S(2)}) collective-permute-start(bf16[16,32,128]{2,1,0:T(8,128)(2,1)} %get-tuple-element.19.i0), channel_id=1, source_target_pairs={{0,32},{32,64},{64,96},{96,0},{1,33},{33,65},{65,97},{97,1},{2,34}... | collective-permute-start | bytes 393224 | tf_op jit(solution)/shard_map/ppermute | solution.py:384
  61.2 8.7 %collective-permute-start.5 = (bf16[16,32,128]{2,1,0:T(8,128)(2,1)}, bf16[16,32,128]{2,1,0:T(8,128)(2,1)S(1)}, u32[]{:S(2)}, u32[]{:S(2)}) collective-permute-start(bf16[16,32,128]{2,1,0:T(8,128)(2,1)} %get-tuple-element.19.i0), channel_id=1, source_target_pairs={{0,64},{32,96},{64,0},{96,32},{1,65},{33,97},{65,1},{97,33},{2,66}... | collective-permute-start | bytes 393224 | tf_op jit(solution)/shard_map/ppermute | solution.py:384
  63.3 6.6 %collective-permute-start.6 = (bf16[16,32,128]{2,1,0:T(8,128)(2,1)}, bf16[16,32,128]{2,1,0:T(8,128)(2,1)S(1)}, u32[]{:S(2)}, u32[]{:S(2)}) collective-permute-start(bf16[16,32,128]{2,1,0:T(8,128)(2,1)} %get-tuple-element.19.i0), channel_id=1, source_target_pairs={{0,96},{32,0},{64,32},{96,64},{1,97},{33,1},{65,33},{97,65},{2,98}... | collective-permute-start | bytes 393224 | tf_op jit(solution)/shard_map/ppermute | solution.py:384
  66.7 7.5 %copy-start.9 = (bf16[16,32,128]{2,1,0:T(8,128)(2,1)}, bf16[16,32,128]{2,1,0:T(8,128)(2,1)S(1)}, u32[]{:S(2)}) copy-start(bf16[16,32,128]{2,1,0:T(8,128)(2,1)S(1)} %collective-permute-done.4.i1) | copy-start | bytes 393220
  69.9 4.3 %copy-start.10 = (bf16[16,32,128]{2,1,0:T(8,128)(2,1)}, bf16[16,32,128]{2,1,0:T(8,128)(2,1)S(1)}, u32[]{:S(2)}) copy-start(bf16[16,32,128]{2,1,0:T(8,128)(2,1)S(1)} %collective-permute-done.5.i2) | copy-start | bytes 393220
  69.9 15.6 %collective-permute-start.7 = (bf16[16,144,128]{2,1,0:T(8,128)(2,1)}, bf16[16,144,128]{2,1,0:T(8,128)(2,1)S(1)}, u32[]{:S(2)}, u32[]{:S(2)}) collective-permute-start(bf16[16,144,128]{2,1,0:T(8,128)(2,1)} %get-tuple-element.22.l0), channel_id=1, source_target_pairs={{0,32},{32,64},{64,96},{96,0},{1,33},{33,65},{65,97},{97,1},{2,34}... | collective-permute-start | bytes 1769480 | tf_op jit(solution)/shard_map/ppermute | solution.py:384
  71.7 27.8 %collective-permute-start.8 = (bf16[16,144,128]{2,1,0:T(8,128)(2,1)}, bf16[16,144,128]{2,1,0:T(8,128)(2,1)S(1)}, u32[]{:S(2)}, u32[]{:S(2)}) collective-permute-start(bf16[16,144,128]{2,1,0:T(8,128)(2,1)} %get-tuple-element.22.l0), channel_id=1, source_target_pairs={{0,64},{32,96},{64,0},{96,32},{1,65},{33,97},{65,1},{97,33},{2,66}... | collective-permute-start | bytes 1769480 | tf_op jit(solution)/shard_map/ppermute | solution.py:384
  73.9 25.6 %collective-permute-start.9 = (bf16[16,144,128]{2,1,0:T(8,128)(2,1)}, bf16[16,144,128]{2,1,0:T(8,128)(2,1)S(1)}, u32[]{:S(2)}, u32[]{:S(2)}) collective-permute-start(bf16[16,144,128]{2,1,0:T(8,128)(2,1)} %get-tuple-element.22.l0), channel_id=1, source_target_pairs={{0,96},{32,0},{64,32},{96,64},{1,97},{33,1},{65,33},{97,65},{2,98}... | collective-permute-start | bytes 1769480 | tf_op jit(solution)/shard_map/ppermute | solution.py:384
  79.1 20.4 %copy-start.3 = (bf16[16,576,128]{2,1,0:T(8,128)(2,1)}, bf16[16,576,128]{2,1,0:T(8,128)(2,1)S(1)}, u32[]{:S(2)}) copy-start(bf16[16,576,128]{2,1,0:T(8,128)(2,1)S(1)} %collective-permute-done.10.q_other) | copy-start | bytes 7077892
  85.5 14.1 %copy-start.6 = (bf16[16,144,128]{2,1,0:T(8,128)(2,1)}, bf16[16,144,128]{2,1,0:T(8,128)(2,1)S(1)}, u32[]{:S(2)}) copy-start(bf16[16,144,128]{2,1,0:T(8,128)(2,1)S(1)} %collective-permute-done.7.l1) | copy-start | bytes 1769476
  126.6 52.2 %collective-permute-start.17 = (bf16[4096,768]{1,0:T(8,128)(2,1)}, bf16[4096,768]{1,0:T(8,128)(2,1)S(1)}, u32[]{:S(2)}, u32[]{:S(2)}) collective-permute-start(bf16[4096,768]{1,0:T(8,128)(2,1)} %all-gather.3.cloned.1.call-done.xa), channel_id=1, source_target_pairs={{0,16},{16,0},{1,17},{17,1},{2,18},{18,2},{3,19},{19,3},{4,20},{20... | collective-permute-start | bytes 18874376 | tf_op jit(solution)/shard_map/ppermute | solution.py:466
  128.2 6.6 %collective-permute-start.11 = (bf16[528,128]{1,0:T(8,128)(2,1)}, bf16[528,128]{1,0:T(8,128)(2,1)S(1)}, u32[]{:S(2)}, u32[]{:S(2)}) collective-permute-start(bf16[528,128]{1,0:T(8,128)(2,1)} %get-tuple-element.24), channel_id=1, source_target_pairs={{0,32},{32,64},{64,96},{96,0},{1,33},{33,65},{65,97},{97,1},{2,34}... | collective-permute-start | bytes 405512 | tf_op jit(solution)/shard_map/ppermute | solution.py:467
  128.8 8.8 %collective-permute-start.12 = (bf16[528,128]{1,0:T(8,128)(2,1)}, bf16[528,128]{1,0:T(8,128)(2,1)S(1)}, u32[]{:S(2)}, u32[]{:S(2)}) collective-permute-start(bf16[528,128]{1,0:T(8,128)(2,1)} %get-tuple-element.25), channel_id=1, source_target_pairs={{0,64},{32,96},{64,0},{96,32},{1,65},{33,97},{65,1},{97,33},{2,66}... | collective-permute-start | bytes 405512 | tf_op jit(solution)/shard_map/ppermute | solution.py:467
  130.9 7.0 %collective-permute-start.13 = (bf16[528,128]{1,0:T(8,128)(2,1)}, bf16[528,128]{1,0:T(8,128)(2,1)S(1)}, u32[]{:S(2)}, u32[]{:S(2)}) collective-permute-start(bf16[528,128]{1,0:T(8,128)(2,1)} %get-tuple-element.26), channel_id=1, source_target_pairs={{0,96},{32,0},{64,32},{96,64},{1,97},{33,1},{65,33},{97,65},{2,98}... | collective-permute-start | bytes 405512 | tf_op jit(solution)/shard_map/ppermute | solution.py:467
  140.6 6.1 %collective-permute-start.14 = (bf16[528,128]{1,0:T(8,128)(2,1)}, bf16[528,128]{1,0:T(8,128)(2,1)S(1)}, u32[]{:S(2)}, u32[]{:S(2)}) collective-permute-start(bf16[528,128]{1,0:T(8,128)(2,1)} %loss.1.g0), channel_id=1, source_target_pairs={{0,32},{32,64},{64,96},{96,0},{1,33},{33,65},{65,97},{97,1},{2,34}... | collective-permute-start | bytes 405512 | tf_op jit(solution)/shard_map/ppermute | solution.py:384
  141.9 9.2 %collective-permute-start.15 = (bf16[528,128]{1,0:T(8,128)(2,1)}, bf16[528,128]{1,0:T(8,128)(2,1)S(1)}, u32[]{:S(2)}, u32[]{:S(2)}) collective-permute-start(bf16[528,128]{1,0:T(8,128)(2,1)} %loss.1.g0), channel_id=1, source_target_pairs={{0,64},{32,96},{64,0},{96,32},{1,65},{33,97},{65,1},{97,33},{2,66}... | collective-permute-start | bytes 405512 | tf_op jit(solution)/shard_map/ppermute | solution.py:384
  144.8 6.3 %collective-permute-start.16 = (bf16[528,128]{1,0:T(8,128)(2,1)}, bf16[528,128]{1,0:T(8,128)(2,1)S(1)}, u32[]{:S(2)}, u32[]{:S(2)}) collective-permute-start(bf16[528,128]{1,0:T(8,128)(2,1)} %loss.1.g0), channel_id=1, source_target_pairs={{0,96},{32,0},{64,32},{96,64},{1,97},{33,1},{65,33},{97,65},{2,98}... | collective-permute-start | bytes 405512 | tf_op jit(solution)/shard_map/ppermute | solution.py:384
  146.7 4.4 %copy-start.12 = (bf16[528,128]{1,0:T(8,128)(2,1)}, bf16[528,128]{1,0:T(8,128)(2,1)S(1)}, u32[]{:S(2)}) copy-start(bf16[528,128]{1,0:T(8,128)(2,1)S(1)} %collective-permute-done.14.g1) | copy-start | bytes 405508
  178.8 11.6 %copy-start.18 = (f32[8,128]{1,0:T(8,128)S(1)}, f32[8,128]{1,0:T(8,128)}, u32[]{:S(2)}) copy-start(f32[8,128]{1,0:T(8,128)} %get-tuple-element.31) | copy-start | bytes 12292
  190.4 1.3 collective-permute-start.18
  (9 other events, 14.8 us)
Sparse Core Ops, SparseCore 0:
  59.0 62.9 all-gather.2
  190.5 43.6 all-gather.4

commit v3 on v2

--- a/solution.py
+++ b/solution.py
@@ -35,7 +35,7 @@
 score_scale = 192.0 ** (-0.5)
 exp2_scale = score_scale * 1.4426950408889634
 masked_value = -1e30
-VMEM_LIMIT = 56 * 1024 * 1024
+VMEM_LIMIT = 40 * 1024 * 1024
 
 ANY = pl.BlockSpec(memory_space=pl.ANY)
 VMEM = pl.BlockSpec(memory_space=pltpu.VMEM)
@@ -56,6 +56,14 @@
 
 def shape(dims, dtype):
     return jax.ShapeDtypeStruct(dims, dtype)
+
+
+def in_hbm(array):
+    return pltpu.with_memory_space_constraint(array, pltpu.HBM)
+
+
+def in_vmem(array):
+    return pltpu.with_memory_space_constraint(array, pltpu.VMEM)
 
 
 def place():
@@ -206,7 +214,7 @@
 
 
 def target_kernel(
-    counts, stats, l0, l1, l2, l3, q_own, q_other, o0, o1, o2, o3, keys, keys_t, qa, qb, buf_a, buf_b, total, sems
+    counts, stats, l0, l1, l2, l3, q_own, qb, o0, o1, o2, o3, keys, keys_t, qa, buf_a, buf_b, total, sems
 ):
     y, core, _ = place()
     count = slots_in_use(counts)
@@ -222,7 +230,6 @@
     lanes = pl.multiple_of(core * BLK, BLK)
     queries = [
         pltpu.make_async_copy(q_own.at[:, :, pl.ds(lanes, BLK)], qa, sems.at[1]),
-        pltpu.make_async_copy(q_other, qb, sems.at[2]),
     ]
     for c in copies + queries:
         c.start()
@@ -234,56 +241,75 @@
     for c in queries:
         c.wait()
 
-    chunk = 256
+    chunk = 512
     token = lax.broadcasted_iota(I32, (BLK, 2 * BLK), 1) % BLK
     causal = lax.broadcasted_iota(I32, (BLK, 2 * BLK), 0) <= token
 
-    def scores(p, buf):
-        pair = jnp.concatenate([qa[p], qb[p]], axis=1)
-        peak = jnp.full((8, 2 * BLK), masked_value, F32)
-        for k in range(KEYS // chunk):
-            part = jnp.dot(
-                keys_t[k * chunk : (k + 1) * chunk, :], pair, preferred_element_type=F32
-            )
-            for j in range(chunk // BLK):
-                slot = k * (chunk // BLK) + j
-                tile = part[j * BLK : (j + 1) * BLK]
-                if slot == 0:
-                    tile = jnp.where(causal, tile, masked_value)
-                else:
-                    tile = jnp.where(slot < count, tile, masked_value)
-                buf[slot * BLK : (slot + 1) * BLK, :] = tile
-                peak = jnp.maximum(peak, jnp.max(tile.reshape(BLK // 8, 8, 2 * BLK), axis=0))
-        return jnp.max(peak, axis=0, keepdims=True)
-
-    def spread(buf, peak):
-        shift = peak * exp2_scale
+    def rows_of(tile):
+        return tile.reshape(tile.shape[0] // 8, 8, 2 * BLK)
+
+    def score_part(pair, buf, k, peak):
+        part = jnp.dot(keys_t[k * chunk : (k + 1) * chunk, :], pair, preferred_element_type=F32)
+        for j in range(chunk // BLK):
+            slot = k * (chunk // BLK) + j
+            tile = part[j * BLK : (j + 1) * BLK]
+            if slot == 0:
+                tile = jnp.where(causal, tile, masked_value)
+            buf[slot * BLK : (slot + 1) * BLK, :] = tile
+            top = jnp.max(rows_of(tile), axis=0)
+            peak = jnp.maximum(peak, jnp.where(slot < count, top, masked_value))
+        return peak
+
+    def exp_part(buf, k, shift, mass):
+        span = slice(k * BLK, (k + 1) * BLK)
+        tile = jnp.exp2(buf[span, :] * exp2_scale - shift)
+        buf[span, :] = tile
+        return mass + jnp.where(k < count, jnp.sum(rows_of(tile), axis=0), 0.0)
+
+    def add_part(buf, k, share):
+        span = slice(k * BLK, (k + 1) * BLK)
+        tile = buf[span, :] * share
+        total[span, :] += tile[:, :BLK] + tile[:, BLK:]
+
+    low = jnp.full((8, 2 * BLK), masked_value, F32)
+    parts = KEYS // chunk
+    step_slots = SEL // (parts // 2)
+
+    def both(p, buf, done, shift):
+        peak = low
+        if p is not None:
+            pair = jnp.concatenate([qa[p], qb[p]], axis=1)
         mass = jnp.zeros((8, 2 * BLK), F32)
-        for j in range(SEL):
-            tile = jnp.exp2(buf[j * BLK : (j + 1) * BLK, :] * exp2_scale - shift)
-            buf[j * BLK : (j + 1) * BLK, :] = tile
-            mass = mass + jnp.sum(tile.reshape(BLK // 8, 8, 2 * BLK), axis=0)
-        share = 1.0 / (jnp.sum(mass, axis=0, keepdims=True) * H)
-        for j in range(SEL):
-            tile = buf[j * BLK : (j + 1) * BLK, :] * share
-            total[j * BLK : (j + 1) * BLK, :] += tile[:, :BLK] + tile[:, BLK:]
-
-    def step(k, peak_a):
-        peak_b = scores(2 * k + 1, buf_b)
-        spread(buf_a, peak_a)
-        peak_next = scores(2 * k + 2, buf_a)
-        spread(buf_b, peak_b)
-        return peak_next
+        for k in range(parts // 2):
+            if p is not None:
+                peak = score_part(pair, buf, k, peak)
+            if done is not None:
+                for n in range(step_slots * k, step_slots * (k + 1)):
+                    mass = exp_part(done, n, shift, mass)
+        if done is not None:
+            share = 1.0 / (jnp.sum(mass, axis=0, keepdims=True) * H)
+        for k in range(parts // 2):
+            if p is not None:
+                peak = score_part(pair, buf, parts // 2 + k, peak)
+            if done is not None:
+                for n in range(step_slots * k, step_slots * (k + 1)):
+                    add_part(done, n, share)
+        return jnp.max(peak, axis=0, keepdims=True) * exp2_scale
+
+    def step(k, shift):
+        shift = both(2 * k + 1, buf_b, buf_a, shift)
+        return both(2 * k + 2, buf_a, buf_b, shift)
 
     pairs = qa.shape[0]
-    peak_a = lax.fori_loop(0, pairs // 2 - 1, step, scores(0, buf_a))
-    peak_b = scores(pairs - 1, buf_b)
-    spread(buf_a, peak_a)
-    spread(buf_b, peak_b)
+    shift = both(0, buf_a, None, None)
+    shift = lax.fori_loop(0, pairs // 2 - 1, step, shift)
+    shift = both(pairs - 1, buf_b, buf_a, shift)
+    both(None, None, buf_b, shift)
     tail = tail_tile(split_rows(stats[0:1, :]) + split_rows(stats[1:2, :]))
     for s, out in enumerate((o0, o1, o2, o3)):
         start = pl.multiple_of(lax.rem(y + s, NY) * OWNK, OWNK)
-        out[:OWNK, :] = total[pl.ds(start, OWNK), :].astype(BF16)
+        used = lax.broadcasted_iota(I32, (OWNK, BLK), 0) + start < count * BLK
+        out[:OWNK, :] = jnp.where(used, total[pl.ds(start, OWNK), :], 0.0).astype(BF16)
         out[OWNK:, :] = tail
 
 
@@ -342,34 +368,70 @@
             acc = acc.astype(BF16)
             for n, head in enumerate((a, b)):
                 lanes = slice(n * BLK, (n + 1) * BLK)
-                out[4 * head + core] = acc[:COLS, lanes]
-                out[4 * head + 2 + core] = acc[COLS:, lanes]
-
-
-def weight_kernel(qg, xa, xb, out, lhs, acc):
-    step = pl.program_id(0)
-    chunk = xa.shape[0]
-
-    @pl.when(step == 0)
-    def _():
-        for s in range(2 * NQ):
-            lhs[s // 4, :, (s % 4) * BLK : (s % 4 + 1) * BLK] = qg[s]
-        acc[...] = jnp.zeros_like(acc)
-
-    left = lhs[step]
-    acc[0] += jnp.dot(left, xa[...], preferred_element_type=F32)
-    acc[1] += jnp.dot(left, xb[...], preferred_element_type=F32)
-
-    @pl.when(step == pl.num_programs(0) - 1)
-    def _():
-        own_first = jnp.broadcast_to(lax.axis_index("c") == 0, acc.shape[1:])
-        half = acc.shape[2]
-        out[:, :half] = jnp.where(own_first, acc[0], acc[1]).astype(BF16)
-        out[:, half:] = jnp.where(own_first, acc[1], acc[0]).astype(BF16)
-
-
-def finish_kernel(gathered, out):
-    out[...] = gathered[...].astype(F32).T
+                out[2 * owner_of_piece(2 * head) + core] = acc[:COLS, lanes]
+                out[2 * owner_of_piece(2 * head + 1) + core] = acc[COLS:, lanes]
+
+
+def owner_of_piece(piece):
+    k, x = piece // 4, piece % 4
+    return (k - 2 * x) % 4 * 4 + x
+
+
+def weight_kernel(qg, xa, xb, out, lhs, own_x, sems):
+    parts = sems.shape[0]
+    span = QUERIES // parts
+    copies = []
+    for k in range(parts):
+        rows = pl.ds(k * span, span)
+        copies.append(pltpu.make_async_copy(xa.at[rows, :], own_x.at[rows, :], sems.at[k]))
+        copies[-1].start()
+    for s in range(2 * NQ):
+        lhs[:, s * BLK : (s + 1) * BLK] = qg[s]
+    other = jnp.dot(lhs[...], xb[...], preferred_element_type=F32).astype(BF16)
+    own = jnp.zeros(other.shape, F32)
+    for k in range(parts):
+        rows = slice(k * span, (k + 1) * span)
+        copies[k].wait()
+        own = own + jnp.dot(lhs[:, rows], own_x[rows, :], preferred_element_type=F32)
+    own = own.astype(BF16)
+    own_first = jnp.broadcast_to(lax.axis_index("c") == 0, own.shape)
+    half = own.shape[1]
+    out[:, :half] = jnp.where(own_first, own, other)
+    out[:, half:] = jnp.where(own_first, other, own)
+
+
+def quarter_kernel(p0, p1, p2, p3, full, top, bottom, rows):
+    x = lax.axis_index("x")
+    for s, piece in enumerate((p0, p1, p2, p3)):
+        start = pl.multiple_of(lax.rem(x + 4 - s, 4) * COLS, COLS)
+        rows[pl.ds(start, COLS), :] = piece[...]
+    for k in range(6):
+        tile = rows[:, k * 256 : (k + 1) * 256].T
+        full[k * 256 : (k + 1) * 256, :] = tile
+        half = top if k < 3 else bottom
+        half[k % 3 * 256 : (k % 3 + 1) * 256, :] = tile
+
+
+def finish_kernel(own, below, above, top, bottom, out, wide, sems):
+    colour = lax.rem(lax.axis_index("z") + 2 * lax.axis_index("x"), 4)
+    half = DQ // 2
+    copies = []
+    for n, (shift, pieces) in enumerate(
+        ((0, (own,)), (2, (top, bottom)), (3, (below,)), (1, (above,)))
+    ):
+        for m, piece in enumerate(pieces):
+            wide[n, m * half : m * half + piece.shape[0], :] = piece[...].astype(F32)
+        lanes = pl.multiple_of(lax.rem(colour + shift, 4) * 256, 256)
+        copies.append(pltpu.make_async_copy(wide.at[n], out.at[:, pl.ds(lanes, 256)], sems.at[n]))
+        copies[-1].start()
+    for c in copies:
+        c.wait()
+
+
+def plane(dz, dx):
+    return [
+        (z * 4 + x, (z + dz) % 4 * 4 + (x + dx) % 4) for z in range(4) for x in range(4)
+    ]
 
 
 def ring(shift):
@@ -398,7 +460,7 @@
         VMEM,
         [pltpu.SemaphoreType.DMA((2,))],
         "pick_outgoing",
-    )(ids, key_cache)
+    )(ids, in_hbm(key_cache))
     arrived = lax.all_to_all(outgoing, ("z", "x"), split_axis=0, concat_axis=0, tiled=True)
 
     iq_own, iq_send = call(
@@ -428,8 +490,8 @@
         "pick_listed",
     )(ids, arrived, q_send, *iq_all[1:])
     idx_all = around_y(idx)
-    lat = lax.optimization_barrier((lat, *idx_all[1:]))[0]
-    lat_all = around_y(lat)
+    lat_sent = lax.optimization_barrier((lat, *idx_all[1:]))[0]
+    lat_all = (lat, *around_y(lat_sent)[1:])
 
     half = DQ // 2
     x_half = lax.dynamic_slice_in_dim(index_input, core * half, half, 1)
@@ -443,25 +505,24 @@
         (VMEM, VMEM),
         [pltpu.VMEM((ID, OWNK), BF16), pltpu.VMEM((OWNK, BLK), F32)],
         "index_logits",
-    )(block_counts, *idx_all, *iq_all)
+    )(block_counts, *map(in_vmem, (*idx_all, *iq_all)))
 
     targets = call(
         target_kernel,
         (shape((LG_ROWS, BLK), BF16),) * 4,
-        [SMEM, VMEM] + [ANY] * 6,
+        [SMEM, VMEM] + [VMEM] * 4 + [ANY, VMEM],
         (VMEM,) * 4,
         [
             pltpu.VMEM((DK, KEYS), BF16),
             pltpu.VMEM((KEYS, DK), BF16),
             pltpu.VMEM((16, DK, BLK), BF16),
-            pltpu.VMEM((16, DK, BLK), BF16),
             pltpu.VMEM((KEYS, 2 * BLK), F32),
             pltpu.VMEM((KEYS, 2 * BLK), F32),
             pltpu.VMEM((KEYS, BLK), F32),
-            pltpu.SemaphoreType.DMA((3,)),
+            pltpu.SemaphoreType.DMA((2,)),
         ],
         "attention_target",
-    )(block_counts, stats, *lat_all, q_t, q_other)
+    )(block_counts, stats, *map(in_vmem, lat_all), in_hbm(q_t), in_vmem(q_other))
     x_own, _ = lax.optimization_barrier((x_own, targets[0]))
     x_other = lax.ppermute(x_own, "c", SWAP)
     arrived_targets = {s: lax.ppermute(targets[s], "y", ring(s)) for s in SHIFTS}
@@ -472,7 +533,7 @@
         [VMEM] * 5,
         VMEM,
         name="loss",
-    )(targets[0], arrived_targets[1], arrived_targets[2], arrived_targets[3], logits)
+    )(*map(in_vmem, (targets[0], *(arrived_targets[s] for s in (1, 2, 3)), logits)))
     grads_all = around_y(grads)
 
     query_grad, entropy = call(
@@ -486,7 +547,7 @@
             pltpu.VMEM((KEYS, BLK), F32),
         ],
         "index_backward",
-    )(*grads_all, *idx_all, iq_pair)
+    )(*map(in_vmem, (*grads_all, *idx_all, iq_pair)))
     entropy_other = lax.ppermute(entropy, "c", SWAP)
     entropy_both = jnp.where(
         first,
@@ -497,34 +558,40 @@
     entropy_mine = lax.dynamic_slice_in_dim(entropy_both, (2 * y + core) * share, share, 0)
 
     swapped = lax.all_to_all(query_grad, ("z", "x", "c"), split_axis=0, concat_axis=0, tiled=True)
-    chunk = 512
-    piece = pl.pallas_call(
+    qblk = ("z", "x")
+    piece = call(
         weight_kernel,
-        grid=(QUERIES // chunk,),
-        out_shape=shape((COLS, DQ), BF16),
-        in_specs=[
-            pl.BlockSpec((2 * NQ, COLS, BLK), lambda i: (0, 0, 0)),
-            pl.BlockSpec((chunk, half), lambda i: (i, 0)),
-            pl.BlockSpec((chunk, half), lambda i: (i, 0)),
+        shape((COLS, DQ), BF16),
+        [VMEM, ANY, VMEM],
+        VMEM,
+        [
+            pltpu.VMEM((COLS, QUERIES), BF16),
+            pltpu.VMEM((QUERIES, half), BF16),
+            pltpu.SemaphoreType.DMA((4,)),
         ],
-        out_specs=pl.BlockSpec((COLS, DQ), lambda i: (0, 0)),
-        scratch_shapes=[
-            pltpu.VMEM((QUERIES // chunk, COLS, chunk), BF16),
-            pltpu.VMEM((2, COLS, half), F32),
-        ],
-        compiler_params=pltpu.CompilerParams(vmem_limit_bytes=VMEM_LIMIT),
-        name="weight_piece",
-    )(swapped, x_own, x_other)
-    gathered = lax.all_gather(piece, ("z", "x"), axis=0, tiled=True)
-    weight_grad = pl.pallas_call(
+        "weight_piece",
+    )(in_vmem(swapped), in_hbm(x_own), in_vmem(x_other))
+    same = [piece] + [lax.ppermute(piece, qblk, plane(-2 * d, d)) for d in (1, 2, 3)]
+    full, top, bottom = call(
+        quarter_kernel,
+        (shape((DQ, 256), BF16), shape((half, 256), BF16), shape((half, 256), BF16)),
+        [VMEM] * 4,
+        (VMEM,) * 3,
+        [pltpu.VMEM((256, DQ), BF16)],
+        "quarter",
+    )(*map(in_vmem, same))
+    below = lax.ppermute(full, qblk, plane(1, 0))
+    above = lax.ppermute(full, qblk, plane(-1, 0))
+    top = lax.ppermute(top, qblk, plane(0, -1))
+    bottom = lax.ppermute(bottom, qblk, plane(0, 1))
+    weight_grad = call(
         finish_kernel,
-        grid=(6,),
-        out_shape=shape((DQ, HALF_COLS), F32),
-        in_specs=[pl.BlockSpec((HALF_COLS, 256), lambda i: (0, i))],
-        out_specs=pl.BlockSpec((256, HALF_COLS), lambda i: (i, 0)),
-        compiler_params=pltpu.CompilerParams(vmem_limit_bytes=VMEM_LIMIT),
-        name="finish",
-    )(gathered)
+        shape((DQ, HALF_COLS), F32),
+        [VMEM] * 5,
+        ANY,
+        [pltpu.VMEM((4, DQ, 256), F32), pltpu.SemaphoreType.DMA((4,))],
+        "finish",
+    )(*map(in_vmem, (full, below, above, top, bottom)))
     return weight_grad, entropy_mine
 
 

time: 248 us -> 221 us (0.89)
  waiting for transfers between devices: 101 us -> 77.9 us
  Pallas kernels: 65.9 us -> 47.5 us
  starting transfers between devices: 34.3 us -> 46.7 us
    all_gather x1 -> x0, waiting for transfers between devices: 41.8 us -> none  [on_device(): gathered = lax.all_gather(piece, ('z', 'x'), axis=0, tiled=True)]
    ppermute x0 -> x7, waiting for transfers between devices: none -> 20.2 us  [the longest x3 9.07 us: on_device(): lax.ppermute(piece, qblk, plane(-2 * d, d))]
    ppermute x0 -> x7, starting transfers between devices: none -> 10.1 us  [the longest x3 5.15 us: on_device(): lax.ppermute(piece, qblk, plane(-2 * d, d))]
    pallas_call x3 -> x4, Pallas kernels: 40.9 us -> 31.3 us  [the longest x1 23 us: on_device(): call(target_kernel, (shape((LG_ROWS, BLK), BF16),) * 4, [SMEM, VMEM] + [V...]
  transfers between devices with their start and end apart: 22 -> 28, of which waited for: 14 -> 17; matrix products, arithmetic and copies ran while one was open for 2% -> 2% of each run, Pallas kernels for 17% -> 15%
where the time goes in v3:
time: 221 us; the launch traced here: 218 us
  waiting for transfers between devices  77.9 us (35%)
  Pallas kernels  47.5 us (21%)
  starting transfers between devices  46.7 us (21%)
  blocking collectives  19.9 us (9%)
  between operations  14.3 us (6%)
  local copies, waits for them, and re-layouts  12.1 us (5%)
    ppermute x12, waiting for transfers between devices, around_y(): moved = {s: lax.ppermute(array, 'y', ring(s)) for s in SHIFTS}  50.4 us
    pallas_call x1, Pallas kernels, on_device(): call(target_kernel, (shape((LG_ROWS, BLK), BF16),) * 4, [SMEM, VMEM] + [V...  23 us
    all_to_all x1, blocking collectives, on_device(): lax.all_to_all(query_grad, ('z', 'x', 'c'), split_axis=0, concat_axis=0,...  19.9 us
    ppermute x12, starting transfers between devices, around_y(): moved = {s: lax.ppermute(array, 'y', ring(s)) for s in SHIFTS}  18 us
    ppermute x3, waiting for transfers between devices, on_device(): lax.ppermute(piece, qblk, plane(-2 * d, d))  9.07 us
    all_to_all x1, starting transfers between devices, on_device(): lax.all_to_all(outgoing, ('z', 'x'), split_axis=0, concat_axis=0, tiled=T...  8.75 us
    ppermute x1, waiting for transfers between devices, on_device(): top = lax.ppermute(top, qblk, plane(0, -1))  7.93 us
    unnamed x38, local copies, waits for them, and re-layouts  7.83 us
  transfers between devices with their start and end apart: 28, of which 17 were waited for; matrix products, arithmetic and copies ran while one was open for 2% of the time, Pallas kernels for 15%

profile of v3, /device:TPU:1, one launch (start us, length us, event | category | flops | bytes accessed | tf_op | source)
XLA Modules:
  0.0 218.4 jit_solution(10259268812207218977)
XLA Ops:
  7.9 4.7 %pick_outgoing.1 = bf16[16,3,176,128]{3,2,1,0:T(8,128)(2,1)} custom-call(s32[16,32]{1,0:T(8,128)S(1)} %bitcast.13, bf16[32,704,128]{2,1,0:T(8,128)(2,1)} %cache.1), custom_call_target="tpu_custom_call" | custom-call | tf_op jit(solution)/shard_map/pick_outgoing/pallas_call | solution.py:456
  12.6 8.7 %all-to-all-start = ((bf16[16,3,176,128]{3,2,1,0:T(8,128)(2,1)}), bf16[16,3,176,128]{3,2,1,0:T(8,128)(2,1)}, u32[]{:S(2)}, u32[]{:S(2)}) async-start(bf16[16,3,176,128]{3,2,1,0:T(8,128)(2,1)} %pick_outgoing.1), calls=%async_computation | async-start | bytes 4325376 | tf_op jit(solution)/shard_map/all_to_all | solution.py:464
  28.2 2.6 %collective-permute-start.2 = (bf16[2,1056,128]{2,1,0:T(8,128)(2,1)S(1)}, bf16[2,1056,128]{2,1,0:T(8,128)(2,1)}, u32[]{:S(2)}, u32[]{:S(2)}) collective-permute-start(bf16[2,1056,128]{2,1,0:T(8,128)(2,1)S(1)} %pad_maximum_fusion.rest_0_.iq), channel_id=1, source_target_pairs={{0,64},{32,96},{64,0},{96,32},{1,65},{33,97},{65,1},{97,33},{2,66}... | collective-permute-start | bytes 1622024 | tf_op jit(solution)/shard_map/ppermute | solution.py:446
  31.9 1.8 constant_dynamic-slice_fusion
  33.7 1.8 dynamic-slice_bitcast_fusion.refs_0_
  35.5 6.3 %collective-permute-done.1.refs_1_.rest_1_ = bf16[2,1056,128]{2,1,0:T(8,128)(2,1)S(1)} collective-permute-done((bf16[2,1056,128]{2,1,0:T(8,128)(2,1)S(1)}, bf16[2,1056,128]{2,1,0:T(8,128)(2,1)S(1)}, u32[]{:S(2)}, u32[]{:S(2)}) %collective-permute-start.1) | collective-permute-done | bytes 540704 | tf_op jit(solution)/shard_map/ppermute | solution.py:446
  41.8 12.7 %collective-permute-done.2.refs_2_.rest_2_ = bf16[2,1056,128]{2,1,0:T(8,128)(2,1)} collective-permute-done((bf16[2,1056,128]{2,1,0:T(8,128)(2,1)S(1)}, bf16[2,1056,128]{2,1,0:T(8,128)(2,1)}, u32[]{:S(2)}, u32[]{:S(2)}) %collective-permute-start.2) | collective-permute-done | bytes 540704 | tf_op jit(solution)/shard_map/ppermute | solution.py:446
  54.5 1.9 pick_listed.1
  60.1 2.1 collective-permute-start.5
  63.6 2.1 collective-permute-done.4.i1
  65.7 3.2 %collective-permute-done.5.i2 = bf16[16,32,128]{2,1,0:T(8,128)(2,1)S(1)} collective-permute-done((bf16[16,32,128]{2,1,0:T(8,128)(2,1)}, bf16[16,32,128]{2,1,0:T(8,128)(2,1)S(1)}, u32[]{:S(2)}, u32[]{:S(2)}) %collective-permute-start.5) | collective-permute-done | bytes 131104 | tf_op jit(solution)/shard_map/ppermute | solution.py:446
  70.7 2.2 %collective-permute-start.8 = (bf16[16,144,128]{2,1,0:T(8,128)(2,1)}, bf16[16,144,128]{2,1,0:T(8,128)(2,1)S(1)}, u32[]{:S(2)}, u32[]{:S(2)}) collective-permute-start(bf16[16,144,128]{2,1,0:T(8,128)(2,1)} %copy-done.2), channel_id=1, source_target_pairs={{0,64},{32,96},{64,0},{96,32},{1,65},{33,97},{65,1},{97,33},{2,66}... | collective-permute-start | bytes 1769480 | tf_op jit(solution)/shard_map/ppermute | solution.py:446
  74.1 3.8 %index_logits.1 = (f32[512,128]{1,0:T(8,128)S(1)}, f32[8,128]{1,0:T(8,128)S(1)}) custom-call(s32[32]{0:T(128)S(1)} %copy-done.18, bf16[16,32,128]{2,1,0:T(8,128)(2,1)S(1)} %copy-done.5, bf16[16,32,128]{2,1,0:T(8,128)(2,1)S(1)} %collective-permute-done.4.i1, bf16[16,32,128]{2,1,0:T(8,128)(2,1)S(1)} %collective-permute-done.5.i2, ...), custom_call_target="tpu_custom_call" | custom-call | tf_op jit(solution)/shard_map/index_logits/pallas_call | solution.py:501
  78.6 5.9 %collective-permute-done.7.l1 = bf16[16,144,128]{2,1,0:T(8,128)(2,1)S(1)} collective-permute-done((bf16[16,144,128]{2,1,0:T(8,128)(2,1)}, bf16[16,144,128]{2,1,0:T(8,128)(2,1)S(1)}, u32[]{:S(2)}, u32[]{:S(2)}) %collective-permute-start.7) | collective-permute-done | bytes 589856 | tf_op jit(solution)/shard_map/ppermute | solution.py:446
  84.5 14.0 %collective-permute-done.8.l2 = bf16[16,144,128]{2,1,0:T(8,128)(2,1)S(1)} collective-permute-done((bf16[16,144,128]{2,1,0:T(8,128)(2,1)}, bf16[16,144,128]{2,1,0:T(8,128)(2,1)S(1)}, u32[]{:S(2)}, u32[]{:S(2)}) %collective-permute-start.8) | collective-permute-done | bytes 589856 | tf_op jit(solution)/shard_map/ppermute | solution.py:446
  99.6 23.0 %attention_target.1 = (bf16[528,128]{1,0:T(8,128)(2,1)S(1)}, bf16[528,128]{1,0:T(8,128)(2,1)S(1)}, bf16[528,128]{1,0:T(8,128)(2,1)S(1)}, bf16[528,128]{1,0:T(8,128)(2,1)S(1)}) custom-call(s32[32]{0:T(128)S(1)} %copy-done.18, f32[8,128]{1,0:T(8,128)S(1)} %get-tuple-element.23.stats, bf16[16,144,128]{2,1,0:T(8,128)(2,1)S(1)} %copy-done.3, ...), custom_call_target="tpu_custom_call" | custom-call | tf_op jit(solution)/shard_map/attention_target/pallas_call | solution.py:510
  125.1 2.2 collective-permute-start.12
  127.9 2.7 %collective-permute-done.11.t1 = bf16[528,128]{1,0:T(8,128)(2,1)S(1)} collective-permute-done((bf16[528,128]{1,0:T(8,128)(2,1)S(1)}, bf16[528,128]{1,0:T(8,128)(2,1)S(1)}, u32[]{:S(2)}, u32[]{:S(2)}) %collective-permute-start.11) | collective-permute-done | bytes 135200 | tf_op jit(solution)/shard_map/ppermute | solution.py:528
  130.6 3.2 %collective-permute-done.12.t2 = bf16[528,128]{1,0:T(8,128)(2,1)S(1)} collective-permute-done((bf16[528,128]{1,0:T(8,128)(2,1)S(1)}, bf16[528,128]{1,0:T(8,128)(2,1)S(1)}, u32[]{:S(2)}, u32[]{:S(2)}) %collective-permute-start.12) | collective-permute-done | bytes 135200 | tf_op jit(solution)/shard_map/ppermute | solution.py:528
  135.7 2.6 %collective-permute-start.15 = (bf16[528,128]{1,0:T(8,128)(2,1)S(1)}, bf16[528,128]{1,0:T(8,128)(2,1)S(1)}, u32[]{:S(2)}, u32[]{:S(2)}) collective-permute-start(bf16[528,128]{1,0:T(8,128)(2,1)S(1)} %loss.1.g0), channel_id=1, source_target_pairs={{0,64},{32,96},{64,0},{96,32},{1,65},{33,97},{65,1},{97,33},{2,66}... | collective-permute-start | bytes 405512 | tf_op jit(solution)/shard_map/ppermute | solution.py:446
  140.0 4.4 %collective-permute-done.15.g2 = bf16[528,128]{1,0:T(8,128)(2,1)S(1)} collective-permute-done((bf16[528,128]{1,0:T(8,128)(2,1)S(1)}, bf16[528,128]{1,0:T(8,128)(2,1)S(1)}, u32[]{:S(2)}, u32[]{:S(2)}) %collective-permute-start.15) | collective-permute-done | bytes 135200 | tf_op jit(solution)/shard_map/ppermute | solution.py:446
  146.2 3.9 %index_backward.1 = (bf16[32,64,128]{2,1,0:T(8,128)(2,1)S(1)}, f32[8,128]{1,0:T(8,128)S(1)}) custom-call(bf16[528,128]{1,0:T(8,128)(2,1)S(1)} %loss.1.g0, bf16[528,128]{1,0:T(8,128)(2,1)S(1)} %collective-permute-done.14.g1, bf16[528,128]{1,0:T(8,128)(2,1)S(1)} %collective-permute-done.15.g2, bf16[528,128]{1,0:T(8,128)(2,1)S(1)} %collective-permute-done.16.g3, ...), custom_call_target="tpu_custom_call" | custom-call | tf_op jit(solution)/shard_map/index_backward/pallas_call | solution.py:539
  150.0 19.9 %all_to_all.10.qg = bf16[32,64,128]{2,1,0:T(8,128)(2,1)S(1)} all-to-all(bf16[32,64,128]{2,1,0:T(8,128)(2,1)S(1)} %get-tuple-element.31), channel_id=1, replica_groups=mesh['y'=4,'c'=2,'z'=4,'x'=4] {'z','x','c'}, dimensions={0} | all-to-all | bytes 1048576 | tf_op jit(solution)/shard_map/all_to_all | solution.py:560
  170.0 5.1 %weight_piece.1.p0 = bf16[64,1536]{1,0:T(8,128)(2,1)S(1)} custom-call(bf16[32,64,128]{2,1,0:T(8,128)(2,1)S(1)} %all_to_all.10.qg, bf16[4096,768]{1,0:T(8,128)(2,1)} %all-gather.2.cloned.1.call-done.xa, bf16[4096,768]{1,0:T(8,128)(2,1)S(1)} %collective-permute-done.17.xb), custom_call_target="tpu_custom_call" | custom-call | tf_op jit(solution)/shard_map/weight_piece/pallas_call | solution.py:562
  177.6 2.6 %collective-permute-start.20 = (bf16[64,1536]{1,0:T(8,128)(2,1)S(1)}, bf16[64,1536]{1,0:T(8,128)(2,1)S(1)}, u32[]{:S(2)}, u32[]{:S(2)}) collective-permute-start(bf16[64,1536]{1,0:T(8,128)(2,1)S(1)} %weight_piece.1.p0), channel_id=1, source_target_pairs={{0,11},{1,8},{2,9},{3,10},{4,15},{5,12},{6,13},{7,14},{8,3},{9,0},... | collective-permute-start | bytes 589832 | tf_op jit(solution)/shard_map/ppermute | solution.py:574
  180.2 4.6 %collective-permute-done.18.p1 = bf16[64,1536]{1,0:T(8,128)(2,1)S(1)} collective-permute-done((bf16[64,1536]{1,0:T(8,128)(2,1)S(1)}, bf16[64,1536]{1,0:T(8,128)(2,1)S(1)}, u32[]{:S(2)}, u32[]{:S(2)}) %collective-permute-start.18) | collective-permute-done | bytes 196640 | tf_op jit(solution)/shard_map/ppermute | solution.py:574
  186.5 2.8 %collective-permute-done.20.p3 = bf16[64,1536]{1,0:T(8,128)(2,1)S(1)} collective-permute-done((bf16[64,1536]{1,0:T(8,128)(2,1)S(1)}, bf16[64,1536]{1,0:T(8,128)(2,1)S(1)}, u32[]{:S(2)}, u32[]{:S(2)}) %collective-permute-start.20) | collective-permute-done | bytes 196640 | tf_op jit(solution)/shard_map/ppermute | solution.py:574
  192.4 2.3 %collective-permute-start.25 = (f32[8,128]{1,0:T(8,128)S(1)}, f32[8,128]{1,0:T(8,128)S(1)}, u32[]{:S(2)}, u32[]{:S(2)}) collective-permute-start(f32[8,128]{1,0:T(8,128)S(1)} %get-tuple-element.37), channel_id=1, source_target_pairs={{0,16},{16,0},{1,17},{17,1},{2,18},{18,2},{3,19},{19,3},{4,20},{20... | collective-permute-start | bytes 12296 | tf_op jit(solution)/shard_map/ppermute | solution.py:551
  194.7 2.2 %collective-permute-start.23 = (bf16[768,256]{1,0:T(8,128)(2,1)S(1)}, bf16[768,256]{1,0:T(8,128)(2,1)S(1)}, u32[]{:S(2)}, u32[]{:S(2)}) collective-permute-start(bf16[768,256]{1,0:T(8,128)(2,1)S(1)} %get-tuple-element.35), channel_id=1, source_target_pairs={{0,3},{1,0},{2,1},{3,2},{4,7},{5,4},{6,5},{7,6},{8,11},{9,8},{10,9... | collective-permute-start | bytes 1179656 | tf_op jit(solution)/shard_map/ppermute | solution.py:585
  197.6 7.9 %collective-permute-done.23.top = bf16[768,256]{1,0:T(8,128)(2,1)S(1)} collective-permute-done((bf16[768,256]{1,0:T(8,128)(2,1)S(1)}, bf16[768,256]{1,0:T(8,128)(2,1)S(1)}, u32[]{:S(2)}, u32[]{:S(2)}) %collective-permute-start.23) | collective-permute-done | bytes 393248 | tf_op jit(solution)/shard_map/ppermute | solution.py:585
  205.5 3.1 %collective-permute-done.24.bottom = bf16[768,256]{1,0:T(8,128)(2,1)S(1)} collective-permute-done((bf16[768,256]{1,0:T(8,128)(2,1)S(1)}, bf16[768,256]{1,0:T(8,128)(2,1)S(1)}, u32[]{:S(2)}, u32[]{:S(2)}) %collective-permute-start.24) | collective-permute-done | bytes 393248 | tf_op jit(solution)/shard_map/ppermute | solution.py:586
  208.7 2.8 %finish.1 = f32[1536,1024]{1,0:T(8,128)} custom-call(bf16[1536,256]{1,0:T(8,128)(2,1)S(1)} %get-tuple-element.34.own, bf16[1536,256]{1,0:T(8,128)(2,1)S(1)} %collective-permute-done.21.below, bf16[1536,256]{1,0:T(8,128)(2,1)S(1)} %collective-permute-done.22.above, bf16[768,256]{1,0:T(8,128)(2,1)S(1)} %collective-permute-done.23.top, ...), custom_call_target="tpu_custom_call" | custom-call | tf_op jit(solution)/shard_map/finish/pallas_call | solution.py:587
  (82 shorter events, 34.9 us)
Async XLA Ops:
  12.6 41.9 %all-to-all-start = ((bf16[16,3,176,128]{3,2,1,0:T(8,128)(2,1)}), bf16[16,3,176,128]{3,2,1,0:T(8,128)(2,1)}, u32[]{:S(2)}, u32[]{:S(2)}) async-start(bf16[16,3,176,128]{3,2,1,0:T(8,128)(2,1)} %pick_outgoing.1), calls=%async_computation | async-start | bytes 4325376 | tf_op jit(solution)/shard_map/all_to_all | solution.py:464
  21.4 101.3 %all-gather.2.cloned.1.call-start = ((), (), s32[]{:S(2)}) async-start(), calls=%async_computation.2 | async-start | bytes 6684672 | tf_op jit(solution)/shard_map/all_gather | solution.py:499
  24.4 2.4 %collective-permute-start = (bf16[1056,128]{1,0:T(8,128)(2,1)}, bf16[1056,128]{1,0:T(8,128)(2,1)S(1)}, u32[]{:S(2)}, u32[]{:S(2)}) collective-permute-start(bf16[1056,128]{1,0:T(8,128)(2,1)} %get-tuple-element.21), channel_id=1, source_target_pairs={{0,16},{16,0},{1,17},{17,1},{2,18},{18,2},{3,19},{19,3},{4,20},{20... | collective-permute-start | bytes 811016 | tf_op jit(solution)/shard_map/ppermute | solution.py:473
  26.8 15.0 %collective-permute-start.1 = (bf16[2,1056,128]{2,1,0:T(8,128)(2,1)S(1)}, bf16[2,1056,128]{2,1,0:T(8,128)(2,1)S(1)}, u32[]{:S(2)}, u32[]{:S(2)}) collective-permute-start(bf16[2,1056,128]{2,1,0:T(8,128)(2,1)S(1)} %pad_maximum_fusion.rest_0_.iq), channel_id=1, source_target_pairs={{0,32},{32,64},{64,96},{96,0},{1,33},{33,65},{65,97},{97,1},{2,34}... | collective-permute-start | bytes 1622024 | tf_op jit(solution)/shard_map/ppermute | solution.py:446
  28.2 26.3 %collective-permute-start.2 = (bf16[2,1056,128]{2,1,0:T(8,128)(2,1)S(1)}, bf16[2,1056,128]{2,1,0:T(8,128)(2,1)}, u32[]{:S(2)}, u32[]{:S(2)}) collective-permute-start(bf16[2,1056,128]{2,1,0:T(8,128)(2,1)S(1)} %pad_maximum_fusion.rest_0_.iq), channel_id=1, source_target_pairs={{0,64},{32,96},{64,0},{96,32},{1,65},{33,97},{65,1},{97,33},{2,66}... | collective-permute-start | bytes 1622024 | tf_op jit(solution)/shard_map/ppermute | solution.py:446
  30.8 23.7 %collective-permute-start.3 = (bf16[2,1056,128]{2,1,0:T(8,128)(2,1)S(1)}, bf16[2,1056,128]{2,1,0:T(8,128)(2,1)}, u32[]{:S(2)}, u32[]{:S(2)}) collective-permute-start(bf16[2,1056,128]{2,1,0:T(8,128)(2,1)S(1)} %pad_maximum_fusion.rest_0_.iq), channel_id=1, source_target_pairs={{0,96},{32,0},{64,32},{96,64},{1,97},{33,1},{65,33},{97,65},{2,98}... | collective-permute-start | bytes 1622024 | tf_op jit(solution)/shard_map/ppermute | solution.py:446
  33.7 39.5 %copy-start.18 = (s32[32]{0:T(128)S(1)}, s32[32]{0:T(128)}, u32[]{:S(2)}) copy-start(s32[32]{0:T(128)} %counts.3) | copy-start | bytes 388
  57.9 20.6 %collective-permute-start.10 = (bf16[16,576,128]{2,1,0:T(8,128)(2,1)S(1)}, bf16[16,576,128]{2,1,0:T(8,128)(2,1)S(1)}, u32[]{:S(2)}, u32[]{:S(2)}) collective-permute-start(bf16[16,576,128]{2,1,0:T(8,128)(2,1)S(1)} %dynamic-slice_bitcast_fusion.refs_0_), channel_id=1, source_target_pairs={{0,16},{16,0},{1,17},{17,1},{2,18},{18,2},{3,19},{19,3},{4,20},{20... | collective-permute-start | bytes 7077896 | tf_op jit(solution)/shard_map/ppermute | solution.py:482
  59.2 6.5 %collective-permute-start.4 = (bf16[16,32,128]{2,1,0:T(8,128)(2,1)}, bf16[16,32,128]{2,1,0:T(8,128)(2,1)S(1)}, u32[]{:S(2)}, u32[]{:S(2)}) collective-permute-start(bf16[16,32,128]{2,1,0:T(8,128)(2,1)} %copy-done.4), channel_id=1, source_target_pairs={{0,32},{32,64},{64,96},{96,0},{1,33},{33,65},{65,97},{97,1},{2,34}... | collective-permute-start | bytes 393224 | tf_op jit(solution)/shard_map/ppermute | solution.py:446
  60.1 8.7 %collective-permute-start.5 = (bf16[16,32,128]{2,1,0:T(8,128)(2,1)}, bf16[16,32,128]{2,1,0:T(8,128)(2,1)S(1)}, u32[]{:S(2)}, u32[]{:S(2)}) collective-permute-start(bf16[16,32,128]{2,1,0:T(8,128)(2,1)} %copy-done.4), channel_id=1, source_target_pairs={{0,64},{32,96},{64,0},{96,32},{1,65},{33,97},{65,1},{97,33},{2,66}... | collective-permute-start | bytes 393224 | tf_op jit(solution)/shard_map/ppermute | solution.py:446
  62.3 6.6 %collective-permute-start.6 = (bf16[16,32,128]{2,1,0:T(8,128)(2,1)}, bf16[16,32,128]{2,1,0:T(8,128)(2,1)S(1)}, u32[]{:S(2)}, u32[]{:S(2)}) collective-permute-start(bf16[16,32,128]{2,1,0:T(8,128)(2,1)} %copy-done.4), channel_id=1, source_target_pairs={{0,96},{32,0},{64,32},{96,64},{1,97},{33,1},{65,33},{97,65},{2,98}... | collective-permute-start | bytes 393224 | tf_op jit(solution)/shard_map/ppermute | solution.py:446
  68.9 15.6 %collective-permute-start.7 = (bf16[16,144,128]{2,1,0:T(8,128)(2,1)}, bf16[16,144,128]{2,1,0:T(8,128)(2,1)S(1)}, u32[]{:S(2)}, u32[]{:S(2)}) collective-permute-start(bf16[16,144,128]{2,1,0:T(8,128)(2,1)} %copy-done.2), channel_id=1, source_target_pairs={{0,32},{32,64},{64,96},{96,0},{1,33},{33,65},{65,97},{97,1},{2,34}... | collective-permute-start | bytes 1769480 | tf_op jit(solution)/shard_map/ppermute | solution.py:446
  70.7 27.8 %collective-permute-start.8 = (bf16[16,144,128]{2,1,0:T(8,128)(2,1)}, bf16[16,144,128]{2,1,0:T(8,128)(2,1)S(1)}, u32[]{:S(2)}, u32[]{:S(2)}) collective-permute-start(bf16[16,144,128]{2,1,0:T(8,128)(2,1)} %copy-done.2), channel_id=1, source_target_pairs={{0,64},{32,96},{64,0},{96,32},{1,65},{33,97},{65,1},{97,33},{2,66}... | collective-permute-start | bytes 1769480 | tf_op jit(solution)/shard_map/ppermute | solution.py:446
  72.9 25.6 %collective-permute-start.9 = (bf16[16,144,128]{2,1,0:T(8,128)(2,1)}, bf16[16,144,128]{2,1,0:T(8,128)(2,1)S(1)}, u32[]{:S(2)}, u32[]{:S(2)}) collective-permute-start(bf16[16,144,128]{2,1,0:T(8,128)(2,1)} %copy-done.2), channel_id=1, source_target_pairs={{0,96},{32,0},{64,32},{96,64},{1,97},{33,1},{65,33},{97,65},{2,98}... | collective-permute-start | bytes 1769480 | tf_op jit(solution)/shard_map/ppermute | solution.py:446
  99.6 34.2 %copy-start.14 = (f32[512,128]{1,0:T(8,128)S(1)}, f32[512,128]{1,0:T(8,128)}, u32[]{:S(2)}) copy-start(f32[512,128]{1,0:T(8,128)} %copy-done.13) | copy-start | bytes 786436
  99.6 44.7 %copy-start.6 = (bf16[16,32,128]{2,1,0:T(8,128)(2,1)S(1)}, bf16[16,32,128]{2,1,0:T(8,128)(2,1)}, u32[]{:S(2)}) copy-start(bf16[16,32,128]{2,1,0:T(8,128)(2,1)} %copy-done.4) | copy-start | bytes 393220
  99.6 44.7 %copy-start.8 = (bf16[16,32,128]{2,1,0:T(8,128)(2,1)S(1)}, bf16[16,32,128]{2,1,0:T(8,128)(2,1)}, u32[]{:S(2)}) copy-start(bf16[16,32,128]{2,1,0:T(8,128)(2,1)} %copy-done.7) | copy-start | bytes 393220
  122.7 47.3 %collective-permute-start.17 = (bf16[4096,768]{1,0:T(8,128)(2,1)}, bf16[4096,768]{1,0:T(8,128)(2,1)S(1)}, u32[]{:S(2)}, u32[]{:S(2)}) collective-permute-start(bf16[4096,768]{1,0:T(8,128)(2,1)} %all-gather.2.cloned.1.call-done.xa), channel_id=1, source_target_pairs={{0,16},{16,0},{1,17},{17,1},{2,18},{18,2},{3,19},{19,3},{4,20},{20... | collective-permute-start | bytes 18874376 | tf_op jit(solution)/shard_map/ppermute | solution.py:527
  124.2 6.4 %collective-permute-start.11 = (bf16[528,128]{1,0:T(8,128)(2,1)S(1)}, bf16[528,128]{1,0:T(8,128)(2,1)S(1)}, u32[]{:S(2)}, u32[]{:S(2)}) collective-permute-start(bf16[528,128]{1,0:T(8,128)(2,1)S(1)} %get-tuple-element.27), channel_id=1, source_target_pairs={{0,32},{32,64},{64,96},{96,0},{1,33},{33,65},{65,97},{97,1},{2,34}... | collective-permute-start | bytes 405512 | tf_op jit(solution)/shard_map/ppermute | solution.py:528
  125.1 8.7 %collective-permute-start.12 = (bf16[528,128]{1,0:T(8,128)(2,1)S(1)}, bf16[528,128]{1,0:T(8,128)(2,1)S(1)}, u32[]{:S(2)}, u32[]{:S(2)}) collective-permute-start(bf16[528,128]{1,0:T(8,128)(2,1)S(1)} %get-tuple-element.28), channel_id=1, source_target_pairs={{0,64},{32,96},{64,0},{96,32},{1,65},{33,97},{65,1},{97,33},{2,66}... | collective-permute-start | bytes 405512 | tf_op jit(solution)/shard_map/ppermute | solution.py:528
  127.2 6.6 %collective-permute-start.13 = (bf16[528,128]{1,0:T(8,128)(2,1)S(1)}, bf16[528,128]{1,0:T(8,128)(2,1)S(1)}, u32[]{:S(2)}, u32[]{:S(2)}) collective-permute-start(bf16[528,128]{1,0:T(8,128)(2,1)S(1)} %get-tuple-element.29), channel_id=1, source_target_pairs={{0,96},{32,0},{64,32},{96,64},{1,97},{33,1},{65,33},{97,65},{2,98}... | collective-permute-start | bytes 405512 | tf_op jit(solution)/shard_map/ppermute | solution.py:528
  134.0 6.0 %collective-permute-start.14 = (bf16[528,128]{1,0:T(8,128)(2,1)S(1)}, bf16[528,128]{1,0:T(8,128)(2,1)S(1)}, u32[]{:S(2)}, u32[]{:S(2)}) collective-permute-start(bf16[528,128]{1,0:T(8,128)(2,1)S(1)} %loss.1.g0), channel_id=1, source_target_pairs={{0,32},{32,64},{64,96},{96,0},{1,33},{33,65},{65,97},{97,1},{2,34}... | collective-permute-start | bytes 405512 | tf_op jit(solution)/shard_map/ppermute | solution.py:446
  135.7 8.7 %collective-permute-start.15 = (bf16[528,128]{1,0:T(8,128)(2,1)S(1)}, bf16[528,128]{1,0:T(8,128)(2,1)S(1)}, u32[]{:S(2)}, u32[]{:S(2)}) collective-permute-start(bf16[528,128]{1,0:T(8,128)(2,1)S(1)} %loss.1.g0), channel_id=1, source_target_pairs={{0,64},{32,96},{64,0},{96,32},{1,65},{33,97},{65,1},{97,33},{2,66}... | collective-permute-start | bytes 405512 | tf_op jit(solution)/shard_map/ppermute | solution.py:446
  138.3 6.1 %collective-permute-start.16 = (bf16[528,128]{1,0:T(8,128)(2,1)S(1)}, bf16[528,128]{1,0:T(8,128)(2,1)S(1)}, u32[]{:S(2)}, u32[]{:S(2)}) collective-permute-start(bf16[528,128]{1,0:T(8,128)(2,1)S(1)} %loss.1.g0), channel_id=1, source_target_pairs={{0,96},{32,0},{64,32},{96,64},{1,97},{33,1},{65,33},{97,65},{2,98}... | collective-permute-start | bytes 405512 | tf_op jit(solution)/shard_map/ppermute | solution.py:446
  175.1 9.7 %collective-permute-start.18 = (bf16[64,1536]{1,0:T(8,128)(2,1)S(1)}, bf16[64,1536]{1,0:T(8,128)(2,1)S(1)}, u32[]{:S(2)}, u32[]{:S(2)}) collective-permute-start(bf16[64,1536]{1,0:T(8,128)(2,1)S(1)} %weight_piece.1.p0), channel_id=1, source_target_pairs={{0,9},{1,10},{2,11},{3,8},{4,13},{5,14},{6,15},{7,12},{8,1},{9,2},... | collective-permute-start | bytes 589832 | tf_op jit(solution)/shard_map/ppermute | solution.py:574
  176.5 9.9 %collective-permute-start.19 = (bf16[64,1536]{1,0:T(8,128)(2,1)S(1)}, bf16[64,1536]{1,0:T(8,128)(2,1)S(1)}, u32[]{:S(2)}, u32[]{:S(2)}) collective-permute-start(bf16[64,1536]{1,0:T(8,128)(2,1)S(1)} %weight_piece.1.p0), channel_id=1, source_target_pairs={{0,2},{1,3},{2,0},{3,1},{4,6},{5,7},{6,4},{7,5},{8,10},{9,11},{10,... | collective-permute-start | bytes 589832 | tf_op jit(solution)/shard_map/ppermute | solution.py:574
  177.6 11.7 %collective-permute-start.20 = (bf16[64,1536]{1,0:T(8,128)(2,1)S(1)}, bf16[64,1536]{1,0:T(8,128)(2,1)S(1)}, u32[]{:S(2)}, u32[]{:S(2)}) collective-permute-start(bf16[64,1536]{1,0:T(8,128)(2,1)S(1)} %weight_piece.1.p0), channel_id=1, source_target_pairs={{0,11},{1,8},{2,9},{3,10},{4,15},{5,12},{6,13},{7,14},{8,3},{9,0},... | collective-permute-start | bytes 589832 | tf_op jit(solution)/shard_map/ppermute | solution.py:574
  189.7 18.9 %collective-permute-start.21 = (bf16[1536,256]{1,0:T(8,128)(2,1)S(1)}, bf16[1536,256]{1,0:T(8,128)(2,1)S(1)}, u32[]{:S(2)}, u32[]{:S(2)}) collective-permute-start(bf16[1536,256]{1,0:T(8,128)(2,1)S(1)} %get-tuple-element.34.own), channel_id=1, source_target_pairs={{0,4},{1,5},{2,6},{3,7},{4,8},{5,9},{6,10},{7,11},{8,12},{9,13},{1... | collective-permute-start | bytes 2359304 | tf_op jit(solution)/shard_map/ppermute | solution.py:583
  190.7 18.0 %collective-permute-start.22 = (bf16[1536,256]{1,0:T(8,128)(2,1)S(1)}, bf16[1536,256]{1,0:T(8,128)(2,1)S(1)}, u32[]{:S(2)}, u32[]{:S(2)}) collective-permute-start(bf16[1536,256]{1,0:T(8,128)(2,1)S(1)} %get-tuple-element.34.own), channel_id=1, source_target_pairs={{0,12},{1,13},{2,14},{3,15},{4,0},{5,1},{6,2},{7,3},{8,4},{9,5},{1... | collective-permute-start | bytes 2359304 | tf_op jit(solution)/shard_map/ppermute | solution.py:584
  192.4 4.5 %collective-permute-start.25 = (f32[8,128]{1,0:T(8,128)S(1)}, f32[8,128]{1,0:T(8,128)S(1)}, u32[]{:S(2)}, u32[]{:S(2)}) collective-permute-start(f32[8,128]{1,0:T(8,128)S(1)} %get-tuple-element.37), channel_id=1, source_target_pairs={{0,16},{16,0},{1,17},{17,1},{2,18},{18,2},{3,19},{19,3},{4,20},{20... | collective-permute-start | bytes 12296 | tf_op jit(solution)/shard_map/ppermute | solution.py:551
  194.7 10.7 %collective-permute-start.23 = (bf16[768,256]{1,0:T(8,128)(2,1)S(1)}, bf16[768,256]{1,0:T(8,128)(2,1)S(1)}, u32[]{:S(2)}, u32[]{:S(2)}) collective-permute-start(bf16[768,256]{1,0:T(8,128)(2,1)S(1)} %get-tuple-element.35), channel_id=1, source_target_pairs={{0,3},{1,0},{2,1},{3,2},{4,7},{5,4},{6,5},{7,6},{8,11},{9,8},{10,9... | collective-permute-start | bytes 1179656 | tf_op jit(solution)/shard_map/ppermute | solution.py:585
  196.9 11.6 %collective-permute-start.24 = (bf16[768,256]{1,0:T(8,128)(2,1)S(1)}, bf16[768,256]{1,0:T(8,128)(2,1)S(1)}, u32[]{:S(2)}, u32[]{:S(2)}) collective-permute-start(bf16[768,256]{1,0:T(8,128)(2,1)S(1)} %get-tuple-element.36), channel_id=1, source_target_pairs={{0,1},{1,2},{2,3},{3,0},{4,5},{5,6},{6,7},{7,4},{8,9},{9,10},{10,1... | collective-permute-start | bytes 1179656 | tf_op jit(solution)/shard_map/ppermute | solution.py:586
  (15 other events, 157.2 us)
Sparse Core Ops, SparseCore 0:
  58.0 62.9 all-gather.1

commit v4 on v3

--- a/solution.py
+++ b/solution.py
@@ -35,11 +35,12 @@
 score_scale = 192.0 ** (-0.5)
 exp2_scale = score_scale * 1.4426950408889634
 masked_value = -1e30
-VMEM_LIMIT = 40 * 1024 * 1024
+VMEM_LIMIT = 24 * 1024 * 1024
 
 ANY = pl.BlockSpec(memory_space=pl.ANY)
 VMEM = pl.BlockSpec(memory_space=pltpu.VMEM)
 SMEM = pl.BlockSpec(memory_space=pltpu.SMEM)
+HBM = pl.BlockSpec(memory_space=pltpu.HBM)
 
 
 def call(kernel, out_shape, in_specs, out_specs, scratch=(), name=None):
@@ -75,47 +76,40 @@
     return counts[2 * me + core]
 
 
-def pick_outgoing_kernel(ids, cache, out, sem):
+def pick_outgoing_kernel(ids, cache, out, found, sem):
     y, core, me = place()
-    lat = pl.multiple_of(y * LATC, 16)
-    idx = pl.multiple_of(DK + y * IDXC, 16)
-
-    def copies(block, dst, slot):
-        return (
-            pltpu.make_async_copy(
-                cache.at[block, pl.ds(lat, LATC), :], out.at[dst, slot, pl.ds(0, LATC), :], sem.at[0]
-            ),
-            pltpu.make_async_copy(
-                cache.at[block, pl.ds(idx, IDXC), :], out.at[dst, slot, pl.ds(LATC, IDXC), :], sem.at[1]
-            ),
-        )
+    rows = pl.ds(pl.multiple_of(y * PIECE, 16), PIECE)
+    first = me * SHARD
+
+    def copy(block, place_out):
+        return pltpu.make_async_copy(cache.at[block, rows, :], out.at[place_out], sem)
 
     def per_dst(dst, total):
         count = jnp.int32(0)
         for s in range(SEL):
-            block = ids[s, 2 * dst + core]
-            mine = lax.shift_right_logical(block, 5) == me
-
-            @pl.when(mine)
-            def _(block=block, count=count):
-                for c in copies(block - me * SHARD, dst, jnp.minimum(count, CAP - 1)):
-                    c.start()
-
-            count = count + mine.astype(I32)
+            local = ids[s, 2 * dst + core] - first
+            found[total + count] = local * (NQ * CAP) + dst * CAP + jnp.minimum(count, CAP - 1)
+            count = count + ((local >= 0) & (local < SHARD)).astype(I32)
         return total + count
 
     total = lax.fori_loop(0, NQ, per_dst, jnp.int32(0))
 
-    def wait(_, carry):
-        for c in copies(0, 0, 0):
-            c.wait()
+    def start(n, carry):
+        code = found[n]
+        block = code // (NQ * CAP)
+        copy(block, code - block * (NQ * CAP)).start()
         return carry
 
+    def wait(n, carry):
+        copy(0, 0).wait()
+        return carry
+
+    lax.fori_loop(0, total, start, 0)
     lax.fori_loop(0, total, wait, 0)
 
 
 def pick_listed_kernel(ids, arrived, *refs):
-    lat, idx, seen, sem = refs[-4:]
+    sent, listed, seen, sem = refs[-4:]
     _, core, me = place()
     row = 2 * me + core
     for i in range(NQ):
@@ -125,16 +119,13 @@
         owner = lax.shift_right_logical(ids[s, row], 5)
         rank = jnp.minimum(seen[owner], CAP - 1)
         seen[owner] = seen[owner] + 1
-        pending.append(
-            pltpu.make_async_copy(arrived.at[owner, rank, pl.ds(LATC, IDXC), :], idx.at[s], sem.at[0])
-        )
-        pending.append(
-            pltpu.make_async_copy(arrived.at[owner, rank, pl.ds(0, LATC), :], lat.at[s], sem.at[1])
-        )
-        pending[-2].start()
+        pending.append(pltpu.make_async_copy(arrived.at[owner * CAP + rank], listed.at[s], sem.at[0]))
         pending[-1].start()
     for c in pending:
         c.wait()
+    out = pltpu.make_async_copy(listed, sent, sem.at[1])
+    out.start()
+    out.wait()
 
 
 def index_query_kernel(x, w, hw, mine, other):
@@ -168,14 +159,27 @@
     return tail[0:8] + tail[8:16] + tail[16:24]
 
 
-def logits_kernel(counts, i0, i1, i2, i3, *rest):
-    iq_refs, (logits_ref, stats_ref, keys, total) = rest[:4], rest[4:]
+def logits_kernel(counts, p0, p1, p2, p3, iq0, iq1, iq2, iq3, *rest):
+    logits_ref, stats_ref, latent_t, keys_out, keys_t_out, index_t, keys, total, own, sems = rest
     y, count = lax.axis_index("y"), slots_in_use(counts)
-    for s, piece in enumerate((i0, i1, i2, i3)):
-        start = pl.multiple_of(lax.rem(y + NY - s, NY) * IDXC, IDXC)
-        for j in range(4):
-            keys[pl.ds(start, IDXC), j * BLK : (j + 1) * BLK] = piece[4 * y + j]
-    keys_t = keys[...].T
+    load = pltpu.make_async_copy(p0, own, sems.at[2])
+    load.start()
+    for s, piece in ((1, p1), (2, p2), (3, p3), (0, own)):
+        if s == 0:
+            load.wait()
+        rows = pl.ds(pl.multiple_of(lax.rem(y + NY - s, NY) * PIECE, 16), PIECE)
+        for j in range(SEL):
+            keys[rows, j * BLK : (j + 1) * BLK] = piece[j]
+    copies = [pltpu.make_async_copy(keys.at[pl.ds(DK, ID), :], keys_out, sems.at[0])]
+    copies[0].start()
+    for j in range(SEL):
+        span = slice(j * BLK, (j + 1) * BLK)
+        latent_t[span, :] = keys[:DK, span].T
+        index_t[span, :] = keys[DK:, span].T
+    copies.append(pltpu.make_async_copy(index_t, keys_t_out, sems.at[1]))
+    copies[1].start()
+    iq_refs = (iq0, iq1, iq2, iq3)
+    keys_t = index_t[pl.ds(pl.multiple_of(y * OWNK, OWNK), OWNK), :]
     total[...] = jnp.zeros_like(total)
     for ref in [r.at[n] for r in iq_refs for n in range(2)]:
         rows = head_rows(ref[HALF_COLS:, :])
@@ -197,6 +201,8 @@
     mass = jnp.sum(jnp.exp(masked - peak), axis=0, keepdims=True)
     row = lax.broadcasted_iota(I32, (8, BLK), 0)
     stats_ref[...] = jnp.where(row == 0, peak, mass)
+    for c in copies:
+        c.wait()
 
 
 def split_rows(row):
@@ -214,34 +220,17 @@
 
 
 def target_kernel(
-    counts, stats, l0, l1, l2, l3, q_own, qb, o0, o1, o2, o3, keys, keys_t, qa, buf_a, buf_b, total, sems
+    counts, stats, keys_t, q_own, qb, o0, o1, o2, o3, qa, buf_a, buf_b, total, sem
 ):
     y, core, _ = place()
     count = slots_in_use(counts)
-    copies = []
-    for s, piece in enumerate((l0, l1, l2, l3)):
-        start = pl.multiple_of(lax.rem(y + NY - s, NY) * LATC, LATC)
-        for j in range(SEL):
-            copies.append(
-                pltpu.make_async_copy(
-                    piece.at[j], keys.at[pl.ds(start, LATC), pl.ds(j * BLK, BLK)], sems.at[0]
-                )
-            )
     lanes = pl.multiple_of(core * BLK, BLK)
-    queries = [
-        pltpu.make_async_copy(q_own.at[:, :, pl.ds(lanes, BLK)], qa, sems.at[1]),
-    ]
-    for c in copies + queries:
-        c.start()
-    for c in copies:
-        c.wait()
-    for j in range(SEL):
-        keys_t[j * BLK : (j + 1) * BLK, :] = keys[:, j * BLK : (j + 1) * BLK].T
+    own = pltpu.make_async_copy(q_own.at[:, :, pl.ds(lanes, BLK)], qa, sem)
+    own.start()
     total[...] = jnp.zeros_like(total)
-    for c in queries:
-        c.wait()
-
-    chunk = 512
+    own.wait()
+
+    chunk = 1024
     token = lax.broadcasted_iota(I32, (BLK, 2 * BLK), 1) % BLK
     causal = lax.broadcasted_iota(I32, (BLK, 2 * BLK), 0) <= token
 
@@ -331,9 +320,7 @@
     out[OWNK:, :] = tail_tile(split_rows(entropy))
 
 
-def backward_kernel(
-    g0, g1, g2, g3, i0, i1, i2, i3, iq, out, entropy_ref, keys, keys_t, grads
-):
+def backward_kernel(g0, g1, g2, g3, keys, keys_t, iq, out, entropy_ref, grads):
     y = lax.axis_index("y")
     entropy = jnp.zeros((1, BLK), F32)
     for s, piece in enumerate((g0, g1, g2, g3)):
@@ -342,12 +329,6 @@
         tail = piece[OWNK:, :].astype(F32)
         entropy = entropy + tail[0:1] + tail[1:2] + tail[2:3]
     entropy_ref[...] = jnp.broadcast_to(entropy, (8, BLK))
-    for s, piece in enumerate((i0, i1, i2, i3)):
-        start = pl.multiple_of(lax.rem(y + NY - s, NY) * IDXC, IDXC)
-        for j in range(SEL):
-            keys[pl.ds(start, IDXC), j * BLK : (j + 1) * BLK] = piece[j]
-    for j in range(SEL):
-        keys_t[j * BLK : (j + 1) * BLK, :] = keys[:, j * BLK : (j + 1) * BLK].T
     chunk = 512
     for core in range(2):
         ref = iq.at[core]
@@ -455,10 +436,10 @@
 
     outgoing = call(
         pick_outgoing_kernel,
-        shape((NQ, CAP, PIECE, BLK), BF16),
+        shape((NQ * CAP, PIECE, BLK), BF16),
         [SMEM, ANY],
         VMEM,
-        [pltpu.SemaphoreType.DMA((2,))],
+        [pltpu.SMEM((NQ * SEL + 1,), I32), pltpu.SemaphoreType.DMA],
         "pick_outgoing",
     )(ids, in_hbm(key_cache))
     arrived = lax.all_to_all(outgoing, ("z", "x"), split_axis=0, concat_axis=0, tiled=True)
@@ -481,48 +462,60 @@
     q_send = lax.dynamic_slice_in_dim(q_t, (1 - core) * BLK, BLK, 2)
     q_other = lax.ppermute(q_send, "c", SWAP)
 
-    lat, idx = call(
+    listed = call(
         pick_listed_kernel,
-        (shape((SEL, LATC, BLK), BF16), shape((SEL, IDXC, BLK), BF16)),
+        pltpu.HBM((SEL, PIECE, BLK), BF16),
         [SMEM] + [ANY] * 5,
-        (VMEM, VMEM),
-        [pltpu.SMEM((NQ,), I32), pltpu.SemaphoreType.DMA((2,))],
+        HBM,
+        [
+            pltpu.VMEM((SEL, PIECE, BLK), BF16),
+            pltpu.SMEM((NQ,), I32),
+            pltpu.SemaphoreType.DMA((2,)),
+        ],
         "pick_listed",
     )(ids, arrived, q_send, *iq_all[1:])
-    idx_all = around_y(idx)
-    lat_sent = lax.optimization_barrier((lat, *idx_all[1:]))[0]
-    lat_all = (lat, *around_y(lat_sent)[1:])
+    pieces = around_y(listed)
 
     half = DQ // 2
     x_half = lax.dynamic_slice_in_dim(index_input, core * half, half, 1)
-    x_half, _ = lax.optimization_barrier((x_half, idx))
+    x_half, _ = lax.optimization_barrier((x_half, listed))
     x_own = lax.all_gather(x_half, ("z", "x"), axis=0, tiled=True)
 
-    logits, stats = call(
+    logits, stats, latent_t, index_keys, index_t = call(
         logits_kernel,
-        (shape((OWNK, BLK), F32), shape((8, BLK), F32)),
-        [SMEM] + [VMEM] * 8,
-        (VMEM, VMEM),
-        [pltpu.VMEM((ID, OWNK), BF16), pltpu.VMEM((OWNK, BLK), F32)],
+        (
+            shape((OWNK, BLK), F32),
+            shape((8, BLK), F32),
+            shape((KEYS, DK), BF16),
+            pltpu.HBM((ID, KEYS), BF16),
+            pltpu.HBM((KEYS, ID), BF16),
+        ),
+        [SMEM, ANY] + [VMEM] * 7,
+        (VMEM, VMEM, VMEM, HBM, HBM),
+        [
+            pltpu.VMEM((KEYS, ID), BF16),
+            pltpu.VMEM((DK + ID, KEYS), BF16),
+            pltpu.VMEM((OWNK, BLK), F32),
+            pltpu.VMEM((SEL, PIECE, BLK), BF16),
+            pltpu.SemaphoreType.DMA((3,)),
+        ],
         "index_logits",
-    )(block_counts, *map(in_vmem, (*idx_all, *iq_all)))
+    )(block_counts, in_hbm(pieces[0]), *map(in_vmem, (*pieces[1:], *iq_all)))
 
     targets = call(
         target_kernel,
         (shape((LG_ROWS, BLK), BF16),) * 4,
-        [SMEM, VMEM] + [VMEM] * 4 + [ANY, VMEM],
+        [SMEM, VMEM, VMEM, ANY, VMEM],
         (VMEM,) * 4,
         [
-            pltpu.VMEM((DK, KEYS), BF16),
-            pltpu.VMEM((KEYS, DK), BF16),
             pltpu.VMEM((16, DK, BLK), BF16),
             pltpu.VMEM((KEYS, 2 * BLK), F32),
             pltpu.VMEM((KEYS, 2 * BLK), F32),
             pltpu.VMEM((KEYS, BLK), F32),
-            pltpu.SemaphoreType.DMA((2,)),
+            pltpu.SemaphoreType.DMA,
         ],
         "attention_target",
-    )(block_counts, stats, *map(in_vmem, lat_all), in_hbm(q_t), in_vmem(q_other))
+    )(block_counts, stats, in_vmem(latent_t), in_hbm(q_t), in_vmem(q_other))
     x_own, _ = lax.optimization_barrier((x_own, targets[0]))
     x_other = lax.ppermute(x_own, "c", SWAP)
     arrived_targets = {s: lax.ppermute(targets[s], "y", ring(s)) for s in SHIFTS}
@@ -539,15 +532,11 @@
     query_grad, entropy = call(
         backward_kernel,
         (shape((2 * NQ, COLS, BLK), BF16), shape((8, BLK), F32)),
-        [VMEM] * 9,
+        [VMEM] * 7,
         (VMEM, VMEM),
-        [
-            pltpu.VMEM((ID, KEYS), BF16),
-            pltpu.VMEM((KEYS, ID), BF16),
-            pltpu.VMEM((KEYS, BLK), F32),
-        ],
+        [pltpu.VMEM((KEYS, BLK), F32)],
         "index_backward",
-    )(*map(in_vmem, (*grads_all, *idx_all, iq_pair)))
+    )(*map(in_vmem, (*grads_all, index_keys, index_t, iq_pair)))
     entropy_other = lax.ppermute(entropy, "c", SWAP)
     entropy_both = jnp.where(
         first,

time: 221 us -> 218 us (0.986)
  local copies, waits for them, and re-layouts: 12.1 us -> 6.77 us
  waiting for transfers between devices: 77.9 us -> 82.9 us
  starting transfers between devices: 46.7 us -> 42.2 us
    unnamed x38 -> x20, local copies, waits for them, and re-layouts: 7.83 us -> 2.55 us
    ppermute x12 -> x9, waiting for transfers between devices: 50.4 us -> 55.4 us  [around_y(): moved = {s: lax.ppermute(array, 'y', ring(s)) for s in SHIFTS}]
    ppermute x12 -> x9, starting transfers between devices: 18 us -> 13.4 us  [around_y(): moved = {s: lax.ppermute(array, 'y', ring(s)) for s in SHIFTS}]
  transfers between devices with their start and end apart: 28 -> 25, of which waited for: 17 -> 15; matrix products, arithmetic and copies ran while one was open for 2% -> 2% of each run, Pallas kernels for 15% -> 16%
where the time goes in v4:
time: 218 us; the launch traced here: 215 us
  waiting for transfers between devices  82.9 us (38%)
  Pallas kernels  49.1 us (23%)
  starting transfers between devices  42.2 us (19%)
  blocking collectives  20 us (9%)
  between operations  14.3 us (7%)
  local copies, waits for them, and re-layouts  6.77 us (3%)
    ppermute x9, waiting for transfers between devices, around_y(): moved = {s: lax.ppermute(array, 'y', ring(s)) for s in SHIFTS}  55.4 us
    pallas_call x1, Pallas kernels, on_device(): call(target_kernel, (shape((LG_ROWS, BLK), BF16),) * 4, [SMEM, VMEM, VMEM...  21.4 us
    all_to_all x1, blocking collectives, on_device(): lax.all_to_all(query_grad, ('z', 'x', 'c'), split_axis=0, concat_axis=0,...  20 us
    ppermute x9, starting transfers between devices, around_y(): moved = {s: lax.ppermute(array, 'y', ring(s)) for s in SHIFTS}  13.4 us
    ppermute x3, waiting for transfers between devices, on_device(): lax.ppermute(piece, qblk, plane(-2 * d, d))  9.07 us
    all_to_all x1, starting transfers between devices, on_device(): lax.all_to_all(outgoing, ('z', 'x'), split_axis=0, concat_axis=0, tiled=T...  8.76 us
    ppermute x1, waiting for transfers between devices, on_device(): top = lax.ppermute(top, qblk, plane(0, -1))  7.93 us
    pallas_call x1, Pallas kernels, on_device(): call(logits_kernel, (shape((OWNK, BLK), F32), shape((8, BLK), F32), shape...  6.58 us
  transfers between devices with their start and end apart: 25, of which 15 were waited for; matrix products, arithmetic and copies ran while one was open for 2% of the time, Pallas kernels for 16%

profile of v4, /device:TPU:1, one launch (start us, length us, event | category | flops | bytes accessed | tf_op | source)
XLA Modules:
  0.0 215.4 jit_solution(4518439610081784820)
XLA Ops:
  7.9 4.5 %pick_outgoing.1 = bf16[48,176,128]{2,1,0:T(8,128)(2,1)} custom-call(s32[16,32]{1,0:T(8,128)S(1)} %bitcast.13, bf16[32,704,128]{2,1,0:T(8,128)(2,1)} %cache.1), custom_call_target="tpu_custom_call" | custom-call | tf_op jit(solution)/shard_map/pick_outgoing/pallas_call | solution.py:437
  12.4 8.8 %all-to-all-start = ((bf16[48,176,128]{2,1,0:T(8,128)(2,1)}), bf16[48,176,128]{2,1,0:T(8,128)(2,1)}, u32[]{:S(2)}, u32[]{:S(2)}) async-start(bf16[48,176,128]{2,1,0:T(8,128)(2,1)} %pick_outgoing.1), calls=%async_computation | async-start | bytes 4325376 | tf_op jit(solution)/shard_map/all_to_all | solution.py:445
  22.3 1.8 index_query.1
  27.9 2.6 %collective-permute-start.2 = (bf16[2,1056,128]{2,1,0:T(8,128)(2,1)S(1)}, bf16[2,1056,128]{2,1,0:T(8,128)(2,1)}, u32[]{:S(2)}, u32[]{:S(2)}) collective-permute-start(bf16[2,1056,128]{2,1,0:T(8,128)(2,1)S(1)} %pad_maximum_fusion.iq0.iq), channel_id=1, source_target_pairs={{0,64},{32,96},{64,0},{96,32},{1,65},{33,97},{65,1},{97,33},{2,66}... | collective-permute-start | bytes 1622024 | tf_op jit(solution)/shard_map/ppermute | solution.py:427
  31.6 1.8 constant_dynamic-slice_fusion
  33.4 1.8 dynamic-slice_bitcast_fusion.refs_0_
  35.3 6.3 %collective-permute-done.1.refs_1_.iq1 = bf16[2,1056,128]{2,1,0:T(8,128)(2,1)S(1)} collective-permute-done((bf16[2,1056,128]{2,1,0:T(8,128)(2,1)S(1)}, bf16[2,1056,128]{2,1,0:T(8,128)(2,1)S(1)}, u32[]{:S(2)}, u32[]{:S(2)}) %collective-permute-start.1) | collective-permute-done | bytes 540704 | tf_op jit(solution)/shard_map/ppermute | solution.py:427
  41.6 12.7 %collective-permute-done.2.refs_2_.iq2 = bf16[2,1056,128]{2,1,0:T(8,128)(2,1)} collective-permute-done((bf16[2,1056,128]{2,1,0:T(8,128)(2,1)S(1)}, bf16[2,1056,128]{2,1,0:T(8,128)(2,1)}, u32[]{:S(2)}, u32[]{:S(2)}) %collective-permute-start.2) | collective-permute-done | bytes 540704 | tf_op jit(solution)/shard_map/ppermute | solution.py:427
  54.3 2.7 %pick_listed.1.p0 = bf16[16,176,128]{2,1,0:T(8,128)(2,1)} custom-call(s32[16,32]{1,0:T(8,128)S(1)} %bitcast.14, bf16[48,176,128]{2,1,0:T(8,128)(2,1)} %all-to-all-done.arrived, bf16[16,576,128]{2,1,0:T(8,128)(2,1)S(1)} %dynamic-slice_bitcast_fusion.refs_0_, bf16[2,1056,128]{2,1,0:T(8,128)(2,1)S(1)} %collective-permute-done.1.refs_1_.iq1, ...), custom_call_target="tpu_custom_call" | custom-call | tf_op jit(solution)/shard_map/pick_listed/pallas_call | solution.py:465
  59.2 2.2 %collective-permute-start.5 = (bf16[16,176,128]{2,1,0:T(8,128)(2,1)}, bf16[16,176,128]{2,1,0:T(8,128)(2,1)S(1)}, u32[]{:S(2)}, u32[]{:S(2)}) collective-permute-start(bf16[16,176,128]{2,1,0:T(8,128)(2,1)} %pick_listed.1.p0), channel_id=1, source_target_pairs={{0,64},{32,96},{64,0},{96,32},{1,65},{33,97},{65,1},{97,33},{2,66}... | collective-permute-start | bytes 2162696 | tf_op jit(solution)/shard_map/ppermute | solution.py:427
  62.7 14.7 %collective-permute-done.4.p1 = bf16[16,176,128]{2,1,0:T(8,128)(2,1)S(1)} collective-permute-done((bf16[16,176,128]{2,1,0:T(8,128)(2,1)}, bf16[16,176,128]{2,1,0:T(8,128)(2,1)S(1)}, u32[]{:S(2)}, u32[]{:S(2)}) %collective-permute-start.4) | collective-permute-done | bytes 720928 | tf_op jit(solution)/shard_map/ppermute | solution.py:427
  77.4 15.9 %collective-permute-done.5.p2 = bf16[16,176,128]{2,1,0:T(8,128)(2,1)S(1)} collective-permute-done((bf16[16,176,128]{2,1,0:T(8,128)(2,1)}, bf16[16,176,128]{2,1,0:T(8,128)(2,1)S(1)}, u32[]{:S(2)}, u32[]{:S(2)}) %collective-permute-start.5) | collective-permute-done | bytes 720928 | tf_op jit(solution)/shard_map/ppermute | solution.py:427
  93.3 6.6 %index_logits.1 = (f32[512,128]{1,0:T(8,128)S(1)}, f32[8,128]{1,0:T(8,128)S(1)}, bf16[2048,576]{1,0:T(8,128)(2,1)S(1)}, bf16[128,2048]{1,0:T(8,128)(2,1)}, bf16[2048,128]{1,0:T(8,128)(2,1)}) custom-call(s32[32]{0:T(128)S(1)} %copy-done.9, bf16[16,176,128]{2,1,0:T(8,128)(2,1)} %pick_listed.1.p0, bf16[16,176,128]{2,1,0:T(8,128)(2,1)S(1)} %collective-permute-done.4.p1, ...), custom_call_target="tpu_custom_call" | custom-call | tf_op jit(solution)/shard_map/index_logits/pallas_call | solution.py:484
  100.6 21.4 %attention_target.1 = (bf16[528,128]{1,0:T(8,128)(2,1)S(1)}, bf16[528,128]{1,0:T(8,128)(2,1)S(1)}, bf16[528,128]{1,0:T(8,128)(2,1)S(1)}, bf16[528,128]{1,0:T(8,128)(2,1)S(1)}) custom-call(s32[32]{0:T(128)S(1)} %copy-done.9, f32[8,128]{1,0:T(8,128)S(1)} %get-tuple-element.22.stats, bf16[2048,576]{1,0:T(8,128)(2,1)S(1)} %get-tuple-element.23.keys_t, ...), custom_call_target="tpu_custom_call" | custom-call | tf_op jit(solution)/shard_map/attention_target/pallas_call | solution.py:505
  124.6 2.1 collective-permute-start.9
  127.5 2.0 collective-permute-done.8.t1
  129.5 3.7 %collective-permute-done.9.t2 = bf16[528,128]{1,0:T(8,128)(2,1)S(1)} collective-permute-done((bf16[528,128]{1,0:T(8,128)(2,1)S(1)}, bf16[528,128]{1,0:T(8,128)(2,1)S(1)}, u32[]{:S(2)}, u32[]{:S(2)}) %collective-permute-start.9) | collective-permute-done | bytes 135200 | tf_op jit(solution)/shard_map/ppermute | solution.py:521
  134.9 2.2 %collective-permute-start.12 = (bf16[528,128]{1,0:T(8,128)(2,1)S(1)}, bf16[528,128]{1,0:T(8,128)(2,1)S(1)}, u32[]{:S(2)}, u32[]{:S(2)}) collective-permute-start(bf16[528,128]{1,0:T(8,128)(2,1)S(1)} %loss.1.g0), channel_id=1, source_target_pairs={{0,64},{32,96},{64,0},{96,32},{1,65},{33,97},{65,1},{97,33},{2,66}... | collective-permute-start | bytes 405512 | tf_op jit(solution)/shard_map/ppermute | solution.py:427
  139.0 4.2 %collective-permute-done.12.g2 = bf16[528,128]{1,0:T(8,128)(2,1)S(1)} collective-permute-done((bf16[528,128]{1,0:T(8,128)(2,1)S(1)}, bf16[528,128]{1,0:T(8,128)(2,1)S(1)}, u32[]{:S(2)}, u32[]{:S(2)}) %collective-permute-start.12) | collective-permute-done | bytes 135200 | tf_op jit(solution)/shard_map/ppermute | solution.py:427
  143.1 3.8 %index_backward.1 = (bf16[32,64,128]{2,1,0:T(8,128)(2,1)S(1)}, f32[8,128]{1,0:T(8,128)S(1)}) custom-call(bf16[528,128]{1,0:T(8,128)(2,1)S(1)} %loss.1.g0, bf16[528,128]{1,0:T(8,128)(2,1)S(1)} %collective-permute-done.11.g1, bf16[528,128]{1,0:T(8,128)(2,1)S(1)} %collective-permute-done.12.g2, bf16[528,128]{1,0:T(8,128)(2,1)S(1)} %collective-permute-done.13.g3, ...), custom_call_target="tpu_custom_call" | custom-call | tf_op jit(solution)/shard_map/index_backward/pallas_call | solution.py:532
  146.9 20.0 %all_to_all.10.qg = bf16[32,64,128]{2,1,0:T(8,128)(2,1)S(1)} all-to-all(bf16[32,64,128]{2,1,0:T(8,128)(2,1)S(1)} %get-tuple-element.31), channel_id=1, replica_groups=mesh['y'=4,'c'=2,'z'=4,'x'=4] {'z','x','c'}, dimensions={0} | all-to-all | bytes 1048576 | tf_op jit(solution)/shard_map/all_to_all | solution.py:549
  166.9 5.1 %weight_piece.1.p0 = bf16[64,1536]{1,0:T(8,128)(2,1)S(1)} custom-call(bf16[32,64,128]{2,1,0:T(8,128)(2,1)S(1)} %all_to_all.10.qg, bf16[4096,768]{1,0:T(8,128)(2,1)} %all-gather.2.cloned.1.call-done.xa, bf16[4096,768]{1,0:T(8,128)(2,1)S(1)} %collective-permute-done.14.xb), custom_call_target="tpu_custom_call" | custom-call | tf_op jit(solution)/shard_map/weight_piece/pallas_call | solution.py:551
  174.6 2.6 %collective-permute-start.17 = (bf16[64,1536]{1,0:T(8,128)(2,1)S(1)}, bf16[64,1536]{1,0:T(8,128)(2,1)S(1)}, u32[]{:S(2)}, u32[]{:S(2)}) collective-permute-start(bf16[64,1536]{1,0:T(8,128)(2,1)S(1)} %weight_piece.1.p0), channel_id=1, source_target_pairs={{0,11},{1,8},{2,9},{3,10},{4,15},{5,12},{6,13},{7,14},{8,3},{9,0},... | collective-permute-start | bytes 589832 | tf_op jit(solution)/shard_map/ppermute | solution.py:563
  177.2 4.6 %collective-permute-done.15.p1 = bf16[64,1536]{1,0:T(8,128)(2,1)S(1)} collective-permute-done((bf16[64,1536]{1,0:T(8,128)(2,1)S(1)}, bf16[64,1536]{1,0:T(8,128)(2,1)S(1)}, u32[]{:S(2)}, u32[]{:S(2)}) %collective-permute-start.15) | collective-permute-done | bytes 196640 | tf_op jit(solution)/shard_map/ppermute | solution.py:563
  181.7 1.7 collective-permute-done.16.p2
  183.4 2.9 %collective-permute-done.17.p3 = bf16[64,1536]{1,0:T(8,128)(2,1)S(1)} collective-permute-done((bf16[64,1536]{1,0:T(8,128)(2,1)S(1)}, bf16[64,1536]{1,0:T(8,128)(2,1)S(1)}, u32[]{:S(2)}, u32[]{:S(2)}) %collective-permute-start.17) | collective-permute-done | bytes 196640 | tf_op jit(solution)/shard_map/ppermute | solution.py:563
  187.7 1.7 collective-permute-start.19
  189.4 2.3 %collective-permute-start.22 = (f32[8,128]{1,0:T(8,128)S(1)}, f32[8,128]{1,0:T(8,128)S(1)}, u32[]{:S(2)}, u32[]{:S(2)}) collective-permute-start(f32[8,128]{1,0:T(8,128)S(1)} %get-tuple-element.37), channel_id=1, source_target_pairs={{0,16},{16,0},{1,17},{17,1},{2,18},{18,2},{3,19},{19,3},{4,20},{20... | collective-permute-start | bytes 12296 | tf_op jit(solution)/shard_map/ppermute | solution.py:540
  191.7 2.2 %collective-permute-start.20 = (bf16[768,256]{1,0:T(8,128)(2,1)S(1)}, bf16[768,256]{1,0:T(8,128)(2,1)S(1)}, u32[]{:S(2)}, u32[]{:S(2)}) collective-permute-start(bf16[768,256]{1,0:T(8,128)(2,1)S(1)} %get-tuple-element.35), channel_id=1, source_target_pairs={{0,3},{1,0},{2,1},{3,2},{4,7},{5,4},{6,5},{7,6},{8,11},{9,8},{10,9... | collective-permute-start | bytes 1179656 | tf_op jit(solution)/shard_map/ppermute | solution.py:574
  194.5 7.9 %collective-permute-done.20.top = bf16[768,256]{1,0:T(8,128)(2,1)S(1)} collective-permute-done((bf16[768,256]{1,0:T(8,128)(2,1)S(1)}, bf16[768,256]{1,0:T(8,128)(2,1)S(1)}, u32[]{:S(2)}, u32[]{:S(2)}) %collective-permute-start.20) | collective-permute-done | bytes 393248 | tf_op jit(solution)/shard_map/ppermute | solution.py:574
  202.4 3.1 %collective-permute-done.21.bottom = bf16[768,256]{1,0:T(8,128)(2,1)S(1)} collective-permute-done((bf16[768,256]{1,0:T(8,128)(2,1)S(1)}, bf16[768,256]{1,0:T(8,128)(2,1)S(1)}, u32[]{:S(2)}, u32[]{:S(2)}) %collective-permute-start.21) | collective-permute-done | bytes 393248 | tf_op jit(solution)/shard_map/ppermute | solution.py:575
  205.7 2.8 %finish.1 = f32[1536,1024]{1,0:T(8,128)} custom-call(bf16[1536,256]{1,0:T(8,128)(2,1)S(1)} %get-tuple-element.34.own, bf16[1536,256]{1,0:T(8,128)(2,1)S(1)} %collective-permute-done.18.below, bf16[1536,256]{1,0:T(8,128)(2,1)S(1)} %collective-permute-done.19.above, bf16[768,256]{1,0:T(8,128)(2,1)S(1)} %collective-permute-done.20.top, ...), custom_call_target="tpu_custom_call" | custom-call | tf_op jit(solution)/shard_map/finish/pallas_call | solution.py:576
  (58 shorter events, 22.4 us)
Async XLA Ops:
  12.3 8.8 %copy-start = (bf16[1536,1024]{1,0:T(8,128)(2,1)S(1)}, bf16[1536,1024]{1,0:T(8,128)(2,1)}, u32[]{:S(2)}) copy-start(bf16[1536,1024]{1,0:T(8,128)(2,1)} %w.1) | copy-start | bytes 9437188
  12.3 8.8 %copy-start.8 = (f32[256,8]{0,1:T(8,128)S(1)}, f32[256,8]{0,1:T(8,128)}, u32[]{:S(2)}) copy-start(f32[256,8]{0,1:T(8,128)} %param.11) | copy-start | bytes 24580
  12.4 41.9 %all-to-all-start = ((bf16[48,176,128]{2,1,0:T(8,128)(2,1)}), bf16[48,176,128]{2,1,0:T(8,128)(2,1)}, u32[]{:S(2)}, u32[]{:S(2)}) async-start(bf16[48,176,128]{2,1,0:T(8,128)(2,1)} %pick_outgoing.1), calls=%async_computation | async-start | bytes 4325376 | tf_op jit(solution)/shard_map/all_to_all | solution.py:445
  21.1 101.0 %all-gather.2.cloned.1.call-start = ((), (), s32[]{:S(2)}) async-start(), calls=%async_computation.2 | async-start | bytes 6684672 | tf_op jit(solution)/shard_map/all_gather | solution.py:482
  24.1 2.3 %collective-permute-start = (bf16[1056,128]{1,0:T(8,128)(2,1)}, bf16[1056,128]{1,0:T(8,128)(2,1)S(1)}, u32[]{:S(2)}, u32[]{:S(2)}) collective-permute-start(bf16[1056,128]{1,0:T(8,128)(2,1)} %get-tuple-element.21), channel_id=1, source_target_pairs={{0,16},{16,0},{1,17},{17,1},{2,18},{18,2},{3,19},{19,3},{4,20},{20... | collective-permute-start | bytes 811016 | tf_op jit(solution)/shard_map/ppermute | solution.py:454
  26.5 27.8 %copy-start.7 = (s32[32,16]{0,1:T(8,128)S(1)}, s32[32,16]{0,1:T(8,128)}, u32[]{:S(2)}) copy-start(s32[32,16]{0,1:T(8,128)} %param.12) | copy-start | bytes 6148
  26.6 15.0 %collective-permute-start.1 = (bf16[2,1056,128]{2,1,0:T(8,128)(2,1)S(1)}, bf16[2,1056,128]{2,1,0:T(8,128)(2,1)S(1)}, u32[]{:S(2)}, u32[]{:S(2)}) collective-permute-start(bf16[2,1056,128]{2,1,0:T(8,128)(2,1)S(1)} %pad_maximum_fusion.iq0.iq), channel_id=1, source_target_pairs={{0,32},{32,64},{64,96},{96,0},{1,33},{33,65},{65,97},{97,1},{2,34}... | collective-permute-start | bytes 1622024 | tf_op jit(solution)/shard_map/ppermute | solution.py:427
  27.9 26.3 %collective-permute-start.2 = (bf16[2,1056,128]{2,1,0:T(8,128)(2,1)S(1)}, bf16[2,1056,128]{2,1,0:T(8,128)(2,1)}, u32[]{:S(2)}, u32[]{:S(2)}) collective-permute-start(bf16[2,1056,128]{2,1,0:T(8,128)(2,1)S(1)} %pad_maximum_fusion.iq0.iq), channel_id=1, source_target_pairs={{0,64},{32,96},{64,0},{96,32},{1,65},{33,97},{65,1},{97,33},{2,66}... | collective-permute-start | bytes 1622024 | tf_op jit(solution)/shard_map/ppermute | solution.py:427
  30.6 23.7 %collective-permute-start.3 = (bf16[2,1056,128]{2,1,0:T(8,128)(2,1)S(1)}, bf16[2,1056,128]{2,1,0:T(8,128)(2,1)}, u32[]{:S(2)}, u32[]{:S(2)}) collective-permute-start(bf16[2,1056,128]{2,1,0:T(8,128)(2,1)S(1)} %pad_maximum_fusion.iq0.iq), channel_id=1, source_target_pairs={{0,96},{32,0},{64,32},{96,64},{1,97},{33,1},{65,33},{97,65},{2,98}... | collective-permute-start | bytes 1622024 | tf_op jit(solution)/shard_map/ppermute | solution.py:427
  35.3 58.1 %copy-start.9 = (s32[32]{0:T(128)S(1)}, s32[32]{0:T(128)}, u32[]{:S(2)}) copy-start(s32[32]{0:T(128)} %counts.3) | copy-start | bytes 388
  57.0 43.6 %collective-permute-start.7 = (bf16[16,576,128]{2,1,0:T(8,128)(2,1)S(1)}, bf16[16,576,128]{2,1,0:T(8,128)(2,1)S(1)}, u32[]{:S(2)}, u32[]{:S(2)}) collective-permute-start(bf16[16,576,128]{2,1,0:T(8,128)(2,1)S(1)} %dynamic-slice_bitcast_fusion.refs_0_), channel_id=1, source_target_pairs={{0,16},{16,0},{1,17},{17,1},{2,18},{18,2},{3,19},{19,3},{4,20},{20... | collective-permute-start | bytes 7077896 | tf_op jit(solution)/shard_map/ppermute | solution.py:463
  58.3 19.1 %collective-permute-start.4 = (bf16[16,176,128]{2,1,0:T(8,128)(2,1)}, bf16[16,176,128]{2,1,0:T(8,128)(2,1)S(1)}, u32[]{:S(2)}, u32[]{:S(2)}) collective-permute-start(bf16[16,176,128]{2,1,0:T(8,128)(2,1)} %pick_listed.1.p0), channel_id=1, source_target_pairs={{0,32},{32,64},{64,96},{96,0},{1,33},{33,65},{65,97},{97,1},{2,34}... | collective-permute-start | bytes 2162696 | tf_op jit(solution)/shard_map/ppermute | solution.py:427
  59.2 34.1 %collective-permute-start.5 = (bf16[16,176,128]{2,1,0:T(8,128)(2,1)}, bf16[16,176,128]{2,1,0:T(8,128)(2,1)S(1)}, u32[]{:S(2)}, u32[]{:S(2)}) collective-permute-start(bf16[16,176,128]{2,1,0:T(8,128)(2,1)} %pick_listed.1.p0), channel_id=1, source_target_pairs={{0,64},{32,96},{64,0},{96,32},{1,65},{33,97},{65,1},{97,33},{2,66}... | collective-permute-start | bytes 2162696 | tf_op jit(solution)/shard_map/ppermute | solution.py:427
  61.4 31.9 %collective-permute-start.6 = (bf16[16,176,128]{2,1,0:T(8,128)(2,1)}, bf16[16,176,128]{2,1,0:T(8,128)(2,1)S(1)}, u32[]{:S(2)}, u32[]{:S(2)}) collective-permute-start(bf16[16,176,128]{2,1,0:T(8,128)(2,1)} %pick_listed.1.p0), channel_id=1, source_target_pairs={{0,96},{32,0},{64,32},{96,64},{1,97},{33,1},{65,33},{97,65},{2,98}... | collective-permute-start | bytes 2162696 | tf_op jit(solution)/shard_map/ppermute | solution.py:427
  100.6 32.6 %copy-start.5 = (f32[512,128]{1,0:T(8,128)S(1)}, f32[512,128]{1,0:T(8,128)}, u32[]{:S(2)}) copy-start(f32[512,128]{1,0:T(8,128)} %copy-done.4) | copy-start | bytes 786436
  100.6 42.5 %copy-start.2 = (bf16[128,2048]{1,0:T(8,128)(2,1)S(1)}, bf16[128,2048]{1,0:T(8,128)(2,1)}, u32[]{:S(2)}) copy-start(bf16[128,2048]{1,0:T(8,128)(2,1)} %get-tuple-element.29.keys) | copy-start | bytes 1572868
  100.6 42.5 %copy-start.3 = (bf16[2048,128]{1,0:T(8,128)(2,1)S(1)}, bf16[2048,128]{1,0:T(8,128)(2,1)}, u32[]{:S(2)}) copy-start(bf16[2048,128]{1,0:T(8,128)(2,1)} %get-tuple-element.30.keys_t) | copy-start | bytes 1572868
  122.1 44.8 %collective-permute-start.14 = (bf16[4096,768]{1,0:T(8,128)(2,1)}, bf16[4096,768]{1,0:T(8,128)(2,1)S(1)}, u32[]{:S(2)}, u32[]{:S(2)}) collective-permute-start(bf16[4096,768]{1,0:T(8,128)(2,1)} %all-gather.2.cloned.1.call-done.xa), channel_id=1, source_target_pairs={{0,16},{16,0},{1,17},{17,1},{2,18},{18,2},{3,19},{19,3},{4,20},{20... | collective-permute-start | bytes 18874376 | tf_op jit(solution)/shard_map/ppermute | solution.py:520
  123.1 6.4 %collective-permute-start.8 = (bf16[528,128]{1,0:T(8,128)(2,1)S(1)}, bf16[528,128]{1,0:T(8,128)(2,1)S(1)}, u32[]{:S(2)}, u32[]{:S(2)}) collective-permute-start(bf16[528,128]{1,0:T(8,128)(2,1)S(1)} %get-tuple-element.25), channel_id=1, source_target_pairs={{0,32},{32,64},{64,96},{96,0},{1,33},{33,65},{65,97},{97,1},{2,34}... | collective-permute-start | bytes 405512 | tf_op jit(solution)/shard_map/ppermute | solution.py:521
  124.6 8.7 %collective-permute-start.9 = (bf16[528,128]{1,0:T(8,128)(2,1)S(1)}, bf16[528,128]{1,0:T(8,128)(2,1)S(1)}, u32[]{:S(2)}, u32[]{:S(2)}) collective-permute-start(bf16[528,128]{1,0:T(8,128)(2,1)S(1)} %get-tuple-element.26), channel_id=1, source_target_pairs={{0,64},{32,96},{64,0},{96,32},{1,65},{33,97},{65,1},{97,33},{2,66}... | collective-permute-start | bytes 405512 | tf_op jit(solution)/shard_map/ppermute | solution.py:521
  126.7 6.6 %collective-permute-start.10 = (bf16[528,128]{1,0:T(8,128)(2,1)S(1)}, bf16[528,128]{1,0:T(8,128)(2,1)S(1)}, u32[]{:S(2)}, u32[]{:S(2)}) collective-permute-start(bf16[528,128]{1,0:T(8,128)(2,1)S(1)} %get-tuple-element.27), channel_id=1, source_target_pairs={{0,96},{32,0},{64,32},{96,64},{1,97},{33,1},{65,33},{97,65},{2,98}... | collective-permute-start | bytes 405512 | tf_op jit(solution)/shard_map/ppermute | solution.py:521
  133.4 5.5 %collective-permute-start.11 = (bf16[528,128]{1,0:T(8,128)(2,1)S(1)}, bf16[528,128]{1,0:T(8,128)(2,1)S(1)}, u32[]{:S(2)}, u32[]{:S(2)}) collective-permute-start(bf16[528,128]{1,0:T(8,128)(2,1)S(1)} %loss.1.g0), channel_id=1, source_target_pairs={{0,32},{32,64},{64,96},{96,0},{1,33},{33,65},{65,97},{97,1},{2,34}... | collective-permute-start | bytes 405512 | tf_op jit(solution)/shard_map/ppermute | solution.py:427
  134.9 8.2 %collective-permute-start.12 = (bf16[528,128]{1,0:T(8,128)(2,1)S(1)}, bf16[528,128]{1,0:T(8,128)(2,1)S(1)}, u32[]{:S(2)}, u32[]{:S(2)}) collective-permute-start(bf16[528,128]{1,0:T(8,128)(2,1)S(1)} %loss.1.g0), channel_id=1, source_target_pairs={{0,64},{32,96},{64,0},{96,32},{1,65},{33,97},{65,1},{97,33},{2,66}... | collective-permute-start | bytes 405512 | tf_op jit(solution)/shard_map/ppermute | solution.py:427
  137.1 6.0 %collective-permute-start.13 = (bf16[528,128]{1,0:T(8,128)(2,1)S(1)}, bf16[528,128]{1,0:T(8,128)(2,1)S(1)}, u32[]{:S(2)}, u32[]{:S(2)}) collective-permute-start(bf16[528,128]{1,0:T(8,128)(2,1)S(1)} %loss.1.g0), channel_id=1, source_target_pairs={{0,96},{32,0},{64,32},{96,64},{1,97},{33,1},{65,33},{97,65},{2,98}... | collective-permute-start | bytes 405512 | tf_op jit(solution)/shard_map/ppermute | solution.py:427
  172.0 9.7 %collective-permute-start.15 = (bf16[64,1536]{1,0:T(8,128)(2,1)S(1)}, bf16[64,1536]{1,0:T(8,128)(2,1)S(1)}, u32[]{:S(2)}, u32[]{:S(2)}) collective-permute-start(bf16[64,1536]{1,0:T(8,128)(2,1)S(1)} %weight_piece.1.p0), channel_id=1, source_target_pairs={{0,9},{1,10},{2,11},{3,8},{4,13},{5,14},{6,15},{7,12},{8,1},{9,2},... | collective-permute-start | bytes 589832 | tf_op jit(solution)/shard_map/ppermute | solution.py:563
  173.5 9.9 %collective-permute-start.16 = (bf16[64,1536]{1,0:T(8,128)(2,1)S(1)}, bf16[64,1536]{1,0:T(8,128)(2,1)S(1)}, u32[]{:S(2)}, u32[]{:S(2)}) collective-permute-start(bf16[64,1536]{1,0:T(8,128)(2,1)S(1)} %weight_piece.1.p0), channel_id=1, source_target_pairs={{0,2},{1,3},{2,0},{3,1},{4,6},{5,7},{6,4},{7,5},{8,10},{9,11},{10,... | collective-permute-start | bytes 589832 | tf_op jit(solution)/shard_map/ppermute | solution.py:563
  174.6 11.7 %collective-permute-start.17 = (bf16[64,1536]{1,0:T(8,128)(2,1)S(1)}, bf16[64,1536]{1,0:T(8,128)(2,1)S(1)}, u32[]{:S(2)}, u32[]{:S(2)}) collective-permute-start(bf16[64,1536]{1,0:T(8,128)(2,1)S(1)} %weight_piece.1.p0), channel_id=1, source_target_pairs={{0,11},{1,8},{2,9},{3,10},{4,15},{5,12},{6,13},{7,14},{8,3},{9,0},... | collective-permute-start | bytes 589832 | tf_op jit(solution)/shard_map/ppermute | solution.py:563
  186.6 18.9 %collective-permute-start.18 = (bf16[1536,256]{1,0:T(8,128)(2,1)S(1)}, bf16[1536,256]{1,0:T(8,128)(2,1)S(1)}, u32[]{:S(2)}, u32[]{:S(2)}) collective-permute-start(bf16[1536,256]{1,0:T(8,128)(2,1)S(1)} %get-tuple-element.34.own), channel_id=1, source_target_pairs={{0,4},{1,5},{2,6},{3,7},{4,8},{5,9},{6,10},{7,11},{8,12},{9,13},{1... | collective-permute-start | bytes 2359304 | tf_op jit(solution)/shard_map/ppermute | solution.py:572
  187.7 18.0 %collective-permute-start.19 = (bf16[1536,256]{1,0:T(8,128)(2,1)S(1)}, bf16[1536,256]{1,0:T(8,128)(2,1)S(1)}, u32[]{:S(2)}, u32[]{:S(2)}) collective-permute-start(bf16[1536,256]{1,0:T(8,128)(2,1)S(1)} %get-tuple-element.34.own), channel_id=1, source_target_pairs={{0,12},{1,13},{2,14},{3,15},{4,0},{5,1},{6,2},{7,3},{8,4},{9,5},{1... | collective-permute-start | bytes 2359304 | tf_op jit(solution)/shard_map/ppermute | solution.py:573
  189.4 4.5 %collective-permute-start.22 = (f32[8,128]{1,0:T(8,128)S(1)}, f32[8,128]{1,0:T(8,128)S(1)}, u32[]{:S(2)}, u32[]{:S(2)}) collective-permute-start(f32[8,128]{1,0:T(8,128)S(1)} %get-tuple-element.37), channel_id=1, source_target_pairs={{0,16},{16,0},{1,17},{17,1},{2,18},{18,2},{3,19},{19,3},{4,20},{20... | collective-permute-start | bytes 12296 | tf_op jit(solution)/shard_map/ppermute | solution.py:540
  191.7 10.7 %collective-permute-start.20 = (bf16[768,256]{1,0:T(8,128)(2,1)S(1)}, bf16[768,256]{1,0:T(8,128)(2,1)S(1)}, u32[]{:S(2)}, u32[]{:S(2)}) collective-permute-start(bf16[768,256]{1,0:T(8,128)(2,1)S(1)} %get-tuple-element.35), channel_id=1, source_target_pairs={{0,3},{1,0},{2,1},{3,2},{4,7},{5,4},{6,5},{7,6},{8,11},{9,8},{10,9... | collective-permute-start | bytes 1179656 | tf_op jit(solution)/shard_map/ppermute | solution.py:574
  193.9 11.6 %collective-permute-start.21 = (bf16[768,256]{1,0:T(8,128)(2,1)S(1)}, bf16[768,256]{1,0:T(8,128)(2,1)S(1)}, u32[]{:S(2)}, u32[]{:S(2)}) collective-permute-start(bf16[768,256]{1,0:T(8,128)(2,1)S(1)} %get-tuple-element.36), channel_id=1, source_target_pairs={{0,1},{1,2},{2,3},{3,0},{4,5},{5,6},{6,7},{7,4},{8,9},{9,10},{10,1... | collective-permute-start | bytes 1179656 | tf_op jit(solution)/shard_map/ppermute | solution.py:575
  (3 other events, 2.5 us)
Sparse Core Ops, SparseCore 0:
  57.1 62.9 all-gather.1

commit v5 on v4

--- a/solution.py
+++ b/solution.py
@@ -109,7 +109,7 @@
 
 
 def pick_listed_kernel(ids, arrived, *refs):
-    sent, listed, seen, sem = refs[-4:]
+    low, high, listed, seen, sem = refs[-5:]
     _, core, me = place()
     row = 2 * me + core
     for i in range(NQ):
@@ -123,9 +123,15 @@
         pending[-1].start()
     for c in pending:
         c.wait()
-    out = pltpu.make_async_copy(listed, sent, sem.at[1])
-    out.start()
-    out.wait()
+    half = SEL // 2
+    outs = [
+        pltpu.make_async_copy(listed.at[pl.ds(n * half, half)], out, sem.at[1])
+        for n, out in enumerate((low, high))
+    ]
+    for c in outs:
+        c.start()
+    for c in outs:
+        c.wait()
 
 
 def index_query_kernel(x, w, hw, mine, other):
@@ -159,17 +165,24 @@
     return tail[0:8] + tail[8:16] + tail[16:24]
 
 
-def logits_kernel(counts, p0, p1, p2, p3, iq0, iq1, iq2, iq3, *rest):
+def logits_kernel(counts, own_low, own_high, a1, b1, a2, b2, a3, b3, iq0, iq1, iq2, iq3, *rest):
     logits_ref, stats_ref, latent_t, keys_out, keys_t_out, index_t, keys, total, own, sems = rest
     y, count = lax.axis_index("y"), slots_in_use(counts)
-    load = pltpu.make_async_copy(p0, own, sems.at[2])
-    load.start()
-    for s, piece in ((1, p1), (2, p2), (3, p3), (0, own)):
+    half = SEL // 2
+    loads = [
+        pltpu.make_async_copy(own_low, own.at[pl.ds(0, half)], sems.at[2]),
+        pltpu.make_async_copy(own_high, own.at[pl.ds(half, half)], sems.at[3]),
+    ]
+    for c in loads:
+        c.start()
+    for s, low, high in ((1, a1, b1), (2, a2, b2), (3, a3, b3), (0, own, own.at[pl.ds(half, half)])):
         if s == 0:
-            load.wait()
+            for c in loads:
+                c.wait()
         rows = pl.ds(pl.multiple_of(lax.rem(y + NY - s, NY) * PIECE, 16), PIECE)
-        for j in range(SEL):
-            keys[rows, j * BLK : (j + 1) * BLK] = piece[j]
+        for j in range(half):
+            keys[rows, j * BLK : (j + 1) * BLK] = low[j]
+            keys[rows, (half + j) * BLK : (half + j + 1) * BLK] = high[j]
     copies = [pltpu.make_async_copy(keys.at[pl.ds(DK, ID), :], keys_out, sems.at[0])]
     copies[0].start()
     for j in range(SEL):
@@ -462,11 +475,11 @@
     q_send = lax.dynamic_slice_in_dim(q_t, (1 - core) * BLK, BLK, 2)
     q_other = lax.ppermute(q_send, "c", SWAP)
 
-    listed = call(
+    low, high = call(
         pick_listed_kernel,
-        pltpu.HBM((SEL, PIECE, BLK), BF16),
+        (pltpu.HBM((SEL // 2, PIECE, BLK), BF16),) * 2,
         [SMEM] + [ANY] * 5,
-        HBM,
+        (HBM, HBM),
         [
             pltpu.VMEM((SEL, PIECE, BLK), BF16),
             pltpu.SMEM((NQ,), I32),
@@ -474,11 +487,14 @@
         ],
         "pick_listed",
     )(ids, arrived, q_send, *iq_all[1:])
-    pieces = around_y(listed)
+    low_up, high_down = lax.ppermute(low, "y", ring(1)), lax.ppermute(high, "y", ring(3))
+    high_up, low_down = lax.ppermute(high, "y", ring(1)), lax.ppermute(low, "y", ring(3))
+    low_far, high_far = lax.ppermute(low_up, "y", ring(1)), lax.ppermute(high_down, "y", ring(3))
+    moved = (low_up, high_up, low_far, high_far, low_down, high_down)
 
     half = DQ // 2
     x_half = lax.dynamic_slice_in_dim(index_input, core * half, half, 1)
-    x_half, _ = lax.optimization_barrier((x_half, listed))
+    x_half, _ = lax.optimization_barrier((x_half, low))
     x_own = lax.all_gather(x_half, ("z", "x"), axis=0, tiled=True)
 
     logits, stats, latent_t, index_keys, index_t = call(
@@ -490,17 +506,17 @@
             pltpu.HBM((ID, KEYS), BF16),
             pltpu.HBM((KEYS, ID), BF16),
         ),
-        [SMEM, ANY] + [VMEM] * 7,
+        [SMEM, ANY, ANY] + [VMEM] * 10,
         (VMEM, VMEM, VMEM, HBM, HBM),
         [
             pltpu.VMEM((KEYS, ID), BF16),
             pltpu.VMEM((DK + ID, KEYS), BF16),
             pltpu.VMEM((OWNK, BLK), F32),
             pltpu.VMEM((SEL, PIECE, BLK), BF16),
-            pltpu.SemaphoreType.DMA((3,)),
+            pltpu.SemaphoreType.DMA((4,)),
         ],
         "index_logits",
-    )(block_counts, in_hbm(pieces[0]), *map(in_vmem, (*pieces[1:], *iq_all)))
+    )(block_counts, in_hbm(low), in_hbm(high), *map(in_vmem, (*moved, *iq_all)))
 
     targets = call(
         target_kernel,
@@ -516,8 +532,6 @@
         ],
         "attention_target",
     )(block_counts, stats, in_vmem(latent_t), in_hbm(q_t), in_vmem(q_other))
-    x_own, _ = lax.optimization_barrier((x_own, targets[0]))
-    x_other = lax.ppermute(x_own, "c", SWAP)
     arrived_targets = {s: lax.ppermute(targets[s], "y", ring(s)) for s in SHIFTS}
 
     grads = call(
@@ -527,6 +541,8 @@
         VMEM,
         name="loss",
     )(*map(in_vmem, (targets[0], *(arrived_targets[s] for s in (1, 2, 3)), logits)))
+    x_own, _ = lax.optimization_barrier((x_own, grads))
+    x_other = lax.ppermute(x_own, "c", SWAP)
     grads_all = around_y(grads)
 
     query_grad, entropy = call(

time: 218 us -> 209 us (0.959)
  waiting for transfers between devices: 82.9 us -> 70.5 us
  starting transfers between devices: 42.2 us -> 47.5 us
    ppermute x9 -> x6, waiting for transfers between devices: 55.4 us -> 25 us  [around_y(): moved = {s: lax.ppermute(array, 'y', ring(s)) for s in SHIFTS}]
    ppermute x0 -> x6, waiting for transfers between devices: none -> 18.8 us  [the longest x1 7.72 us: on_device(): lax.ppermute(low_up, 'y', ring(1))]
    ppermute x0 -> x6, starting transfers between devices: none -> 8.04 us  [the longest x1 2.67 us: on_device(): lax.ppermute(high_down, 'y', ring(3))]
    ppermute x9 -> x6, starting transfers between devices: 13.4 us -> 9.05 us  [around_y(): moved = {s: lax.ppermute(array, 'y', ring(s)) for s in SHIFTS}]
  transfers between devices with their start and end apart: 25 -> 28, of which waited for: 15 -> 17; matrix products, arithmetic and copies ran while one was open for 2% -> 2% of each run, Pallas kernels for 16% -> 16%
where the time goes in v5:
time: 209 us; the launch traced here: 207 us
  waiting for transfers between devices  70.5 us (34%)
  Pallas kernels  48.9 us (23%)
  starting transfers between devices  47.5 us (23%)
  blocking collectives  19.4 us (9%)
  between operations  14.3 us (7%)
  local copies, waits for them, and re-layouts  6.06 us (3%)
    ppermute x6, waiting for transfers between devices, around_y(): moved = {s: lax.ppermute(array, 'y', ring(s)) for s in SHIFTS}  25 us
    pallas_call x1, Pallas kernels, on_device(): call(target_kernel, (shape((LG_ROWS, BLK), BF16),) * 4, [SMEM, VMEM, VMEM...  21.3 us
    all_to_all x1, blocking collectives, on_device(): lax.all_to_all(query_grad, ('z', 'x', 'c'), split_axis=0, concat_axis=0,...  19.4 us
    all_to_all x1, starting transfers between devices, on_device(): lax.all_to_all(outgoing, ('z', 'x'), split_axis=0, concat_axis=0, tiled=T...  9.79 us
    ppermute x3, waiting for transfers between devices, on_device(): lax.ppermute(piece, qblk, plane(-2 * d, d))  9.07 us
    ppermute x6, starting transfers between devices, around_y(): moved = {s: lax.ppermute(array, 'y', ring(s)) for s in SHIFTS}  9.05 us
    ppermute x1, waiting for transfers between devices, on_device(): top = lax.ppermute(top, qblk, plane(0, -1))  7.93 us
    ppermute x1, waiting for transfers between devices, on_device(): lax.ppermute(low_up, 'y', ring(1))  7.72 us
  transfers between devices with their start and end apart: 28, of which 17 were waited for; matrix products, arithmetic and copies ran while one was open for 2% of the time, Pallas kernels for 16%

profile of v5, /device:TPU:1, one launch (start us, length us, event | category | flops | bytes accessed | tf_op | source)
XLA Modules:
  0.0 206.8 jit_solution(10205200475457891039)
XLA Ops:
  7.9 4.5 %pick_outgoing.1 = bf16[48,176,128]{2,1,0:T(8,128)(2,1)} custom-call(s32[16,32]{1,0:T(8,128)S(1)} %bitcast.13, bf16[32,704,128]{2,1,0:T(8,128)(2,1)} %cache.1), custom_call_target="tpu_custom_call" | custom-call | tf_op jit(solution)/shard_map/pick_outgoing/pallas_call | solution.py:450
  12.4 9.8 %all-to-all-start = ((bf16[48,176,128]{2,1,0:T(8,128)(2,1)}), bf16[48,176,128]{2,1,0:T(8,128)(2,1)}, u32[]{:S(2)}, u32[]{:S(2)}) async-start(bf16[48,176,128]{2,1,0:T(8,128)(2,1)} %pick_outgoing.1), calls=%async_computation | async-start | bytes 4325376 | tf_op jit(solution)/shard_map/all_to_all | solution.py:458
  28.9 2.6 %collective-permute-start.2 = (bf16[2,1056,128]{2,1,0:T(8,128)(2,1)S(1)}, bf16[2,1056,128]{2,1,0:T(8,128)(2,1)}, u32[]{:S(2)}, u32[]{:S(2)}) collective-permute-start(bf16[2,1056,128]{2,1,0:T(8,128)(2,1)S(1)} %pad_maximum_fusion.iq0.iq), channel_id=1, source_target_pairs={{0,64},{32,96},{64,0},{96,32},{1,65},{33,97},{65,1},{97,33},{2,66}... | collective-permute-start | bytes 1622024 | tf_op jit(solution)/shard_map/ppermute | solution.py:440
  32.7 1.8 constant_dynamic-slice_fusion
  34.4 1.8 dynamic-slice_bitcast_fusion.refs_0_
  36.3 6.3 %collective-permute-done.1.refs_1_.iq1 = bf16[2,1056,128]{2,1,0:T(8,128)(2,1)S(1)} collective-permute-done((bf16[2,1056,128]{2,1,0:T(8,128)(2,1)S(1)}, bf16[2,1056,128]{2,1,0:T(8,128)(2,1)S(1)}, u32[]{:S(2)}, u32[]{:S(2)}) %collective-permute-start.1) | collective-permute-done | bytes 540704 | tf_op jit(solution)/shard_map/ppermute | solution.py:440
  42.6 12.6 %collective-permute-done.2.refs_2_.iq2 = bf16[2,1056,128]{2,1,0:T(8,128)(2,1)} collective-permute-done((bf16[2,1056,128]{2,1,0:T(8,128)(2,1)S(1)}, bf16[2,1056,128]{2,1,0:T(8,128)(2,1)}, u32[]{:S(2)}, u32[]{:S(2)}) %collective-permute-start.2) | collective-permute-done | bytes 540704 | tf_op jit(solution)/shard_map/ppermute | solution.py:440
  55.2 2.7 %pick_listed.1 = (bf16[8,176,128]{2,1,0:T(8,128)(2,1)}, bf16[8,176,128]{2,1,0:T(8,128)(2,1)}) custom-call(s32[16,32]{1,0:T(8,128)S(1)} %bitcast.14, bf16[48,176,128]{2,1,0:T(8,128)(2,1)} %all-to-all-done.arrived, bf16[16,576,128]{2,1,0:T(8,128)(2,1)S(1)} %dynamic-slice_bitcast_fusion.refs_0_, bf16[2,1056,128]{2,1,0:T(8,128)(2,1)S(1)} %collective-permute-done.1.refs_1_.iq1, ...), custom_call_target="tpu_custom_call" | custom-call | tf_op jit(solution)/shard_map/pick_listed/pallas_call | solution.py:478
  62.0 2.7 %collective-permute-start.9 = (bf16[8,176,128]{2,1,0:T(8,128)(2,1)}, bf16[8,176,128]{2,1,0:T(8,128)(2,1)S(1)}, u32[]{:S(2)}, u32[]{:S(2)}) collective-permute-start(bf16[8,176,128]{2,1,0:T(8,128)(2,1)} %get-tuple-element.24.own_low), channel_id=1, source_target_pairs={{0,96},{32,0},{64,32},{96,64},{1,97},{33,1},{65,33},{97,65},{2,98}... | collective-permute-start | bytes 1081352 | tf_op jit(solution)/shard_map/ppermute | solution.py:491
  64.6 6.0 %collective-permute-done.4.a1 = bf16[8,176,128]{2,1,0:T(8,128)(2,1)S(1)} collective-permute-done((bf16[8,176,128]{2,1,0:T(8,128)(2,1)}, bf16[8,176,128]{2,1,0:T(8,128)(2,1)S(1)}, u32[]{:S(2)}, u32[]{:S(2)}) %collective-permute-start.4) | collective-permute-done | bytes 360480 | tf_op jit(solution)/shard_map/ppermute | solution.py:490
  70.7 2.7 %collective-permute-start.8 = (bf16[8,176,128]{2,1,0:T(8,128)(2,1)S(1)}, bf16[8,176,128]{2,1,0:T(8,128)(2,1)S(1)}, u32[]{:S(2)}, u32[]{:S(2)}) collective-permute-start(bf16[8,176,128]{2,1,0:T(8,128)(2,1)S(1)} %collective-permute-done.7.b3), channel_id=1, source_target_pairs={{0,96},{32,0},{64,32},{96,64},{1,97},{33,1},{65,33},{97,65},{2,98}... | collective-permute-start | bytes 1081352 | tf_op jit(solution)/shard_map/ppermute | solution.py:492
  73.3 5.0 %collective-permute-done.5.b1 = bf16[8,176,128]{2,1,0:T(8,128)(2,1)S(1)} collective-permute-done((bf16[8,176,128]{2,1,0:T(8,128)(2,1)}, bf16[8,176,128]{2,1,0:T(8,128)(2,1)S(1)}, u32[]{:S(2)}, u32[]{:S(2)}) %collective-permute-start.5) | collective-permute-done | bytes 360480 | tf_op jit(solution)/shard_map/ppermute | solution.py:491
  78.4 7.7 %collective-permute-done.6.a2 = bf16[8,176,128]{2,1,0:T(8,128)(2,1)S(1)} collective-permute-done((bf16[8,176,128]{2,1,0:T(8,128)(2,1)S(1)}, bf16[8,176,128]{2,1,0:T(8,128)(2,1)S(1)}, u32[]{:S(2)}, u32[]{:S(2)}) %collective-permute-start.6) | collective-permute-done | bytes 360480 | tf_op jit(solution)/shard_map/ppermute | solution.py:492
  86.1 6.5 %index_logits.1 = (f32[512,128]{1,0:T(8,128)S(1)}, f32[8,128]{1,0:T(8,128)S(1)}, bf16[2048,576]{1,0:T(8,128)(2,1)S(1)}, bf16[128,2048]{1,0:T(8,128)(2,1)}, bf16[2048,128]{1,0:T(8,128)(2,1)}) custom-call(s32[32]{0:T(128)S(1)} %copy-done.7, bf16[8,176,128]{2,1,0:T(8,128)(2,1)} %get-tuple-element.24.own_low, bf16[8,176,128]{2,1,0:T(8,128)(2,1)} %get-tuple-element.25.own_high, ...), custom_call_target="tpu_custom_call" | custom-call | tf_op jit(solution)/shard_map/index_logits/pallas_call | solution.py:500
  92.6 21.3 %attention_target.1 = (bf16[528,128]{1,0:T(8,128)(2,1)S(1)}, bf16[528,128]{1,0:T(8,128)(2,1)S(1)}, bf16[528,128]{1,0:T(8,128)(2,1)S(1)}, bf16[528,128]{1,0:T(8,128)(2,1)S(1)}) custom-call(s32[32]{0:T(128)S(1)} %copy-done.7, f32[8,128]{1,0:T(8,128)S(1)} %get-tuple-element.26.stats, bf16[2048,576]{1,0:T(8,128)(2,1)S(1)} %get-tuple-element.27.keys_t, ...), custom_call_target="tpu_custom_call" | custom-call | tf_op jit(solution)/shard_map/attention_target/pallas_call | solution.py:521
  115.0 2.5 %collective-permute-start.12 = (bf16[528,128]{1,0:T(8,128)(2,1)S(1)}, bf16[528,128]{1,0:T(8,128)(2,1)S(1)}, u32[]{:S(2)}, u32[]{:S(2)}) collective-permute-start(bf16[528,128]{1,0:T(8,128)(2,1)S(1)} %get-tuple-element.30), channel_id=1, source_target_pairs={{0,64},{32,96},{64,0},{96,32},{1,65},{33,97},{65,1},{97,33},{2,66}... | collective-permute-start | bytes 405512 | tf_op jit(solution)/shard_map/ppermute | solution.py:535
  119.6 3.0 %collective-permute-done.12.t2 = bf16[528,128]{1,0:T(8,128)(2,1)S(1)} collective-permute-done((bf16[528,128]{1,0:T(8,128)(2,1)S(1)}, bf16[528,128]{1,0:T(8,128)(2,1)S(1)}, u32[]{:S(2)}, u32[]{:S(2)}) %collective-permute-start.12) | collective-permute-done | bytes 135200 | tf_op jit(solution)/shard_map/ppermute | solution.py:535
  123.3 1.9 collective-permute-start.17
  126.4 2.1 %collective-permute-start.15 = (bf16[528,128]{1,0:T(8,128)(2,1)S(1)}, bf16[528,128]{1,0:T(8,128)(2,1)S(1)}, u32[]{:S(2)}, u32[]{:S(2)}) collective-permute-start(bf16[528,128]{1,0:T(8,128)(2,1)S(1)} %loss.1.g0), channel_id=1, source_target_pairs={{0,64},{32,96},{64,0},{96,32},{1,65},{33,97},{65,1},{97,33},{2,66}... | collective-permute-start | bytes 405512 | tf_op jit(solution)/shard_map/ppermute | solution.py:440
  129.1 2.5 %collective-permute-done.14.g1 = bf16[528,128]{1,0:T(8,128)(2,1)S(1)} collective-permute-done((bf16[528,128]{1,0:T(8,128)(2,1)S(1)}, bf16[528,128]{1,0:T(8,128)(2,1)S(1)}, u32[]{:S(2)}, u32[]{:S(2)}) %collective-permute-start.14) | collective-permute-done | bytes 135200 | tf_op jit(solution)/shard_map/ppermute | solution.py:440
  131.6 3.5 %collective-permute-done.15.g2 = bf16[528,128]{1,0:T(8,128)(2,1)S(1)} collective-permute-done((bf16[528,128]{1,0:T(8,128)(2,1)S(1)}, bf16[528,128]{1,0:T(8,128)(2,1)S(1)}, u32[]{:S(2)}, u32[]{:S(2)}) %collective-permute-start.15) | collective-permute-done | bytes 135200 | tf_op jit(solution)/shard_map/ppermute | solution.py:440
  135.1 3.8 %index_backward.1 = (bf16[32,64,128]{2,1,0:T(8,128)(2,1)S(1)}, f32[8,128]{1,0:T(8,128)S(1)}) custom-call(bf16[528,128]{1,0:T(8,128)(2,1)S(1)} %loss.1.g0, bf16[528,128]{1,0:T(8,128)(2,1)S(1)} %collective-permute-done.14.g1, bf16[528,128]{1,0:T(8,128)(2,1)S(1)} %collective-permute-done.15.g2, bf16[528,128]{1,0:T(8,128)(2,1)S(1)} %collective-permute-done.16.g3, ...), custom_call_target="tpu_custom_call" | custom-call | tf_op jit(solution)/shard_map/index_backward/pallas_call | solution.py:548
  138.9 19.4 %all_to_all.10.qg = bf16[32,64,128]{2,1,0:T(8,128)(2,1)S(1)} all-to-all(bf16[32,64,128]{2,1,0:T(8,128)(2,1)S(1)} %get-tuple-element.35), channel_id=1, replica_groups=mesh['y'=4,'c'=2,'z'=4,'x'=4] {'z','x','c'}, dimensions={0} | all-to-all | bytes 1048576 | tf_op jit(solution)/shard_map/all_to_all | solution.py:565
  158.3 5.1 %weight_piece.1.p0 = bf16[64,1536]{1,0:T(8,128)(2,1)S(1)} custom-call(bf16[32,64,128]{2,1,0:T(8,128)(2,1)S(1)} %all_to_all.10.qg, bf16[4096,768]{1,0:T(8,128)(2,1)} %all-gather.2.cloned.1.call-done.xa, bf16[4096,768]{1,0:T(8,128)(2,1)S(1)} %collective-permute-done.17.xb), custom_call_target="tpu_custom_call" | custom-call | tf_op jit(solution)/shard_map/weight_piece/pallas_call | solution.py:567
  166.0 2.6 %collective-permute-start.20 = (bf16[64,1536]{1,0:T(8,128)(2,1)S(1)}, bf16[64,1536]{1,0:T(8,128)(2,1)S(1)}, u32[]{:S(2)}, u32[]{:S(2)}) collective-permute-start(bf16[64,1536]{1,0:T(8,128)(2,1)S(1)} %weight_piece.1.p0), channel_id=1, source_target_pairs={{0,11},{1,8},{2,9},{3,10},{4,15},{5,12},{6,13},{7,14},{8,3},{9,0},... | collective-permute-start | bytes 589832 | tf_op jit(solution)/shard_map/ppermute | solution.py:579
  168.6 4.6 %collective-permute-done.18.p1 = bf16[64,1536]{1,0:T(8,128)(2,1)S(1)} collective-permute-done((bf16[64,1536]{1,0:T(8,128)(2,1)S(1)}, bf16[64,1536]{1,0:T(8,128)(2,1)S(1)}, u32[]{:S(2)}, u32[]{:S(2)}) %collective-permute-start.18) | collective-permute-done | bytes 196640 | tf_op jit(solution)/shard_map/ppermute | solution.py:579
  174.8 2.8 %collective-permute-done.20.p3 = bf16[64,1536]{1,0:T(8,128)(2,1)S(1)} collective-permute-done((bf16[64,1536]{1,0:T(8,128)(2,1)S(1)}, bf16[64,1536]{1,0:T(8,128)(2,1)S(1)}, u32[]{:S(2)}, u32[]{:S(2)}) %collective-permute-start.20) | collective-permute-done | bytes 196640 | tf_op jit(solution)/shard_map/ppermute | solution.py:579
  180.8 2.3 %collective-permute-start.25 = (f32[8,128]{1,0:T(8,128)S(1)}, f32[8,128]{1,0:T(8,128)S(1)}, u32[]{:S(2)}, u32[]{:S(2)}) collective-permute-start(f32[8,128]{1,0:T(8,128)S(1)} %get-tuple-element.41), channel_id=1, source_target_pairs={{0,16},{16,0},{1,17},{17,1},{2,18},{18,2},{3,19},{19,3},{4,20},{20... | collective-permute-start | bytes 12296 | tf_op jit(solution)/shard_map/ppermute | solution.py:556
  183.1 2.2 %collective-permute-start.23 = (bf16[768,256]{1,0:T(8,128)(2,1)S(1)}, bf16[768,256]{1,0:T(8,128)(2,1)S(1)}, u32[]{:S(2)}, u32[]{:S(2)}) collective-permute-start(bf16[768,256]{1,0:T(8,128)(2,1)S(1)} %get-tuple-element.39), channel_id=1, source_target_pairs={{0,3},{1,0},{2,1},{3,2},{4,7},{5,4},{6,5},{7,6},{8,11},{9,8},{10,9... | collective-permute-start | bytes 1179656 | tf_op jit(solution)/shard_map/ppermute | solution.py:590
  185.9 7.9 %collective-permute-done.23.top = bf16[768,256]{1,0:T(8,128)(2,1)S(1)} collective-permute-done((bf16[768,256]{1,0:T(8,128)(2,1)S(1)}, bf16[768,256]{1,0:T(8,128)(2,1)S(1)}, u32[]{:S(2)}, u32[]{:S(2)}) %collective-permute-start.23) | collective-permute-done | bytes 393248 | tf_op jit(solution)/shard_map/ppermute | solution.py:590
  193.9 3.1 %collective-permute-done.24.bottom = bf16[768,256]{1,0:T(8,128)(2,1)S(1)} collective-permute-done((bf16[768,256]{1,0:T(8,128)(2,1)S(1)}, bf16[768,256]{1,0:T(8,128)(2,1)S(1)}, u32[]{:S(2)}, u32[]{:S(2)}) %collective-permute-start.24) | collective-permute-done | bytes 393248 | tf_op jit(solution)/shard_map/ppermute | solution.py:591
  197.1 2.8 %finish.1 = f32[1536,1024]{1,0:T(8,128)} custom-call(bf16[1536,256]{1,0:T(8,128)(2,1)S(1)} %get-tuple-element.38.own, bf16[1536,256]{1,0:T(8,128)(2,1)S(1)} %collective-permute-done.21.below, bf16[1536,256]{1,0:T(8,128)(2,1)S(1)} %collective-permute-done.22.above, bf16[768,256]{1,0:T(8,128)(2,1)S(1)} %collective-permute-done.23.top, ...), custom_call_target="tpu_custom_call" | custom-call | tf_op jit(solution)/shard_map/finish/pallas_call | solution.py:592
  (60 shorter events, 26.2 us)
Async XLA Ops:
  12.4 42.9 %all-to-all-start = ((bf16[48,176,128]{2,1,0:T(8,128)(2,1)}), bf16[48,176,128]{2,1,0:T(8,128)(2,1)}, u32[]{:S(2)}, u32[]{:S(2)}) async-start(bf16[48,176,128]{2,1,0:T(8,128)(2,1)} %pick_outgoing.1), calls=%async_computation | async-start | bytes 4325376 | tf_op jit(solution)/shard_map/all_to_all | solution.py:458
  22.2 101.2 %all-gather.2.cloned.1.call-start = ((), (), s32[]{:S(2)}) async-start(), calls=%async_computation.2 | async-start | bytes 6684672 | tf_op jit(solution)/shard_map/all_gather | solution.py:498
  25.1 2.2 %collective-permute-start = (bf16[1056,128]{1,0:T(8,128)(2,1)}, bf16[1056,128]{1,0:T(8,128)(2,1)S(1)}, u32[]{:S(2)}, u32[]{:S(2)}) collective-permute-start(bf16[1056,128]{1,0:T(8,128)(2,1)} %get-tuple-element.23), channel_id=1, source_target_pairs={{0,16},{16,0},{1,17},{17,1},{2,18},{18,2},{3,19},{19,3},{4,20},{20... | collective-permute-start | bytes 811016 | tf_op jit(solution)/shard_map/ppermute | solution.py:467
  27.4 27.8 %copy-start.5 = (s32[32,16]{0,1:T(8,128)S(1)}, s32[32,16]{0,1:T(8,128)}, u32[]{:S(2)}) copy-start(s32[32,16]{0,1:T(8,128)} %param.12) | copy-start | bytes 6148
  27.5 15.1 %collective-permute-start.1 = (bf16[2,1056,128]{2,1,0:T(8,128)(2,1)S(1)}, bf16[2,1056,128]{2,1,0:T(8,128)(2,1)S(1)}, u32[]{:S(2)}, u32[]{:S(2)}) collective-permute-start(bf16[2,1056,128]{2,1,0:T(8,128)(2,1)S(1)} %pad_maximum_fusion.iq0.iq), channel_id=1, source_target_pairs={{0,32},{32,64},{64,96},{96,0},{1,33},{33,65},{65,97},{97,1},{2,34}... | collective-permute-start | bytes 1622024 | tf_op jit(solution)/shard_map/ppermute | solution.py:440
  28.9 26.3 %collective-permute-start.2 = (bf16[2,1056,128]{2,1,0:T(8,128)(2,1)S(1)}, bf16[2,1056,128]{2,1,0:T(8,128)(2,1)}, u32[]{:S(2)}, u32[]{:S(2)}) collective-permute-start(bf16[2,1056,128]{2,1,0:T(8,128)(2,1)S(1)} %pad_maximum_fusion.iq0.iq), channel_id=1, source_target_pairs={{0,64},{32,96},{64,0},{96,32},{1,65},{33,97},{65,1},{97,33},{2,66}... | collective-permute-start | bytes 1622024 | tf_op jit(solution)/shard_map/ppermute | solution.py:440
  31.5 23.7 %collective-permute-start.3 = (bf16[2,1056,128]{2,1,0:T(8,128)(2,1)S(1)}, bf16[2,1056,128]{2,1,0:T(8,128)(2,1)}, u32[]{:S(2)}, u32[]{:S(2)}) collective-permute-start(bf16[2,1056,128]{2,1,0:T(8,128)(2,1)S(1)} %pad_maximum_fusion.iq0.iq), channel_id=1, source_target_pairs={{0,96},{32,0},{64,32},{96,64},{1,97},{33,1},{65,33},{97,65},{2,98}... | collective-permute-start | bytes 1622024 | tf_op jit(solution)/shard_map/ppermute | solution.py:440
  36.3 49.8 %copy-start.7 = (s32[32]{0:T(128)S(1)}, s32[32]{0:T(128)}, u32[]{:S(2)}) copy-start(s32[32]{0:T(128)} %counts.3) | copy-start | bytes 388
  58.0 34.6 %collective-permute-start.10 = (bf16[16,576,128]{2,1,0:T(8,128)(2,1)S(1)}, bf16[16,576,128]{2,1,0:T(8,128)(2,1)S(1)}, u32[]{:S(2)}, u32[]{:S(2)}) collective-permute-start(bf16[16,576,128]{2,1,0:T(8,128)(2,1)S(1)} %dynamic-slice_bitcast_fusion.refs_0_), channel_id=1, source_target_pairs={{0,16},{16,0},{1,17},{17,1},{2,18},{18,2},{3,19},{19,3},{4,20},{20... | collective-permute-start | bytes 7077896 | tf_op jit(solution)/shard_map/ppermute | solution.py:476
  59.3 11.4 %collective-permute-start.4 = (bf16[8,176,128]{2,1,0:T(8,128)(2,1)}, bf16[8,176,128]{2,1,0:T(8,128)(2,1)S(1)}, u32[]{:S(2)}, u32[]{:S(2)}) collective-permute-start(bf16[8,176,128]{2,1,0:T(8,128)(2,1)} %get-tuple-element.24.own_low), channel_id=1, source_target_pairs={{0,32},{32,64},{64,96},{96,0},{1,33},{33,65},{65,97},{97,1},{2,34}... | collective-permute-start | bytes 1081352 | tf_op jit(solution)/shard_map/ppermute | solution.py:490
  60.2 10.4 %collective-permute-start.7 = (bf16[8,176,128]{2,1,0:T(8,128)(2,1)}, bf16[8,176,128]{2,1,0:T(8,128)(2,1)S(1)}, u32[]{:S(2)}, u32[]{:S(2)}) collective-permute-start(bf16[8,176,128]{2,1,0:T(8,128)(2,1)} %get-tuple-element.25.own_high), channel_id=1, source_target_pairs={{0,96},{32,0},{64,32},{96,64},{1,97},{33,1},{65,33},{97,65},{2,98}... | collective-permute-start | bytes 1081352 | tf_op jit(solution)/shard_map/ppermute | solution.py:490
  62.0 16.4 %collective-permute-start.5 = (bf16[8,176,128]{2,1,0:T(8,128)(2,1)}, bf16[8,176,128]{2,1,0:T(8,128)(2,1)S(1)}, u32[]{:S(2)}, u32[]{:S(2)}) collective-permute-start(bf16[8,176,128]{2,1,0:T(8,128)(2,1)} %get-tuple-element.25.own_high), channel_id=1, source_target_pairs={{0,32},{32,64},{64,96},{96,0},{1,33},{33,65},{65,97},{97,1},{2,34}... | collective-permute-start | bytes 1081352 | tf_op jit(solution)/shard_map/ppermute | solution.py:491
  62.0 16.4 %collective-permute-start.9 = (bf16[8,176,128]{2,1,0:T(8,128)(2,1)}, bf16[8,176,128]{2,1,0:T(8,128)(2,1)S(1)}, u32[]{:S(2)}, u32[]{:S(2)}) collective-permute-start(bf16[8,176,128]{2,1,0:T(8,128)(2,1)} %get-tuple-element.24.own_low), channel_id=1, source_target_pairs={{0,96},{32,0},{64,32},{96,64},{1,97},{33,1},{65,33},{97,65},{2,98}... | collective-permute-start | bytes 1081352 | tf_op jit(solution)/shard_map/ppermute | solution.py:491
  70.7 15.4 %collective-permute-start.6 = (bf16[8,176,128]{2,1,0:T(8,128)(2,1)S(1)}, bf16[8,176,128]{2,1,0:T(8,128)(2,1)S(1)}, u32[]{:S(2)}, u32[]{:S(2)}) collective-permute-start(bf16[8,176,128]{2,1,0:T(8,128)(2,1)S(1)} %collective-permute-done.4.a1), channel_id=1, source_target_pairs={{0,32},{32,64},{64,96},{96,0},{1,33},{33,65},{65,97},{97,1},{2,34}... | collective-permute-start | bytes 1081352 | tf_op jit(solution)/shard_map/ppermute | solution.py:492
  70.7 15.4 %collective-permute-start.8 = (bf16[8,176,128]{2,1,0:T(8,128)(2,1)S(1)}, bf16[8,176,128]{2,1,0:T(8,128)(2,1)S(1)}, u32[]{:S(2)}, u32[]{:S(2)}) collective-permute-start(bf16[8,176,128]{2,1,0:T(8,128)(2,1)S(1)} %collective-permute-done.7.b3), channel_id=1, source_target_pairs={{0,96},{32,0},{64,32},{96,64},{1,97},{33,1},{65,33},{97,65},{2,98}... | collective-permute-start | bytes 1081352 | tf_op jit(solution)/shard_map/ppermute | solution.py:492
  92.6 42.5 %copy-start.2 = (bf16[128,2048]{1,0:T(8,128)(2,1)S(1)}, bf16[128,2048]{1,0:T(8,128)(2,1)}, u32[]{:S(2)}) copy-start(bf16[128,2048]{1,0:T(8,128)(2,1)} %get-tuple-element.33.keys) | copy-start | bytes 1572868
  92.6 42.5 %copy-start.3 = (bf16[2048,128]{1,0:T(8,128)(2,1)S(1)}, bf16[2048,128]{1,0:T(8,128)(2,1)}, u32[]{:S(2)}) copy-start(bf16[2048,128]{1,0:T(8,128)(2,1)} %get-tuple-element.34.keys_t) | copy-start | bytes 1572868
  113.9 5.6 %collective-permute-start.11 = (bf16[528,128]{1,0:T(8,128)(2,1)S(1)}, bf16[528,128]{1,0:T(8,128)(2,1)S(1)}, u32[]{:S(2)}, u32[]{:S(2)}) collective-permute-start(bf16[528,128]{1,0:T(8,128)(2,1)S(1)} %get-tuple-element.29), channel_id=1, source_target_pairs={{0,32},{32,64},{64,96},{96,0},{1,33},{33,65},{65,97},{97,1},{2,34}... | collective-permute-start | bytes 405512 | tf_op jit(solution)/shard_map/ppermute | solution.py:535
  115.0 7.6 %collective-permute-start.12 = (bf16[528,128]{1,0:T(8,128)(2,1)S(1)}, bf16[528,128]{1,0:T(8,128)(2,1)S(1)}, u32[]{:S(2)}, u32[]{:S(2)}) collective-permute-start(bf16[528,128]{1,0:T(8,128)(2,1)S(1)} %get-tuple-element.30), channel_id=1, source_target_pairs={{0,64},{32,96},{64,0},{96,32},{1,65},{33,97},{65,1},{97,33},{2,66}... | collective-permute-start | bytes 405512 | tf_op jit(solution)/shard_map/ppermute | solution.py:535
  117.5 5.6 %collective-permute-start.13 = (bf16[528,128]{1,0:T(8,128)(2,1)S(1)}, bf16[528,128]{1,0:T(8,128)(2,1)S(1)}, u32[]{:S(2)}, u32[]{:S(2)}) collective-permute-start(bf16[528,128]{1,0:T(8,128)(2,1)S(1)} %get-tuple-element.31), channel_id=1, source_target_pairs={{0,96},{32,0},{64,32},{96,64},{1,97},{33,1},{65,33},{97,65},{2,98}... | collective-permute-start | bytes 405512 | tf_op jit(solution)/shard_map/ppermute | solution.py:535
  123.3 35.0 %collective-permute-start.17 = (bf16[4096,768]{1,0:T(8,128)(2,1)}, bf16[4096,768]{1,0:T(8,128)(2,1)S(1)}, u32[]{:S(2)}, u32[]{:S(2)}) collective-permute-start(bf16[4096,768]{1,0:T(8,128)(2,1)} %all-gather.2.cloned.1.call-done.xa), channel_id=1, source_target_pairs={{0,16},{16,0},{1,17},{17,1},{2,18},{18,2},{3,19},{19,3},{4,20},{20... | collective-permute-start | bytes 18874376 | tf_op jit(solution)/shard_map/ppermute | solution.py:545
  125.2 6.4 %collective-permute-start.14 = (bf16[528,128]{1,0:T(8,128)(2,1)S(1)}, bf16[528,128]{1,0:T(8,128)(2,1)S(1)}, u32[]{:S(2)}, u32[]{:S(2)}) collective-permute-start(bf16[528,128]{1,0:T(8,128)(2,1)S(1)} %loss.1.g0), channel_id=1, source_target_pairs={{0,32},{32,64},{64,96},{96,0},{1,33},{33,65},{65,97},{97,1},{2,34}... | collective-permute-start | bytes 405512 | tf_op jit(solution)/shard_map/ppermute | solution.py:440
  126.4 8.7 %collective-permute-start.15 = (bf16[528,128]{1,0:T(8,128)(2,1)S(1)}, bf16[528,128]{1,0:T(8,128)(2,1)S(1)}, u32[]{:S(2)}, u32[]{:S(2)}) collective-permute-start(bf16[528,128]{1,0:T(8,128)(2,1)S(1)} %loss.1.g0), channel_id=1, source_target_pairs={{0,64},{32,96},{64,0},{96,32},{1,65},{33,97},{65,1},{97,33},{2,66}... | collective-permute-start | bytes 405512 | tf_op jit(solution)/shard_map/ppermute | solution.py:440
  128.6 6.6 %collective-permute-start.16 = (bf16[528,128]{1,0:T(8,128)(2,1)S(1)}, bf16[528,128]{1,0:T(8,128)(2,1)S(1)}, u32[]{:S(2)}, u32[]{:S(2)}) collective-permute-start(bf16[528,128]{1,0:T(8,128)(2,1)S(1)} %loss.1.g0), channel_id=1, source_target_pairs={{0,96},{32,0},{64,32},{96,64},{1,97},{33,1},{65,33},{97,65},{2,98}... | collective-permute-start | bytes 405512 | tf_op jit(solution)/shard_map/ppermute | solution.py:440
  163.5 9.7 %collective-permute-start.18 = (bf16[64,1536]{1,0:T(8,128)(2,1)S(1)}, bf16[64,1536]{1,0:T(8,128)(2,1)S(1)}, u32[]{:S(2)}, u32[]{:S(2)}) collective-permute-start(bf16[64,1536]{1,0:T(8,128)(2,1)S(1)} %weight_piece.1.p0), channel_id=1, source_target_pairs={{0,9},{1,10},{2,11},{3,8},{4,13},{5,14},{6,15},{7,12},{8,1},{9,2},... | collective-permute-start | bytes 589832 | tf_op jit(solution)/shard_map/ppermute | solution.py:579
  164.9 9.9 %collective-permute-start.19 = (bf16[64,1536]{1,0:T(8,128)(2,1)S(1)}, bf16[64,1536]{1,0:T(8,128)(2,1)S(1)}, u32[]{:S(2)}, u32[]{:S(2)}) collective-permute-start(bf16[64,1536]{1,0:T(8,128)(2,1)S(1)} %weight_piece.1.p0), channel_id=1, source_target_pairs={{0,2},{1,3},{2,0},{3,1},{4,6},{5,7},{6,4},{7,5},{8,10},{9,11},{10,... | collective-permute-start | bytes 589832 | tf_op jit(solution)/shard_map/ppermute | solution.py:579
  166.0 11.7 %collective-permute-start.20 = (bf16[64,1536]{1,0:T(8,128)(2,1)S(1)}, bf16[64,1536]{1,0:T(8,128)(2,1)S(1)}, u32[]{:S(2)}, u32[]{:S(2)}) collective-permute-start(bf16[64,1536]{1,0:T(8,128)(2,1)S(1)} %weight_piece.1.p0), channel_id=1, source_target_pairs={{0,11},{1,8},{2,9},{3,10},{4,15},{5,12},{6,13},{7,14},{8,3},{9,0},... | collective-permute-start | bytes 589832 | tf_op jit(solution)/shard_map/ppermute | solution.py:579
  178.0 18.9 %collective-permute-start.21 = (bf16[1536,256]{1,0:T(8,128)(2,1)S(1)}, bf16[1536,256]{1,0:T(8,128)(2,1)S(1)}, u32[]{:S(2)}, u32[]{:S(2)}) collective-permute-start(bf16[1536,256]{1,0:T(8,128)(2,1)S(1)} %get-tuple-element.38.own), channel_id=1, source_target_pairs={{0,4},{1,5},{2,6},{3,7},{4,8},{5,9},{6,10},{7,11},{8,12},{9,13},{1... | collective-permute-start | bytes 2359304 | tf_op jit(solution)/shard_map/ppermute | solution.py:588
  179.1 18.0 %collective-permute-start.22 = (bf16[1536,256]{1,0:T(8,128)(2,1)S(1)}, bf16[1536,256]{1,0:T(8,128)(2,1)S(1)}, u32[]{:S(2)}, u32[]{:S(2)}) collective-permute-start(bf16[1536,256]{1,0:T(8,128)(2,1)S(1)} %get-tuple-element.38.own), channel_id=1, source_target_pairs={{0,12},{1,13},{2,14},{3,15},{4,0},{5,1},{6,2},{7,3},{8,4},{9,5},{1... | collective-permute-start | bytes 2359304 | tf_op jit(solution)/shard_map/ppermute | solution.py:589
  180.8 4.5 %collective-permute-start.25 = (f32[8,128]{1,0:T(8,128)S(1)}, f32[8,128]{1,0:T(8,128)S(1)}, u32[]{:S(2)}, u32[]{:S(2)}) collective-permute-start(f32[8,128]{1,0:T(8,128)S(1)} %get-tuple-element.41), channel_id=1, source_target_pairs={{0,16},{16,0},{1,17},{17,1},{2,18},{18,2},{3,19},{19,3},{4,20},{20... | collective-permute-start | bytes 12296 | tf_op jit(solution)/shard_map/ppermute | solution.py:556
  183.1 10.7 %collective-permute-start.23 = (bf16[768,256]{1,0:T(8,128)(2,1)S(1)}, bf16[768,256]{1,0:T(8,128)(2,1)S(1)}, u32[]{:S(2)}, u32[]{:S(2)}) collective-permute-start(bf16[768,256]{1,0:T(8,128)(2,1)S(1)} %get-tuple-element.39), channel_id=1, source_target_pairs={{0,3},{1,0},{2,1},{3,2},{4,7},{5,4},{6,5},{7,6},{8,11},{9,8},{10,9... | collective-permute-start | bytes 1179656 | tf_op jit(solution)/shard_map/ppermute | solution.py:590
  185.3 11.6 %collective-permute-start.24 = (bf16[768,256]{1,0:T(8,128)(2,1)S(1)}, bf16[768,256]{1,0:T(8,128)(2,1)S(1)}, u32[]{:S(2)}, u32[]{:S(2)}) collective-permute-start(bf16[768,256]{1,0:T(8,128)(2,1)S(1)} %get-tuple-element.40), channel_id=1, source_target_pairs={{0,1},{1,2},{2,3},{3,0},{4,5},{5,6},{6,7},{7,4},{8,9},{9,10},{10,1... | collective-permute-start | bytes 1179656 | tf_op jit(solution)/shard_map/ppermute | solution.py:591
  (4 other events, 21.6 us)
Sparse Core Ops, SparseCore 0:
  58.1 63.0 all-gather.1

commit v6 on v5

--- a/solution.py
+++ b/solution.py
@@ -43,7 +43,7 @@
 HBM = pl.BlockSpec(memory_space=pltpu.HBM)
 
 
-def call(kernel, out_shape, in_specs, out_specs, scratch=(), name=None):
+def call(kernel, out_shape, in_specs, out_specs, scratch=(), name=None, aliases=None):
     return pl.pallas_call(
         kernel,
         out_shape=out_shape,
@@ -52,6 +52,7 @@
         scratch_shapes=list(scratch),
         compiler_params=pltpu.CompilerParams(vmem_limit_bytes=VMEM_LIMIT),
         name=name,
+        input_output_aliases=aliases or {},
     )
 
 
@@ -165,7 +166,8 @@
     return tail[0:8] + tail[8:16] + tail[16:24]
 
 
-def logits_kernel(counts, own_low, own_high, a1, b1, a2, b2, a3, b3, iq0, iq1, iq2, iq3, *rest):
+def logits_kernel(counts, own_low, own_high, a1, b1, a2, b2, a3, b3, *refs):
+    iq_refs, rest = refs[:8], refs[8:]
     logits_ref, stats_ref, latent_t, keys_out, keys_t_out, index_t, keys, total, own, sems = rest
     y, count = lax.axis_index("y"), slots_in_use(counts)
     half = SEL // 2
@@ -191,10 +193,9 @@
         index_t[span, :] = keys[DK:, span].T
     copies.append(pltpu.make_async_copy(index_t, keys_t_out, sems.at[1]))
     copies[1].start()
-    iq_refs = (iq0, iq1, iq2, iq3)
     keys_t = index_t[pl.ds(pl.multiple_of(y * OWNK, OWNK), OWNK), :]
     total[...] = jnp.zeros_like(total)
-    for ref in [r.at[n] for r in iq_refs for n in range(2)]:
+    for ref in iq_refs:
         rows = head_rows(ref[HALF_COLS:, :])
         for p in range(4):
             a, b = 2 * p, 2 * p + 1
@@ -333,7 +334,7 @@
     out[OWNK:, :] = tail_tile(split_rows(entropy))
 
 
-def backward_kernel(g0, g1, g2, g3, keys, keys_t, iq, out, entropy_ref, grads):
+def backward_kernel(g0, g1, g2, g3, keys, keys_t, iq_first, iq_second, out, entropy_ref, grads):
     y = lax.axis_index("y")
     entropy = jnp.zeros((1, BLK), F32)
     for s, piece in enumerate((g0, g1, g2, g3)):
@@ -343,8 +344,7 @@
         entropy = entropy + tail[0:1] + tail[1:2] + tail[2:3]
     entropy_ref[...] = jnp.broadcast_to(entropy, (8, BLK))
     chunk = 512
-    for core in range(2):
-        ref = iq.at[core]
+    for core, ref in enumerate((iq_first, iq_second)):
         rows = head_rows(ref[HALF_COLS:, :])
         for p in range(4):
             a, b = 2 * p, 2 * p + 1
@@ -406,15 +406,16 @@
         half[k % 3 * 256 : (k % 3 + 1) * 256, :] = tile
 
 
-def finish_kernel(own, below, above, top, bottom, out, wide, sems):
+def finish_kernel(shifts, *refs):
+    pieces, (out, wide, sems) = refs[:-3], refs[-3:]
     colour = lax.rem(lax.axis_index("z") + 2 * lax.axis_index("x"), 4)
-    half = DQ // 2
-    copies = []
-    for n, (shift, pieces) in enumerate(
-        ((0, (own,)), (2, (top, bottom)), (3, (below,)), (1, (above,)))
-    ):
-        for m, piece in enumerate(pieces):
-            wide[n, m * half : m * half + piece.shape[0], :] = piece[...].astype(F32)
+    copies, at = [], 0
+    for n, shift in enumerate(shifts):
+        row = 0
+        while row < DQ:
+            piece = pieces[at]
+            wide[n, row : row + piece.shape[0], :] = piece[...].astype(F32)
+            row, at = row + piece.shape[0], at + 1
         lanes = pl.multiple_of(lax.rem(colour + shift, 4) * 256, 256)
         copies.append(pltpu.make_async_copy(wide.at[n], out.at[:, pl.ds(lanes, 256)], sems.at[n]))
         copies[-1].start()
@@ -422,6 +423,11 @@
         c.wait()
 
 
+def finish_rest_kernel(started, *refs):
+    del started
+    finish_kernel((3, 1), *refs)
+
+
 def plane(dz, dx):
     return [
         (z * 4 + x, (z + dz) % 4 * 4 + (x + dx) % 4) for z in range(4) for x in range(4)
@@ -434,6 +440,13 @@
 
 SWAP = [(0, 1), (1, 0)]
 SHIFTS = (1, 3, 2)
+
+
+def relayed(low, high):
+    low_up, high_down = lax.ppermute(low, "y", ring(1)), lax.ppermute(high, "y", ring(3))
+    high_up, low_down = lax.ppermute(high, "y", ring(1)), lax.ppermute(low, "y", ring(3))
+    low_far, high_far = lax.ppermute(low_up, "y", ring(1)), lax.ppermute(high_down, "y", ring(3))
+    return low_up, high_up, low_far, high_far, low_down, high_down
 
 
 def around_y(array):
@@ -466,10 +479,8 @@
     )(index_input, index_weight, head_weights.T)
     iq_other = lax.ppermute(iq_send, "c", SWAP)
     first = core == 0
-    iq_pair = jnp.stack(
-        [jnp.where(first, iq_own, iq_other), jnp.where(first, iq_other, iq_own)]
-    )
-    iq_all = around_y(iq_pair)
+    iq_pair = (jnp.where(first, iq_own, iq_other), jnp.where(first, iq_other, iq_own))
+    iq_moved = relayed(*iq_pair)
 
     q_t = jnp.transpose(q_absorbed, (1, 2, 0))
     q_send = lax.dynamic_slice_in_dim(q_t, (1 - core) * BLK, BLK, 2)
@@ -478,7 +489,7 @@
     low, high = call(
         pick_listed_kernel,
         (pltpu.HBM((SEL // 2, PIECE, BLK), BF16),) * 2,
-        [SMEM] + [ANY] * 5,
+        [SMEM] + [ANY] * 8,
         (HBM, HBM),
         [
             pltpu.VMEM((SEL, PIECE, BLK), BF16),
@@ -486,11 +497,8 @@
             pltpu.SemaphoreType.DMA((2,)),
         ],
         "pick_listed",
-    )(ids, arrived, q_send, *iq_all[1:])
-    low_up, high_down = lax.ppermute(low, "y", ring(1)), lax.ppermute(high, "y", ring(3))
-    high_up, low_down = lax.ppermute(high, "y", ring(1)), lax.ppermute(low, "y", ring(3))
-    low_far, high_far = lax.ppermute(low_up, "y", ring(1)), lax.ppermute(high_down, "y", ring(3))
-    moved = (low_up, high_up, low_far, high_far, low_down, high_down)
+    )(ids, arrived, q_send, *iq_moved)
+    moved = relayed(low, high)
 
     half = DQ // 2
     x_half = lax.dynamic_slice_in_dim(index_input, core * half, half, 1)
@@ -506,7 +514,7 @@
             pltpu.HBM((ID, KEYS), BF16),
             pltpu.HBM((KEYS, ID), BF16),
         ),
-        [SMEM, ANY, ANY] + [VMEM] * 10,
+        [SMEM, ANY, ANY] + [VMEM] * 14,
         (VMEM, VMEM, VMEM, HBM, HBM),
         [
             pltpu.VMEM((KEYS, ID), BF16),
@@ -516,7 +524,7 @@
             pltpu.SemaphoreType.DMA((4,)),
         ],
         "index_logits",
-    )(block_counts, in_hbm(low), in_hbm(high), *map(in_vmem, (*moved, *iq_all)))
+    )(block_counts, in_hbm(low), in_hbm(high), *map(in_vmem, (*moved, *iq_pair, *iq_moved)))
 
     targets = call(
         target_kernel,
@@ -548,11 +556,11 @@
     query_grad, entropy = call(
         backward_kernel,
         (shape((2 * NQ, COLS, BLK), BF16), shape((8, BLK), F32)),
-        [VMEM] * 7,
+        [VMEM] * 8,
         (VMEM, VMEM),
         [pltpu.VMEM((KEYS, BLK), F32)],
         "index_backward",
-    )(*map(in_vmem, (*grads_all, index_keys, index_t, iq_pair)))
+    )(*map(in_vmem, (*grads_all, index_keys, index_t, *iq_pair)))
     entropy_other = lax.ppermute(entropy, "c", SWAP)
     entropy_both = jnp.where(
         first,
@@ -589,14 +597,24 @@
     above = lax.ppermute(full, qblk, plane(-1, 0))
     top = lax.ppermute(top, qblk, plane(0, -1))
     bottom = lax.ppermute(bottom, qblk, plane(0, 1))
+    wide = [pltpu.VMEM((2, DQ, 256), F32), pltpu.SemaphoreType.DMA((2,))]
+    started = call(
+        functools.partial(finish_kernel, (0, 2)),
+        pltpu.HBM((DQ, HALF_COLS), F32),
+        [VMEM] * 3,
+        HBM,
+        wide,
+        "finish_first",
+    )(*map(in_vmem, (full, top, bottom)))
     weight_grad = call(
-        finish_kernel,
-        shape((DQ, HALF_COLS), F32),
-        [VMEM] * 5,
-        ANY,
-        [pltpu.VMEM((4, DQ, 256), F32), pltpu.SemaphoreType.DMA((4,))],
-        "finish",
-    )(*map(in_vmem, (full, below, above, top, bottom)))
+        finish_rest_kernel,
+        pltpu.HBM((DQ, HALF_COLS), F32),
+        [HBM, VMEM, VMEM],
+        HBM,
+        wide,
+        "finish_rest",
+        {0: 0},
+    )(in_hbm(started), in_vmem(below), in_vmem(above))
     return weight_grad, entropy_mine
 
 

time: 209 us -> 204 us (0.976)
  waiting for transfers between devices: 70.5 us -> 65.4 us
  starting transfers between devices: 47.5 us -> 52 us
  blocking collectives: 19.4 us -> 15.9 us
    ppermute x6 -> x3, waiting for transfers between devices: 25 us -> 6.02 us  [around_y(): moved = {s: lax.ppermute(array, 'y', ring(s)) for s in SHIFTS}]
    ppermute x6 -> x12, waiting for transfers between devices: 18.8 us -> 27.9 us  [the longest x2 12.9 us: relayed(): lax.ppermute(low_up, 'y', ring(1))]
    ppermute x6 -> x12, starting transfers between devices: 8.04 us -> 16.5 us  [the longest x2 5.18 us: relayed(): lax.ppermute(high_down, 'y', ring(3))]
    all_to_all x1, waiting for transfers between devices: 0.01 us -> 5.27 us  [on_device(): lax.all_to_all(outgoing, ('z', 'x'), split_axis=0, concat_axis=0, tiled=T...]
    ppermute x6 -> x3, starting transfers between devices: 9.05 us -> 3.86 us  [around_y(): moved = {s: lax.ppermute(array, 'y', ring(s)) for s in SHIFTS}]
    all_to_all x1, blocking collectives: 19.4 us -> 15.9 us  [on_device(): lax.all_to_all(query_grad, ('z', 'x', 'c'), split_axis=0, concat_axis=0,...]
  transfers between devices with their start and end apart: 28 -> 31, of which waited for: 17 -> 17; matrix products, arithmetic and copies ran while one was open for 2% -> 2% of each run, Pallas kernels for 16% -> 18%
where the time goes in v6:
time: 204 us
  waiting for transfers between devices  65.4 us (32%)
  starting transfers between devices  52 us (25%)
  Pallas kernels  50.1 us (25%)
  blocking collectives  15.9 us (8%)
  between operations  14.3 us (7%)
  local copies, waits for them, and re-layouts  6.05 us (3%)
    pallas_call x1, Pallas kernels, on_device(): call(target_kernel, (shape((LG_ROWS, BLK), BF16),) * 4, [SMEM, VMEM, VMEM...  21.7 us
    all_to_all x1, blocking collectives, on_device(): lax.all_to_all(query_grad, ('z', 'x', 'c'), split_axis=0, concat_axis=0,...  15.9 us
    ppermute x2, waiting for transfers between devices, relayed(): lax.ppermute(low_up, 'y', ring(1))  12.9 us
    ppermute x2, waiting for transfers between devices, relayed(): lax.ppermute(low, 'y', ring(1))  9.89 us
    all_to_all x1, starting transfers between devices, on_device(): lax.all_to_all(outgoing, ('z', 'x'), split_axis=0, concat_axis=0, tiled=T...  9.87 us
    ppermute x3, waiting for transfers between devices, on_device(): lax.ppermute(piece, qblk, plane(-2 * d, d))  9.07 us
    ppermute x1, waiting for transfers between devices, on_device(): top = lax.ppermute(top, qblk, plane(0, -1))  7.93 us
    pallas_call x1, Pallas kernels, on_device(): call(logits_kernel, (shape((OWNK, BLK), F32), shape((8, BLK), F32), shape...  6.43 us
  transfers between devices with their start and end apart: 31, of which 17 were waited for; matrix products, arithmetic and copies ran while one was open for 2% of the time, Pallas kernels for 18%

profile of v6, /device:TPU:1, one launch (start us, length us, event | category | flops | bytes accessed | tf_op | source)
XLA Modules:
  0.0 203.7 jit_solution(12140192903913097580)
XLA Ops:
  7.9 4.4 %pick_outgoing.1 = bf16[48,176,128]{2,1,0:T(8,128)(2,1)} custom-call(s32[16,32]{1,0:T(8,128)S(1)} %bitcast.9, bf16[32,704,128]{2,1,0:T(8,128)(2,1)} %cache.1), custom_call_target="tpu_custom_call" | custom-call | tf_op jit(solution)/shard_map/pick_outgoing/pallas_call | solution.py:463
  12.3 9.9 %all-to-all-start = ((bf16[48,176,128]{2,1,0:T(8,128)(2,1)}), bf16[48,176,128]{2,1,0:T(8,128)(2,1)}, u32[]{:S(2)}, u32[]{:S(2)}) async-start(bf16[48,176,128]{2,1,0:T(8,128)(2,1)} %pick_outgoing.1), calls=%async_computation | async-start | bytes 4325376 | tf_op jit(solution)/shard_map/all_to_all | solution.py:471
  30.6 2.7 %collective-permute-start.6 = (bf16[1056,128]{1,0:T(8,128)(2,1)S(1)}, bf16[1056,128]{1,0:T(8,128)(2,1)}, u32[]{:S(2)}, u32[]{:S(2)}) collective-permute-start(bf16[1056,128]{1,0:T(8,128)(2,1)S(1)} %get-tuple-element.43.refs_0_.iq_first), channel_id=1, source_target_pairs={{0,96},{32,0},{64,32},{96,64},{1,97},{33,1},{65,33},{97,65},{2,98}... | collective-permute-start | bytes 811016 | tf_op jit(solution)/shard_map/ppermute | solution.py:447
  33.3 3.9 %collective-permute-done.1.refs_1_.refs_2_ = bf16[1056,128]{1,0:T(8,128)(2,1)S(1)} collective-permute-done((bf16[1056,128]{1,0:T(8,128)(2,1)S(1)}, bf16[1056,128]{1,0:T(8,128)(2,1)S(1)}, u32[]{:S(2)}, u32[]{:S(2)}) %collective-permute-start.1) | collective-permute-done | bytes 270368 | tf_op jit(solution)/shard_map/ppermute | solution.py:446
  37.2 2.7 %collective-permute-start.5 = (bf16[1056,128]{1,0:T(8,128)(2,1)S(1)}, bf16[1056,128]{1,0:T(8,128)(2,1)}, u32[]{:S(2)}, u32[]{:S(2)}) collective-permute-start(bf16[1056,128]{1,0:T(8,128)(2,1)S(1)} %collective-permute-done.4.refs_6_.refs_7_), channel_id=1, source_target_pairs={{0,96},{32,0},{64,32},{96,64},{1,97},{33,1},{65,33},{97,65},{2,98}... | collective-permute-start | bytes 811016 | tf_op jit(solution)/shard_map/ppermute | solution.py:448
  43.5 5.3 %collective-permute-done.3.refs_3_.refs_4_ = bf16[1056,128]{1,0:T(8,128)(2,1)} collective-permute-done((bf16[1056,128]{1,0:T(8,128)(2,1)S(1)}, bf16[1056,128]{1,0:T(8,128)(2,1)}, u32[]{:S(2)}, u32[]{:S(2)}) %collective-permute-start.3) | collective-permute-done | bytes 270368 | tf_op jit(solution)/shard_map/ppermute | solution.py:448
  48.7 5.3 %all-to-all-done.arrived = bf16[48,176,128]{2,1,0:T(8,128)(2,1)} async-done(((bf16[48,176,128]{2,1,0:T(8,128)(2,1)}), bf16[48,176,128]{2,1,0:T(8,128)(2,1)}, u32[]{:S(2)}, u32[]{:S(2)}) %all-to-all-start) | async-done | bytes 2162720 | tf_op jit(solution)/shard_map/all_to_all | solution.py:471
  54.0 2.7 %pick_listed.1 = (bf16[8,176,128]{2,1,0:T(8,128)(2,1)}, bf16[8,176,128]{2,1,0:T(8,128)(2,1)}) custom-call(s32[16,32]{1,0:T(8,128)S(1)} %bitcast.10, bf16[48,176,128]{2,1,0:T(8,128)(2,1)} %all-to-all-done.arrived, bf16[16,576,128]{2,1,0:T(8,128)(2,1)S(1)} %dynamic-slice_bitcast_fusion.refs_0_, bf16[1056,128]{1,0:T(8,128)(2,1)S(1)} %collective-permute-done.1.refs_1_.refs_2_, ...), custom_call_target="tpu_custom_call" | custom-call | tf_op jit(solution)/shard_map/pick_listed/pallas_call | solution.py:489
  56.8 1.9 collective-permute-start.13
  61.5 2.5 %collective-permute-start.12 = (bf16[8,176,128]{2,1,0:T(8,128)(2,1)}, bf16[8,176,128]{2,1,0:T(8,128)(2,1)S(1)}, u32[]{:S(2)}, u32[]{:S(2)}) collective-permute-start(bf16[8,176,128]{2,1,0:T(8,128)(2,1)} %get-tuple-element.24.own_low), channel_id=1, source_target_pairs={{0,96},{32,0},{64,32},{96,64},{1,97},{33,1},{65,33},{97,65},{2,98}... | collective-permute-start | bytes 1081352 | tf_op jit(solution)/shard_map/ppermute | solution.py:447
  64.0 6.0 %collective-permute-done.7.a1 = bf16[8,176,128]{2,1,0:T(8,128)(2,1)S(1)} collective-permute-done((bf16[8,176,128]{2,1,0:T(8,128)(2,1)}, bf16[8,176,128]{2,1,0:T(8,128)(2,1)S(1)}, u32[]{:S(2)}, u32[]{:S(2)}) %collective-permute-start.7) | collective-permute-done | bytes 360480 | tf_op jit(solution)/shard_map/ppermute | solution.py:446
  70.3 2.5 %collective-permute-start.11 = (bf16[8,176,128]{2,1,0:T(8,128)(2,1)S(1)}, bf16[8,176,128]{2,1,0:T(8,128)(2,1)S(1)}, u32[]{:S(2)}, u32[]{:S(2)}) collective-permute-start(bf16[8,176,128]{2,1,0:T(8,128)(2,1)S(1)} %collective-permute-done.10.b3), channel_id=1, source_target_pairs={{0,96},{32,0},{64,32},{96,64},{1,97},{33,1},{65,33},{97,65},{2,98}... | collective-permute-start | bytes 1081352 | tf_op jit(solution)/shard_map/ppermute | solution.py:448
  72.8 5.1 %collective-permute-done.8.b1 = bf16[8,176,128]{2,1,0:T(8,128)(2,1)S(1)} collective-permute-done((bf16[8,176,128]{2,1,0:T(8,128)(2,1)}, bf16[8,176,128]{2,1,0:T(8,128)(2,1)S(1)}, u32[]{:S(2)}, u32[]{:S(2)}) %collective-permute-start.8) | collective-permute-done | bytes 360480 | tf_op jit(solution)/shard_map/ppermute | solution.py:447
  77.9 7.6 %collective-permute-done.9.a2 = bf16[8,176,128]{2,1,0:T(8,128)(2,1)S(1)} collective-permute-done((bf16[8,176,128]{2,1,0:T(8,128)(2,1)S(1)}, bf16[8,176,128]{2,1,0:T(8,128)(2,1)S(1)}, u32[]{:S(2)}, u32[]{:S(2)}) %collective-permute-start.9) | collective-permute-done | bytes 360480 | tf_op jit(solution)/shard_map/ppermute | solution.py:448
  85.5 6.4 %index_logits.1 = (f32[512,128]{1,0:T(8,128)S(1)}, f32[8,128]{1,0:T(8,128)S(1)}, bf16[2048,576]{1,0:T(8,128)(2,1)S(1)}, bf16[128,2048]{1,0:T(8,128)(2,1)}, bf16[2048,128]{1,0:T(8,128)(2,1)}) custom-call(s32[32]{0:T(128)S(1)} %copy-done.7, bf16[8,176,128]{2,1,0:T(8,128)(2,1)} %get-tuple-element.24.own_low, bf16[8,176,128]{2,1,0:T(8,128)(2,1)} %get-tuple-element.25.own_high, ...), custom_call_target="tpu_custom_call" | custom-call | tf_op jit(solution)/shard_map/index_logits/pallas_call | solution.py:508
  92.0 21.7 %attention_target.1 = (bf16[528,128]{1,0:T(8,128)(2,1)S(1)}, bf16[528,128]{1,0:T(8,128)(2,1)S(1)}, bf16[528,128]{1,0:T(8,128)(2,1)S(1)}, bf16[528,128]{1,0:T(8,128)(2,1)S(1)}) custom-call(s32[32]{0:T(128)S(1)} %copy-done.7, f32[8,128]{1,0:T(8,128)S(1)} %get-tuple-element.26.stats, bf16[2048,576]{1,0:T(8,128)(2,1)S(1)} %get-tuple-element.27.keys_t, ...), custom_call_target="tpu_custom_call" | custom-call | tf_op jit(solution)/shard_map/attention_target/pallas_call | solution.py:529
  114.9 2.4 %collective-permute-start.15 = (bf16[528,128]{1,0:T(8,128)(2,1)S(1)}, bf16[528,128]{1,0:T(8,128)(2,1)S(1)}, u32[]{:S(2)}, u32[]{:S(2)}) collective-permute-start(bf16[528,128]{1,0:T(8,128)(2,1)S(1)} %get-tuple-element.30), channel_id=1, source_target_pairs={{0,64},{32,96},{64,0},{96,32},{1,65},{33,97},{65,1},{97,33},{2,66}... | collective-permute-start | bytes 405512 | tf_op jit(solution)/shard_map/ppermute | solution.py:543
  118.9 3.5 %collective-permute-done.15.t2 = bf16[528,128]{1,0:T(8,128)(2,1)S(1)} collective-permute-done((bf16[528,128]{1,0:T(8,128)(2,1)S(1)}, bf16[528,128]{1,0:T(8,128)(2,1)S(1)}, u32[]{:S(2)}, u32[]{:S(2)}) %collective-permute-start.15) | collective-permute-done | bytes 135200 | tf_op jit(solution)/shard_map/ppermute | solution.py:543
  122.8 2.3 %collective-permute-start.20 = (bf16[4096,768]{1,0:T(8,128)(2,1)}, bf16[4096,768]{1,0:T(8,128)(2,1)S(1)}, u32[]{:S(2)}, u32[]{:S(2)}) collective-permute-start(bf16[4096,768]{1,0:T(8,128)(2,1)} %all-gather.2.cloned.1.call-done.xa), channel_id=1, source_target_pairs={{0,16},{16,0},{1,17},{17,1},{2,18},{18,2},{3,19},{19,3},{4,20},{20... | collective-permute-start | bytes 18874376 | tf_op jit(solution)/shard_map/ppermute | solution.py:553
  126.3 2.1 %collective-permute-start.18 = (bf16[528,128]{1,0:T(8,128)(2,1)S(1)}, bf16[528,128]{1,0:T(8,128)(2,1)S(1)}, u32[]{:S(2)}, u32[]{:S(2)}) collective-permute-start(bf16[528,128]{1,0:T(8,128)(2,1)S(1)} %loss.1.g0), channel_id=1, source_target_pairs={{0,64},{32,96},{64,0},{96,32},{1,65},{33,97},{65,1},{97,33},{2,66}... | collective-permute-start | bytes 405512 | tf_op jit(solution)/shard_map/ppermute | solution.py:453
  128.9 2.5 %collective-permute-done.17.g1 = bf16[528,128]{1,0:T(8,128)(2,1)S(1)} collective-permute-done((bf16[528,128]{1,0:T(8,128)(2,1)S(1)}, bf16[528,128]{1,0:T(8,128)(2,1)S(1)}, u32[]{:S(2)}, u32[]{:S(2)}) %collective-permute-start.17) | collective-permute-done | bytes 135200 | tf_op jit(solution)/shard_map/ppermute | solution.py:453
  131.4 3.5 %collective-permute-done.18.g2 = bf16[528,128]{1,0:T(8,128)(2,1)S(1)} collective-permute-done((bf16[528,128]{1,0:T(8,128)(2,1)S(1)}, bf16[528,128]{1,0:T(8,128)(2,1)S(1)}, u32[]{:S(2)}, u32[]{:S(2)}) %collective-permute-start.18) | collective-permute-done | bytes 135200 | tf_op jit(solution)/shard_map/ppermute | solution.py:453
  135.0 3.8 %index_backward.1 = (bf16[32,64,128]{2,1,0:T(8,128)(2,1)S(1)}, f32[8,128]{1,0:T(8,128)S(1)}) custom-call(bf16[528,128]{1,0:T(8,128)(2,1)S(1)} %loss.1.g0, bf16[528,128]{1,0:T(8,128)(2,1)S(1)} %collective-permute-done.17.g1, bf16[528,128]{1,0:T(8,128)(2,1)S(1)} %collective-permute-done.18.g2, bf16[528,128]{1,0:T(8,128)(2,1)S(1)} %collective-permute-done.19.g3, ...), custom_call_target="tpu_custom_call" | custom-call | tf_op jit(solution)/shard_map/index_backward/pallas_call | solution.py:556
  138.8 15.9 %all_to_all.10.qg = bf16[32,64,128]{2,1,0:T(8,128)(2,1)S(1)} all-to-all(bf16[32,64,128]{2,1,0:T(8,128)(2,1)S(1)} %get-tuple-element.35), channel_id=1, replica_groups=mesh['y'=4,'c'=2,'z'=4,'x'=4] {'z','x','c'}, dimensions={0} | all-to-all | bytes 1048576 | tf_op jit(solution)/shard_map/all_to_all | solution.py:573
  154.7 5.1 %weight_piece.1.p0 = bf16[64,1536]{1,0:T(8,128)(2,1)S(1)} custom-call(bf16[32,64,128]{2,1,0:T(8,128)(2,1)S(1)} %all_to_all.10.qg, bf16[4096,768]{1,0:T(8,128)(2,1)} %all-gather.2.cloned.1.call-done.xa, bf16[4096,768]{1,0:T(8,128)(2,1)S(1)} %collective-permute-done.20.xb), custom_call_target="tpu_custom_call" | custom-call | tf_op jit(solution)/shard_map/weight_piece/pallas_call | solution.py:575
  162.4 2.6 %collective-permute-start.23 = (bf16[64,1536]{1,0:T(8,128)(2,1)S(1)}, bf16[64,1536]{1,0:T(8,128)(2,1)S(1)}, u32[]{:S(2)}, u32[]{:S(2)}) collective-permute-start(bf16[64,1536]{1,0:T(8,128)(2,1)S(1)} %weight_piece.1.p0), channel_id=1, source_target_pairs={{0,11},{1,8},{2,9},{3,10},{4,15},{5,12},{6,13},{7,14},{8,3},{9,0},... | collective-permute-start | bytes 589832 | tf_op jit(solution)/shard_map/ppermute | solution.py:587
  165.0 4.6 %collective-permute-done.21.p1 = bf16[64,1536]{1,0:T(8,128)(2,1)S(1)} collective-permute-done((bf16[64,1536]{1,0:T(8,128)(2,1)S(1)}, bf16[64,1536]{1,0:T(8,128)(2,1)S(1)}, u32[]{:S(2)}, u32[]{:S(2)}) %collective-permute-start.21) | collective-permute-done | bytes 196640 | tf_op jit(solution)/shard_map/ppermute | solution.py:587
  171.2 2.8 %collective-permute-done.23.p3 = bf16[64,1536]{1,0:T(8,128)(2,1)S(1)} collective-permute-done((bf16[64,1536]{1,0:T(8,128)(2,1)S(1)}, bf16[64,1536]{1,0:T(8,128)(2,1)S(1)}, u32[]{:S(2)}, u32[]{:S(2)}) %collective-permute-start.23) | collective-permute-done | bytes 196640 | tf_op jit(solution)/shard_map/ppermute | solution.py:587
  177.1 2.3 %collective-permute-start.28 = (f32[8,128]{1,0:T(8,128)S(1)}, f32[8,128]{1,0:T(8,128)S(1)}, u32[]{:S(2)}, u32[]{:S(2)}) collective-permute-start(f32[8,128]{1,0:T(8,128)S(1)} %get-tuple-element.41), channel_id=1, source_target_pairs={{0,16},{16,0},{1,17},{17,1},{2,18},{18,2},{3,19},{19,3},{4,20},{20... | collective-permute-start | bytes 12296 | tf_op jit(solution)/shard_map/ppermute | solution.py:564
  179.4 2.2 %collective-permute-start.24 = (bf16[768,256]{1,0:T(8,128)(2,1)S(1)}, bf16[768,256]{1,0:T(8,128)(2,1)S(1)}, u32[]{:S(2)}, u32[]{:S(2)}) collective-permute-start(bf16[768,256]{1,0:T(8,128)(2,1)S(1)} %get-tuple-element.39), channel_id=1, source_target_pairs={{0,3},{1,0},{2,1},{3,2},{4,7},{5,4},{6,5},{7,6},{8,11},{9,8},{10,9... | collective-permute-start | bytes 1179656 | tf_op jit(solution)/shard_map/ppermute | solution.py:598
  182.3 7.9 %collective-permute-done.24.refs_1_ = bf16[768,256]{1,0:T(8,128)(2,1)S(1)} collective-permute-done((bf16[768,256]{1,0:T(8,128)(2,1)S(1)}, bf16[768,256]{1,0:T(8,128)(2,1)S(1)}, u32[]{:S(2)}, u32[]{:S(2)}) %collective-permute-start.24) | collective-permute-done | bytes 393248 | tf_op jit(solution)/shard_map/ppermute | solution.py:598
  190.2 3.1 %collective-permute-done.25.refs_2_ = bf16[768,256]{1,0:T(8,128)(2,1)S(1)} collective-permute-done((bf16[768,256]{1,0:T(8,128)(2,1)S(1)}, bf16[768,256]{1,0:T(8,128)(2,1)S(1)}, u32[]{:S(2)}, u32[]{:S(2)}) %collective-permute-start.25) | collective-permute-done | bytes 393248 | tf_op jit(solution)/shard_map/ppermute | solution.py:599
  (66 shorter events, 32.2 us)
Async XLA Ops:
  12.3 41.7 %all-to-all-start = ((bf16[48,176,128]{2,1,0:T(8,128)(2,1)}), bf16[48,176,128]{2,1,0:T(8,128)(2,1)}, u32[]{:S(2)}, u32[]{:S(2)}) async-start(bf16[48,176,128]{2,1,0:T(8,128)(2,1)} %pick_outgoing.1), calls=%async_computation | async-start | bytes 4325376 | tf_op jit(solution)/shard_map/all_to_all | solution.py:471
  22.2 100.6 %all-gather.2.cloned.1.call-start = ((), (), s32[]{:S(2)}) async-start(), calls=%async_computation.2 | async-start | bytes 6684672 | tf_op jit(solution)/shard_map/all_gather | solution.py:506
  25.2 2.3 %collective-permute-start = (bf16[1056,128]{1,0:T(8,128)(2,1)}, bf16[1056,128]{1,0:T(8,128)(2,1)S(1)}, u32[]{:S(2)}, u32[]{:S(2)}) collective-permute-start(bf16[1056,128]{1,0:T(8,128)(2,1)} %get-tuple-element.23), channel_id=1, source_target_pairs={{0,16},{16,0},{1,17},{17,1},{2,18},{18,2},{3,19},{19,3},{4,20},{20... | collective-permute-start | bytes 811016 | tf_op jit(solution)/shard_map/ppermute | solution.py:480
  27.5 9.6 %collective-permute-start.1 = (bf16[1056,128]{1,0:T(8,128)(2,1)S(1)}, bf16[1056,128]{1,0:T(8,128)(2,1)S(1)}, u32[]{:S(2)}, u32[]{:S(2)}) collective-permute-start(bf16[1056,128]{1,0:T(8,128)(2,1)S(1)} %get-tuple-element.43.refs_0_.iq_first), channel_id=1, source_target_pairs={{0,32},{32,64},{64,96},{96,0},{1,33},{33,65},{65,97},{97,1},{2,34}... | collective-permute-start | bytes 811016 | tf_op jit(solution)/shard_map/ppermute | solution.py:446
  29.0 8.1 %collective-permute-start.4 = (bf16[1056,128]{1,0:T(8,128)(2,1)S(1)}, bf16[1056,128]{1,0:T(8,128)(2,1)S(1)}, u32[]{:S(2)}, u32[]{:S(2)}) collective-permute-start(bf16[1056,128]{1,0:T(8,128)(2,1)S(1)} %get-tuple-element.42.refs_1_.iq_second), channel_id=1, source_target_pairs={{0,96},{32,0},{64,32},{96,64},{1,97},{33,1},{65,33},{97,65},{2,98}... | collective-permute-start | bytes 811016 | tf_op jit(solution)/shard_map/ppermute | solution.py:446
  30.6 12.8 %collective-permute-start.2 = (bf16[1056,128]{1,0:T(8,128)(2,1)S(1)}, bf16[1056,128]{1,0:T(8,128)(2,1)}, u32[]{:S(2)}, u32[]{:S(2)}) collective-permute-start(bf16[1056,128]{1,0:T(8,128)(2,1)S(1)} %get-tuple-element.42.refs_1_.iq_second), channel_id=1, source_target_pairs={{0,32},{32,64},{64,96},{96,0},{1,33},{33,65},{65,97},{97,1},{2,34}... | collective-permute-start | bytes 811016 | tf_op jit(solution)/shard_map/ppermute | solution.py:447
  30.6 12.8 %collective-permute-start.6 = (bf16[1056,128]{1,0:T(8,128)(2,1)S(1)}, bf16[1056,128]{1,0:T(8,128)(2,1)}, u32[]{:S(2)}, u32[]{:S(2)}) collective-permute-start(bf16[1056,128]{1,0:T(8,128)(2,1)S(1)} %get-tuple-element.43.refs_0_.iq_first), channel_id=1, source_target_pairs={{0,96},{32,0},{64,32},{96,64},{1,97},{33,1},{65,33},{97,65},{2,98}... | collective-permute-start | bytes 811016 | tf_op jit(solution)/shard_map/ppermute | solution.py:447
  37.1 11.6 %collective-permute-start.3 = (bf16[1056,128]{1,0:T(8,128)(2,1)S(1)}, bf16[1056,128]{1,0:T(8,128)(2,1)}, u32[]{:S(2)}, u32[]{:S(2)}) collective-permute-start(bf16[1056,128]{1,0:T(8,128)(2,1)S(1)} %collective-permute-done.1.refs_1_.refs_2_), channel_id=1, source_target_pairs={{0,32},{32,64},{64,96},{96,0},{1,33},{33,65},{65,97},{97,1},{2,34}... | collective-permute-start | bytes 811016 | tf_op jit(solution)/shard_map/ppermute | solution.py:448
  37.2 11.6 %collective-permute-start.5 = (bf16[1056,128]{1,0:T(8,128)(2,1)S(1)}, bf16[1056,128]{1,0:T(8,128)(2,1)}, u32[]{:S(2)}, u32[]{:S(2)}) collective-permute-start(bf16[1056,128]{1,0:T(8,128)(2,1)S(1)} %collective-permute-done.4.refs_6_.refs_7_), channel_id=1, source_target_pairs={{0,96},{32,0},{64,32},{96,64},{1,97},{33,1},{65,33},{97,65},{2,98}... | collective-permute-start | bytes 811016 | tf_op jit(solution)/shard_map/ppermute | solution.py:448
  41.6 43.9 %copy-start.7 = (s32[32]{0:T(128)S(1)}, s32[32]{0:T(128)}, u32[]{:S(2)}) copy-start(s32[32]{0:T(128)} %counts.3) | copy-start | bytes 388
  56.8 35.2 %collective-permute-start.13 = (bf16[16,576,128]{2,1,0:T(8,128)(2,1)S(1)}, bf16[16,576,128]{2,1,0:T(8,128)(2,1)S(1)}, u32[]{:S(2)}, u32[]{:S(2)}) collective-permute-start(bf16[16,576,128]{2,1,0:T(8,128)(2,1)S(1)} %dynamic-slice_bitcast_fusion.refs_0_), channel_id=1, source_target_pairs={{0,16},{16,0},{1,17},{17,1},{2,18},{18,2},{3,19},{19,3},{4,20},{20... | collective-permute-start | bytes 7077896 | tf_op jit(solution)/shard_map/ppermute | solution.py:487
  58.7 11.4 %collective-permute-start.7 = (bf16[8,176,128]{2,1,0:T(8,128)(2,1)}, bf16[8,176,128]{2,1,0:T(8,128)(2,1)S(1)}, u32[]{:S(2)}, u32[]{:S(2)}) collective-permute-start(bf16[8,176,128]{2,1,0:T(8,128)(2,1)} %get-tuple-element.24.own_low), channel_id=1, source_target_pairs={{0,32},{32,64},{64,96},{96,0},{1,33},{33,65},{65,97},{97,1},{2,34}... | collective-permute-start | bytes 1081352 | tf_op jit(solution)/shard_map/ppermute | solution.py:446
  60.1 10.2 %collective-permute-start.10 = (bf16[8,176,128]{2,1,0:T(8,128)(2,1)}, bf16[8,176,128]{2,1,0:T(8,128)(2,1)S(1)}, u32[]{:S(2)}, u32[]{:S(2)}) collective-permute-start(bf16[8,176,128]{2,1,0:T(8,128)(2,1)} %get-tuple-element.25.own_high), channel_id=1, source_target_pairs={{0,96},{32,0},{64,32},{96,64},{1,97},{33,1},{65,33},{97,65},{2,98}... | collective-permute-start | bytes 1081352 | tf_op jit(solution)/shard_map/ppermute | solution.py:446
  61.4 16.5 %collective-permute-start.8 = (bf16[8,176,128]{2,1,0:T(8,128)(2,1)}, bf16[8,176,128]{2,1,0:T(8,128)(2,1)S(1)}, u32[]{:S(2)}, u32[]{:S(2)}) collective-permute-start(bf16[8,176,128]{2,1,0:T(8,128)(2,1)} %get-tuple-element.25.own_high), channel_id=1, source_target_pairs={{0,32},{32,64},{64,96},{96,0},{1,33},{33,65},{65,97},{97,1},{2,34}... | collective-permute-start | bytes 1081352 | tf_op jit(solution)/shard_map/ppermute | solution.py:447
  61.5 16.4 %collective-permute-start.12 = (bf16[8,176,128]{2,1,0:T(8,128)(2,1)}, bf16[8,176,128]{2,1,0:T(8,128)(2,1)S(1)}, u32[]{:S(2)}, u32[]{:S(2)}) collective-permute-start(bf16[8,176,128]{2,1,0:T(8,128)(2,1)} %get-tuple-element.24.own_low), channel_id=1, source_target_pairs={{0,96},{32,0},{64,32},{96,64},{1,97},{33,1},{65,33},{97,65},{2,98}... | collective-permute-start | bytes 1081352 | tf_op jit(solution)/shard_map/ppermute | solution.py:447
  70.1 15.4 %collective-permute-start.9 = (bf16[8,176,128]{2,1,0:T(8,128)(2,1)S(1)}, bf16[8,176,128]{2,1,0:T(8,128)(2,1)S(1)}, u32[]{:S(2)}, u32[]{:S(2)}) collective-permute-start(bf16[8,176,128]{2,1,0:T(8,128)(2,1)S(1)} %collective-permute-done.7.a1), channel_id=1, source_target_pairs={{0,32},{32,64},{64,96},{96,0},{1,33},{33,65},{65,97},{97,1},{2,34}... | collective-permute-start | bytes 1081352 | tf_op jit(solution)/shard_map/ppermute | solution.py:448
  70.3 15.3 %collective-permute-start.11 = (bf16[8,176,128]{2,1,0:T(8,128)(2,1)S(1)}, bf16[8,176,128]{2,1,0:T(8,128)(2,1)S(1)}, u32[]{:S(2)}, u32[]{:S(2)}) collective-permute-start(bf16[8,176,128]{2,1,0:T(8,128)(2,1)S(1)} %collective-permute-done.10.b3), channel_id=1, source_target_pairs={{0,96},{32,0},{64,32},{96,64},{1,97},{33,1},{65,33},{97,65},{2,98}... | collective-permute-start | bytes 1081352 | tf_op jit(solution)/shard_map/ppermute | solution.py:448
  113.8 5.1 %collective-permute-start.14 = (bf16[528,128]{1,0:T(8,128)(2,1)S(1)}, bf16[528,128]{1,0:T(8,128)(2,1)S(1)}, u32[]{:S(2)}, u32[]{:S(2)}) collective-permute-start(bf16[528,128]{1,0:T(8,128)(2,1)S(1)} %get-tuple-element.29), channel_id=1, source_target_pairs={{0,32},{32,64},{64,96},{96,0},{1,33},{33,65},{65,97},{97,1},{2,34}... | collective-permute-start | bytes 405512 | tf_op jit(solution)/shard_map/ppermute | solution.py:543
  114.9 7.4 %collective-permute-start.15 = (bf16[528,128]{1,0:T(8,128)(2,1)S(1)}, bf16[528,128]{1,0:T(8,128)(2,1)S(1)}, u32[]{:S(2)}, u32[]{:S(2)}) collective-permute-start(bf16[528,128]{1,0:T(8,128)(2,1)S(1)} %get-tuple-element.30), channel_id=1, source_target_pairs={{0,64},{32,96},{64,0},{96,32},{1,65},{33,97},{65,1},{97,33},{2,66}... | collective-permute-start | bytes 405512 | tf_op jit(solution)/shard_map/ppermute | solution.py:543
  117.3 5.3 %collective-permute-start.16 = (bf16[528,128]{1,0:T(8,128)(2,1)S(1)}, bf16[528,128]{1,0:T(8,128)(2,1)S(1)}, u32[]{:S(2)}, u32[]{:S(2)}) collective-permute-start(bf16[528,128]{1,0:T(8,128)(2,1)S(1)} %get-tuple-element.31), channel_id=1, source_target_pairs={{0,96},{32,0},{64,32},{96,64},{1,97},{33,1},{65,33},{97,65},{2,98}... | collective-permute-start | bytes 405512 | tf_op jit(solution)/shard_map/ppermute | solution.py:543
  122.8 31.9 %collective-permute-start.20 = (bf16[4096,768]{1,0:T(8,128)(2,1)}, bf16[4096,768]{1,0:T(8,128)(2,1)S(1)}, u32[]{:S(2)}, u32[]{:S(2)}) collective-permute-start(bf16[4096,768]{1,0:T(8,128)(2,1)} %all-gather.2.cloned.1.call-done.xa), channel_id=1, source_target_pairs={{0,16},{16,0},{1,17},{17,1},{2,18},{18,2},{3,19},{19,3},{4,20},{20... | collective-permute-start | bytes 18874376 | tf_op jit(solution)/shard_map/ppermute | solution.py:553
  125.1 6.4 %collective-permute-start.17 = (bf16[528,128]{1,0:T(8,128)(2,1)S(1)}, bf16[528,128]{1,0:T(8,128)(2,1)S(1)}, u32[]{:S(2)}, u32[]{:S(2)}) collective-permute-start(bf16[528,128]{1,0:T(8,128)(2,1)S(1)} %loss.1.g0), channel_id=1, source_target_pairs={{0,32},{32,64},{64,96},{96,0},{1,33},{33,65},{65,97},{97,1},{2,34}... | collective-permute-start | bytes 405512 | tf_op jit(solution)/shard_map/ppermute | solution.py:453
  126.3 8.7 %collective-permute-start.18 = (bf16[528,128]{1,0:T(8,128)(2,1)S(1)}, bf16[528,128]{1,0:T(8,128)(2,1)S(1)}, u32[]{:S(2)}, u32[]{:S(2)}) collective-permute-start(bf16[528,128]{1,0:T(8,128)(2,1)S(1)} %loss.1.g0), channel_id=1, source_target_pairs={{0,64},{32,96},{64,0},{96,32},{1,65},{33,97},{65,1},{97,33},{2,66}... | collective-permute-start | bytes 405512 | tf_op jit(solution)/shard_map/ppermute | solution.py:453
  128.4 6.6 %collective-permute-start.19 = (bf16[528,128]{1,0:T(8,128)(2,1)S(1)}, bf16[528,128]{1,0:T(8,128)(2,1)S(1)}, u32[]{:S(2)}, u32[]{:S(2)}) collective-permute-start(bf16[528,128]{1,0:T(8,128)(2,1)S(1)} %loss.1.g0), channel_id=1, source_target_pairs={{0,96},{32,0},{64,32},{96,64},{1,97},{33,1},{65,33},{97,65},{2,98}... | collective-permute-start | bytes 405512 | tf_op jit(solution)/shard_map/ppermute | solution.py:453
  159.8 9.7 %collective-permute-start.21 = (bf16[64,1536]{1,0:T(8,128)(2,1)S(1)}, bf16[64,1536]{1,0:T(8,128)(2,1)S(1)}, u32[]{:S(2)}, u32[]{:S(2)}) collective-permute-start(bf16[64,1536]{1,0:T(8,128)(2,1)S(1)} %weight_piece.1.p0), channel_id=1, source_target_pairs={{0,9},{1,10},{2,11},{3,8},{4,13},{5,14},{6,15},{7,12},{8,1},{9,2},... | collective-permute-start | bytes 589832 | tf_op jit(solution)/shard_map/ppermute | solution.py:587
  161.3 9.9 %collective-permute-start.22 = (bf16[64,1536]{1,0:T(8,128)(2,1)S(1)}, bf16[64,1536]{1,0:T(8,128)(2,1)S(1)}, u32[]{:S(2)}, u32[]{:S(2)}) collective-permute-start(bf16[64,1536]{1,0:T(8,128)(2,1)S(1)} %weight_piece.1.p0), channel_id=1, source_target_pairs={{0,2},{1,3},{2,0},{3,1},{4,6},{5,7},{6,4},{7,5},{8,10},{9,11},{10,... | collective-permute-start | bytes 589832 | tf_op jit(solution)/shard_map/ppermute | solution.py:587
  162.4 11.7 %collective-permute-start.23 = (bf16[64,1536]{1,0:T(8,128)(2,1)S(1)}, bf16[64,1536]{1,0:T(8,128)(2,1)S(1)}, u32[]{:S(2)}, u32[]{:S(2)}) collective-permute-start(bf16[64,1536]{1,0:T(8,128)(2,1)S(1)} %weight_piece.1.p0), channel_id=1, source_target_pairs={{0,11},{1,8},{2,9},{3,10},{4,15},{5,12},{6,13},{7,14},{8,3},{9,0},... | collective-permute-start | bytes 589832 | tf_op jit(solution)/shard_map/ppermute | solution.py:587
  174.4 20.7 %collective-permute-start.26 = (bf16[1536,256]{1,0:T(8,128)(2,1)S(1)}, bf16[1536,256]{1,0:T(8,128)(2,1)S(1)}, u32[]{:S(2)}, u32[]{:S(2)}) collective-permute-start(bf16[1536,256]{1,0:T(8,128)(2,1)S(1)} %get-tuple-element.38.refs_0_), channel_id=1, source_target_pairs={{0,4},{1,5},{2,6},{3,7},{4,8},{5,9},{6,10},{7,11},{8,12},{9,13},{1... | collective-permute-start | bytes 2359304 | tf_op jit(solution)/shard_map/ppermute | solution.py:596
  175.5 19.6 %collective-permute-start.27 = (bf16[1536,256]{1,0:T(8,128)(2,1)S(1)}, bf16[1536,256]{1,0:T(8,128)(2,1)S(1)}, u32[]{:S(2)}, u32[]{:S(2)}) collective-permute-start(bf16[1536,256]{1,0:T(8,128)(2,1)S(1)} %get-tuple-element.38.refs_0_), channel_id=1, source_target_pairs={{0,12},{1,13},{2,14},{3,15},{4,0},{5,1},{6,2},{7,3},{8,4},{9,5},{1... | collective-permute-start | bytes 2359304 | tf_op jit(solution)/shard_map/ppermute | solution.py:597
  177.1 4.5 %collective-permute-start.28 = (f32[8,128]{1,0:T(8,128)S(1)}, f32[8,128]{1,0:T(8,128)S(1)}, u32[]{:S(2)}, u32[]{:S(2)}) collective-permute-start(f32[8,128]{1,0:T(8,128)S(1)} %get-tuple-element.41), channel_id=1, source_target_pairs={{0,16},{16,0},{1,17},{17,1},{2,18},{18,2},{3,19},{19,3},{4,20},{20... | collective-permute-start | bytes 12296 | tf_op jit(solution)/shard_map/ppermute | solution.py:564
  179.4 10.7 %collective-permute-start.24 = (bf16[768,256]{1,0:T(8,128)(2,1)S(1)}, bf16[768,256]{1,0:T(8,128)(2,1)S(1)}, u32[]{:S(2)}, u32[]{:S(2)}) collective-permute-start(bf16[768,256]{1,0:T(8,128)(2,1)S(1)} %get-tuple-element.39), channel_id=1, source_target_pairs={{0,3},{1,0},{2,1},{3,2},{4,7},{5,4},{6,5},{7,6},{8,11},{9,8},{10,9... | collective-permute-start | bytes 1179656 | tf_op jit(solution)/shard_map/ppermute | solution.py:598
  181.6 11.6 %collective-permute-start.25 = (bf16[768,256]{1,0:T(8,128)(2,1)S(1)}, bf16[768,256]{1,0:T(8,128)(2,1)S(1)}, u32[]{:S(2)}, u32[]{:S(2)}) collective-permute-start(bf16[768,256]{1,0:T(8,128)(2,1)S(1)} %get-tuple-element.40), channel_id=1, source_target_pairs={{0,1},{1,2},{2,3},{3,0},{4,5},{5,6},{6,7},{7,4},{8,9},{9,10},{10,1... | collective-permute-start | bytes 1179656 | tf_op jit(solution)/shard_map/ppermute | solution.py:599
  (7 other events, 147.2 us)
Sparse Core Ops, SparseCore 0:
  56.9 60.7 all-gather.1

commit v7 on v6

--- a/solution.py
+++ b/solution.py
@@ -239,10 +239,16 @@
     y, core, _ = place()
     count = slots_in_use(counts)
     lanes = pl.multiple_of(core * BLK, BLK)
-    own = pltpu.make_async_copy(q_own.at[:, :, pl.ds(lanes, BLK)], qa, sem)
-    own.start()
+    early = 2
+    spans = (pl.ds(0, early), pl.ds(early, qa.shape[0] - early))
+    loads = [
+        pltpu.make_async_copy(q_own.at[span, :, pl.ds(lanes, BLK)], qa.at[span], sem.at[n])
+        for n, span in enumerate(spans)
+    ]
+    for c in loads:
+        c.start()
     total[...] = jnp.zeros_like(total)
-    own.wait()
+    loads[0].wait()
 
     chunk = 1024
     token = lax.broadcasted_iota(I32, (BLK, 2 * BLK), 1) % BLK
@@ -305,6 +311,7 @@
 
     pairs = qa.shape[0]
     shift = both(0, buf_a, None, None)
+    loads[1].wait()
     shift = lax.fori_loop(0, pairs // 2 - 1, step, shift)
     shift = both(pairs - 1, buf_b, buf_a, shift)
     both(None, None, buf_b, shift)
@@ -536,7 +543,7 @@
             pltpu.VMEM((KEYS, 2 * BLK), F32),
             pltpu.VMEM((KEYS, 2 * BLK), F32),
             pltpu.VMEM((KEYS, BLK), F32),
-            pltpu.SemaphoreType.DMA,
+            pltpu.SemaphoreType.DMA((2,)),
         ],
         "attention_target",
     )(block_counts, stats, in_vmem(latent_t), in_hbm(q_t), in_vmem(q_other))

time: 204 us -> 203 us (level)
  transfers between devices with their start and end apart: 31 -> 31, of which waited for: 17 -> 17; matrix products, arithmetic and copies ran while one was open for 2% -> 2% of each run, Pallas kernels for 18% -> 17%
where the time goes in v7:
time: 203 us; the launch traced here: 202 us
  waiting for transfers between devices  65.1 us (32%)
  starting transfers between devices  50.9 us (25%)
  Pallas kernels  49.5 us (24%)
  blocking collectives  16 us (8%)
  between operations  14.3 us (7%)
  local copies, waits for them, and re-layouts  6.05 us (3%)
    pallas_call x1, Pallas kernels, on_device(): call(target_kernel, (shape((LG_ROWS, BLK), BF16),) * 4, [SMEM, VMEM, VMEM...  21.1 us
    all_to_all x1, blocking collectives, on_device(): lax.all_to_all(query_grad, ('z', 'x', 'c'), split_axis=0, concat_axis=0,...  16 us
    ppermute x2, waiting for transfers between devices, relayed(): lax.ppermute(low_up, 'y', ring(1))  12.9 us
    ppermute x2, waiting for transfers between devices, relayed(): lax.ppermute(low, 'y', ring(1))  9.74 us
    ppermute x3, waiting for transfers between devices, on_device(): lax.ppermute(piece, qblk, plane(-2 * d, d))  9.07 us
    all_to_all x1, starting transfers between devices, on_device(): lax.all_to_all(outgoing, ('z', 'x'), split_axis=0, concat_axis=0, tiled=T...  8.48 us
    ppermute x1, waiting for transfers between devices, on_device(): top = lax.ppermute(top, qblk, plane(0, -1))  7.93 us
    pallas_call x1, Pallas kernels, on_device(): call(logits_kernel, (shape((OWNK, BLK), F32), shape((8, BLK), F32), shape...  6.43 us
  transfers between devices with their start and end apart: 31, of which 17 were waited for; matrix products, arithmetic and copies ran while one was open for 2% of the time, Pallas kernels for 17%

profile of v7, /device:TPU:1, one launch (start us, length us, event | category | flops | bytes accessed | tf_op | source)
XLA Modules:
  0.0 201.8 jit_solution(9781577852404134998)
XLA Ops:
  7.9 4.5 %pick_outgoing.1 = bf16[48,176,128]{2,1,0:T(8,128)(2,1)} custom-call(s32[16,32]{1,0:T(8,128)S(1)} %bitcast.9, bf16[32,704,128]{2,1,0:T(8,128)(2,1)} %cache.1), custom_call_target="tpu_custom_call" | custom-call | tf_op jit(solution)/shard_map/pick_outgoing/pallas_call | solution.py:470
  12.4 8.5 %all-to-all-start = ((bf16[48,176,128]{2,1,0:T(8,128)(2,1)}), bf16[48,176,128]{2,1,0:T(8,128)(2,1)}, u32[]{:S(2)}, u32[]{:S(2)}) async-start(bf16[48,176,128]{2,1,0:T(8,128)(2,1)} %pick_outgoing.1), calls=%async_computation | async-start | bytes 4325376 | tf_op jit(solution)/shard_map/all_to_all | solution.py:478
  29.1 2.7 %collective-permute-start.6 = (bf16[1056,128]{1,0:T(8,128)(2,1)S(1)}, bf16[1056,128]{1,0:T(8,128)(2,1)}, u32[]{:S(2)}, u32[]{:S(2)}) collective-permute-start(bf16[1056,128]{1,0:T(8,128)(2,1)S(1)} %get-tuple-element.43.refs_0_.iq_first), channel_id=1, source_target_pairs={{0,96},{32,0},{64,32},{96,64},{1,97},{33,1},{65,33},{97,65},{2,98}... | collective-permute-start | bytes 811016 | tf_op jit(solution)/shard_map/ppermute | solution.py:454
  31.8 3.6 %collective-permute-done.1.refs_1_.refs_2_ = bf16[1056,128]{1,0:T(8,128)(2,1)S(1)} collective-permute-done((bf16[1056,128]{1,0:T(8,128)(2,1)S(1)}, bf16[1056,128]{1,0:T(8,128)(2,1)S(1)}, u32[]{:S(2)}, u32[]{:S(2)}) %collective-permute-start.1) | collective-permute-done | bytes 270368 | tf_op jit(solution)/shard_map/ppermute | solution.py:453
  35.5 2.7 %collective-permute-start.5 = (bf16[1056,128]{1,0:T(8,128)(2,1)S(1)}, bf16[1056,128]{1,0:T(8,128)(2,1)}, u32[]{:S(2)}, u32[]{:S(2)}) collective-permute-start(bf16[1056,128]{1,0:T(8,128)(2,1)S(1)} %collective-permute-done.4.refs_6_.refs_7_), channel_id=1, source_target_pairs={{0,96},{32,0},{64,32},{96,64},{1,97},{33,1},{65,33},{97,65},{2,98}... | collective-permute-start | bytes 811016 | tf_op jit(solution)/shard_map/ppermute | solution.py:455
  41.8 5.3 %collective-permute-done.3.refs_3_.refs_4_ = bf16[1056,128]{1,0:T(8,128)(2,1)} collective-permute-done((bf16[1056,128]{1,0:T(8,128)(2,1)S(1)}, bf16[1056,128]{1,0:T(8,128)(2,1)}, u32[]{:S(2)}, u32[]{:S(2)}) %collective-permute-start.3) | collective-permute-done | bytes 270368 | tf_op jit(solution)/shard_map/ppermute | solution.py:455
  47.1 5.2 %all-to-all-done.arrived = bf16[48,176,128]{2,1,0:T(8,128)(2,1)} async-done(((bf16[48,176,128]{2,1,0:T(8,128)(2,1)}), bf16[48,176,128]{2,1,0:T(8,128)(2,1)}, u32[]{:S(2)}, u32[]{:S(2)}) %all-to-all-start) | async-done | bytes 2162720 | tf_op jit(solution)/shard_map/all_to_all | solution.py:478
  52.3 2.7 %pick_listed.1 = (bf16[8,176,128]{2,1,0:T(8,128)(2,1)}, bf16[8,176,128]{2,1,0:T(8,128)(2,1)}) custom-call(s32[16,32]{1,0:T(8,128)S(1)} %bitcast.10, bf16[48,176,128]{2,1,0:T(8,128)(2,1)} %all-to-all-done.arrived, bf16[16,576,128]{2,1,0:T(8,128)(2,1)S(1)} %dynamic-slice_bitcast_fusion.refs_0_, bf16[1056,128]{1,0:T(8,128)(2,1)S(1)} %collective-permute-done.1.refs_1_.refs_2_, ...), custom_call_target="tpu_custom_call" | custom-call | tf_op jit(solution)/shard_map/pick_listed/pallas_call | solution.py:496
  55.1 2.2 %collective-permute-start.13 = (bf16[16,576,128]{2,1,0:T(8,128)(2,1)S(1)}, bf16[16,576,128]{2,1,0:T(8,128)(2,1)S(1)}, u32[]{:S(2)}, u32[]{:S(2)}) collective-permute-start(bf16[16,576,128]{2,1,0:T(8,128)(2,1)S(1)} %dynamic-slice_bitcast_fusion.refs_0_), channel_id=1, source_target_pairs={{0,16},{16,0},{1,17},{17,1},{2,18},{18,2},{3,19},{19,3},{4,20},{20... | collective-permute-start | bytes 7077896 | tf_op jit(solution)/shard_map/ppermute | solution.py:494
  60.1 2.6 %collective-permute-start.12 = (bf16[8,176,128]{2,1,0:T(8,128)(2,1)}, bf16[8,176,128]{2,1,0:T(8,128)(2,1)S(1)}, u32[]{:S(2)}, u32[]{:S(2)}) collective-permute-start(bf16[8,176,128]{2,1,0:T(8,128)(2,1)} %get-tuple-element.24.own_low), channel_id=1, source_target_pairs={{0,96},{32,0},{64,32},{96,64},{1,97},{33,1},{65,33},{97,65},{2,98}... | collective-permute-start | bytes 1081352 | tf_op jit(solution)/shard_map/ppermute | solution.py:454
  62.7 6.1 %collective-permute-done.7.a1 = bf16[8,176,128]{2,1,0:T(8,128)(2,1)S(1)} collective-permute-done((bf16[8,176,128]{2,1,0:T(8,128)(2,1)}, bf16[8,176,128]{2,1,0:T(8,128)(2,1)S(1)}, u32[]{:S(2)}, u32[]{:S(2)}) %collective-permute-start.7) | collective-permute-done | bytes 360480 | tf_op jit(solution)/shard_map/ppermute | solution.py:453
  68.8 2.7 %collective-permute-start.11 = (bf16[8,176,128]{2,1,0:T(8,128)(2,1)S(1)}, bf16[8,176,128]{2,1,0:T(8,128)(2,1)S(1)}, u32[]{:S(2)}, u32[]{:S(2)}) collective-permute-start(bf16[8,176,128]{2,1,0:T(8,128)(2,1)S(1)} %collective-permute-done.10.b3), channel_id=1, source_target_pairs={{0,96},{32,0},{64,32},{96,64},{1,97},{33,1},{65,33},{97,65},{2,98}... | collective-permute-start | bytes 1081352 | tf_op jit(solution)/shard_map/ppermute | solution.py:455
  71.5 5.1 %collective-permute-done.8.b1 = bf16[8,176,128]{2,1,0:T(8,128)(2,1)S(1)} collective-permute-done((bf16[8,176,128]{2,1,0:T(8,128)(2,1)}, bf16[8,176,128]{2,1,0:T(8,128)(2,1)S(1)}, u32[]{:S(2)}, u32[]{:S(2)}) %collective-permute-start.8) | collective-permute-done | bytes 360480 | tf_op jit(solution)/shard_map/ppermute | solution.py:454
  76.6 7.6 %collective-permute-done.9.a2 = bf16[8,176,128]{2,1,0:T(8,128)(2,1)S(1)} collective-permute-done((bf16[8,176,128]{2,1,0:T(8,128)(2,1)S(1)}, bf16[8,176,128]{2,1,0:T(8,128)(2,1)S(1)}, u32[]{:S(2)}, u32[]{:S(2)}) %collective-permute-start.9) | collective-permute-done | bytes 360480 | tf_op jit(solution)/shard_map/ppermute | solution.py:455
  84.2 6.4 %index_logits.1 = (f32[512,128]{1,0:T(8,128)S(1)}, f32[8,128]{1,0:T(8,128)S(1)}, bf16[2048,576]{1,0:T(8,128)(2,1)S(1)}, bf16[128,2048]{1,0:T(8,128)(2,1)}, bf16[2048,128]{1,0:T(8,128)(2,1)}) custom-call(s32[32]{0:T(128)S(1)} %copy-done.7, bf16[8,176,128]{2,1,0:T(8,128)(2,1)} %get-tuple-element.24.own_low, bf16[8,176,128]{2,1,0:T(8,128)(2,1)} %get-tuple-element.25.own_high, ...), custom_call_target="tpu_custom_call" | custom-call | tf_op jit(solution)/shard_map/index_logits/pallas_call | solution.py:515
  90.7 21.1 %attention_target.1 = (bf16[528,128]{1,0:T(8,128)(2,1)S(1)}, bf16[528,128]{1,0:T(8,128)(2,1)S(1)}, bf16[528,128]{1,0:T(8,128)(2,1)S(1)}, bf16[528,128]{1,0:T(8,128)(2,1)S(1)}) custom-call(s32[32]{0:T(128)S(1)} %copy-done.7, f32[8,128]{1,0:T(8,128)S(1)} %get-tuple-element.26.stats, bf16[2048,576]{1,0:T(8,128)(2,1)S(1)} %get-tuple-element.27.keys_t, ...), custom_call_target="tpu_custom_call" | custom-call | tf_op jit(solution)/shard_map/attention_target/pallas_call | solution.py:536
  112.8 2.6 %collective-permute-start.15 = (bf16[528,128]{1,0:T(8,128)(2,1)S(1)}, bf16[528,128]{1,0:T(8,128)(2,1)S(1)}, u32[]{:S(2)}, u32[]{:S(2)}) collective-permute-start(bf16[528,128]{1,0:T(8,128)(2,1)S(1)} %get-tuple-element.30), channel_id=1, source_target_pairs={{0,64},{32,96},{64,0},{96,32},{1,65},{33,97},{65,1},{97,33},{2,66}... | collective-permute-start | bytes 405512 | tf_op jit(solution)/shard_map/ppermute | solution.py:550
  117.3 3.1 %collective-permute-done.15.t2 = bf16[528,128]{1,0:T(8,128)(2,1)S(1)} collective-permute-done((bf16[528,128]{1,0:T(8,128)(2,1)S(1)}, bf16[528,128]{1,0:T(8,128)(2,1)S(1)}, u32[]{:S(2)}, u32[]{:S(2)}) %collective-permute-start.15) | collective-permute-done | bytes 135200 | tf_op jit(solution)/shard_map/ppermute | solution.py:550
  121.2 1.9 collective-permute-start.20
  124.3 2.1 %collective-permute-start.18 = (bf16[528,128]{1,0:T(8,128)(2,1)S(1)}, bf16[528,128]{1,0:T(8,128)(2,1)S(1)}, u32[]{:S(2)}, u32[]{:S(2)}) collective-permute-start(bf16[528,128]{1,0:T(8,128)(2,1)S(1)} %loss.1.g0), channel_id=1, source_target_pairs={{0,64},{32,96},{64,0},{96,32},{1,65},{33,97},{65,1},{97,33},{2,66}... | collective-permute-start | bytes 405512 | tf_op jit(solution)/shard_map/ppermute | solution.py:460
  127.2 2.2 %collective-permute-done.17.g1 = bf16[528,128]{1,0:T(8,128)(2,1)S(1)} collective-permute-done((bf16[528,128]{1,0:T(8,128)(2,1)S(1)}, bf16[528,128]{1,0:T(8,128)(2,1)S(1)}, u32[]{:S(2)}, u32[]{:S(2)}) %collective-permute-start.17) | collective-permute-done | bytes 135200 | tf_op jit(solution)/shard_map/ppermute | solution.py:460
  129.5 3.5 %collective-permute-done.18.g2 = bf16[528,128]{1,0:T(8,128)(2,1)S(1)} collective-permute-done((bf16[528,128]{1,0:T(8,128)(2,1)S(1)}, bf16[528,128]{1,0:T(8,128)(2,1)S(1)}, u32[]{:S(2)}, u32[]{:S(2)}) %collective-permute-start.18) | collective-permute-done | bytes 135200 | tf_op jit(solution)/shard_map/ppermute | solution.py:460
  133.0 3.8 %index_backward.1 = (bf16[32,64,128]{2,1,0:T(8,128)(2,1)S(1)}, f32[8,128]{1,0:T(8,128)S(1)}) custom-call(bf16[528,128]{1,0:T(8,128)(2,1)S(1)} %loss.1.g0, bf16[528,128]{1,0:T(8,128)(2,1)S(1)} %collective-permute-done.17.g1, bf16[528,128]{1,0:T(8,128)(2,1)S(1)} %collective-permute-done.18.g2, bf16[528,128]{1,0:T(8,128)(2,1)S(1)} %collective-permute-done.19.g3, ...), custom_call_target="tpu_custom_call" | custom-call | tf_op jit(solution)/shard_map/index_backward/pallas_call | solution.py:563
  136.8 16.0 %all_to_all.10.qg = bf16[32,64,128]{2,1,0:T(8,128)(2,1)S(1)} all-to-all(bf16[32,64,128]{2,1,0:T(8,128)(2,1)S(1)} %get-tuple-element.35), channel_id=1, replica_groups=mesh['y'=4,'c'=2,'z'=4,'x'=4] {'z','x','c'}, dimensions={0} | all-to-all | bytes 1048576 | tf_op jit(solution)/shard_map/all_to_all | solution.py:580
  152.7 5.1 %weight_piece.1.p0 = bf16[64,1536]{1,0:T(8,128)(2,1)S(1)} custom-call(bf16[32,64,128]{2,1,0:T(8,128)(2,1)S(1)} %all_to_all.10.qg, bf16[4096,768]{1,0:T(8,128)(2,1)} %all-gather.2.cloned.1.call-done.xa, bf16[4096,768]{1,0:T(8,128)(2,1)S(1)} %collective-permute-done.20.xb), custom_call_target="tpu_custom_call" | custom-call | tf_op jit(solution)/shard_map/weight_piece/pallas_call | solution.py:582
  160.4 2.6 %collective-permute-start.23 = (bf16[64,1536]{1,0:T(8,128)(2,1)S(1)}, bf16[64,1536]{1,0:T(8,128)(2,1)S(1)}, u32[]{:S(2)}, u32[]{:S(2)}) collective-permute-start(bf16[64,1536]{1,0:T(8,128)(2,1)S(1)} %weight_piece.1.p0), channel_id=1, source_target_pairs={{0,11},{1,8},{2,9},{3,10},{4,15},{5,12},{6,13},{7,14},{8,3},{9,0},... | collective-permute-start | bytes 589832 | tf_op jit(solution)/shard_map/ppermute | solution.py:594
  163.0 4.6 %collective-permute-done.21.p1 = bf16[64,1536]{1,0:T(8,128)(2,1)S(1)} collective-permute-done((bf16[64,1536]{1,0:T(8,128)(2,1)S(1)}, bf16[64,1536]{1,0:T(8,128)(2,1)S(1)}, u32[]{:S(2)}, u32[]{:S(2)}) %collective-permute-start.21) | collective-permute-done | bytes 196640 | tf_op jit(solution)/shard_map/ppermute | solution.py:594
  169.2 2.8 %collective-permute-done.23.p3 = bf16[64,1536]{1,0:T(8,128)(2,1)S(1)} collective-permute-done((bf16[64,1536]{1,0:T(8,128)(2,1)S(1)}, bf16[64,1536]{1,0:T(8,128)(2,1)S(1)}, u32[]{:S(2)}, u32[]{:S(2)}) %collective-permute-start.23) | collective-permute-done | bytes 196640 | tf_op jit(solution)/shard_map/ppermute | solution.py:594
  175.2 2.3 %collective-permute-start.28 = (f32[8,128]{1,0:T(8,128)S(1)}, f32[8,128]{1,0:T(8,128)S(1)}, u32[]{:S(2)}, u32[]{:S(2)}) collective-permute-start(f32[8,128]{1,0:T(8,128)S(1)} %get-tuple-element.41), channel_id=1, source_target_pairs={{0,16},{16,0},{1,17},{17,1},{2,18},{18,2},{3,19},{19,3},{4,20},{20... | collective-permute-start | bytes 12296 | tf_op jit(solution)/shard_map/ppermute | solution.py:571
  177.5 2.2 %collective-permute-start.24 = (bf16[768,256]{1,0:T(8,128)(2,1)S(1)}, bf16[768,256]{1,0:T(8,128)(2,1)S(1)}, u32[]{:S(2)}, u32[]{:S(2)}) collective-permute-start(bf16[768,256]{1,0:T(8,128)(2,1)S(1)} %get-tuple-element.39), channel_id=1, source_target_pairs={{0,3},{1,0},{2,1},{3,2},{4,7},{5,4},{6,5},{7,6},{8,11},{9,8},{10,9... | collective-permute-start | bytes 1179656 | tf_op jit(solution)/shard_map/ppermute | solution.py:605
  180.3 7.9 %collective-permute-done.24.refs_1_ = bf16[768,256]{1,0:T(8,128)(2,1)S(1)} collective-permute-done((bf16[768,256]{1,0:T(8,128)(2,1)S(1)}, bf16[768,256]{1,0:T(8,128)(2,1)S(1)}, u32[]{:S(2)}, u32[]{:S(2)}) %collective-permute-start.24) | collective-permute-done | bytes 393248 | tf_op jit(solution)/shard_map/ppermute | solution.py:605
  188.3 3.1 %collective-permute-done.25.refs_2_ = bf16[768,256]{1,0:T(8,128)(2,1)S(1)} collective-permute-done((bf16[768,256]{1,0:T(8,128)(2,1)S(1)}, bf16[768,256]{1,0:T(8,128)(2,1)S(1)}, u32[]{:S(2)}, u32[]{:S(2)}) %collective-permute-start.25) | collective-permute-done | bytes 393248 | tf_op jit(solution)/shard_map/ppermute | solution.py:606
  (66 shorter events, 32.5 us)
Async XLA Ops:
  12.4 39.9 %all-to-all-start = ((bf16[48,176,128]{2,1,0:T(8,128)(2,1)}), bf16[48,176,128]{2,1,0:T(8,128)(2,1)}, u32[]{:S(2)}, u32[]{:S(2)}) async-start(bf16[48,176,128]{2,1,0:T(8,128)(2,1)} %pick_outgoing.1), calls=%async_computation | async-start | bytes 4325376 | tf_op jit(solution)/shard_map/all_to_all | solution.py:478
  20.9 100.3 %all-gather.2.cloned.1.call-start = ((), (), s32[]{:S(2)}) async-start(), calls=%async_computation.2 | async-start | bytes 6684672 | tf_op jit(solution)/shard_map/all_gather | solution.py:513
  23.8 2.4 %collective-permute-start = (bf16[1056,128]{1,0:T(8,128)(2,1)}, bf16[1056,128]{1,0:T(8,128)(2,1)S(1)}, u32[]{:S(2)}, u32[]{:S(2)}) collective-permute-start(bf16[1056,128]{1,0:T(8,128)(2,1)} %get-tuple-element.23), channel_id=1, source_target_pairs={{0,16},{16,0},{1,17},{17,1},{2,18},{18,2},{3,19},{19,3},{4,20},{20... | collective-permute-start | bytes 811016 | tf_op jit(solution)/shard_map/ppermute | solution.py:487
  26.3 9.2 %collective-permute-start.1 = (bf16[1056,128]{1,0:T(8,128)(2,1)S(1)}, bf16[1056,128]{1,0:T(8,128)(2,1)S(1)}, u32[]{:S(2)}, u32[]{:S(2)}) collective-permute-start(bf16[1056,128]{1,0:T(8,128)(2,1)S(1)} %get-tuple-element.43.refs_0_.iq_first), channel_id=1, source_target_pairs={{0,32},{32,64},{64,96},{96,0},{1,33},{33,65},{65,97},{97,1},{2,34}... | collective-permute-start | bytes 811016 | tf_op jit(solution)/shard_map/ppermute | solution.py:453
  27.6 7.8 %collective-permute-start.4 = (bf16[1056,128]{1,0:T(8,128)(2,1)S(1)}, bf16[1056,128]{1,0:T(8,128)(2,1)S(1)}, u32[]{:S(2)}, u32[]{:S(2)}) collective-permute-start(bf16[1056,128]{1,0:T(8,128)(2,1)S(1)} %get-tuple-element.42.refs_1_.iq_second), channel_id=1, source_target_pairs={{0,96},{32,0},{64,32},{96,64},{1,97},{33,1},{65,33},{97,65},{2,98}... | collective-permute-start | bytes 811016 | tf_op jit(solution)/shard_map/ppermute | solution.py:453
  29.1 12.6 %collective-permute-start.2 = (bf16[1056,128]{1,0:T(8,128)(2,1)S(1)}, bf16[1056,128]{1,0:T(8,128)(2,1)}, u32[]{:S(2)}, u32[]{:S(2)}) collective-permute-start(bf16[1056,128]{1,0:T(8,128)(2,1)S(1)} %get-tuple-element.42.refs_1_.iq_second), channel_id=1, source_target_pairs={{0,32},{32,64},{64,96},{96,0},{1,33},{33,65},{65,97},{97,1},{2,34}... | collective-permute-start | bytes 811016 | tf_op jit(solution)/shard_map/ppermute | solution.py:454
  29.1 12.6 %collective-permute-start.6 = (bf16[1056,128]{1,0:T(8,128)(2,1)S(1)}, bf16[1056,128]{1,0:T(8,128)(2,1)}, u32[]{:S(2)}, u32[]{:S(2)}) collective-permute-start(bf16[1056,128]{1,0:T(8,128)(2,1)S(1)} %get-tuple-element.43.refs_0_.iq_first), channel_id=1, source_target_pairs={{0,96},{32,0},{64,32},{96,64},{1,97},{33,1},{65,33},{97,65},{2,98}... | collective-permute-start | bytes 811016 | tf_op jit(solution)/shard_map/ppermute | solution.py:454
  35.5 11.6 %collective-permute-start.3 = (bf16[1056,128]{1,0:T(8,128)(2,1)S(1)}, bf16[1056,128]{1,0:T(8,128)(2,1)}, u32[]{:S(2)}, u32[]{:S(2)}) collective-permute-start(bf16[1056,128]{1,0:T(8,128)(2,1)S(1)} %collective-permute-done.1.refs_1_.refs_2_), channel_id=1, source_target_pairs={{0,32},{32,64},{64,96},{96,0},{1,33},{33,65},{65,97},{97,1},{2,34}... | collective-permute-start | bytes 811016 | tf_op jit(solution)/shard_map/ppermute | solution.py:455
  35.5 11.6 %collective-permute-start.5 = (bf16[1056,128]{1,0:T(8,128)(2,1)S(1)}, bf16[1056,128]{1,0:T(8,128)(2,1)}, u32[]{:S(2)}, u32[]{:S(2)}) collective-permute-start(bf16[1056,128]{1,0:T(8,128)(2,1)S(1)} %collective-permute-done.4.refs_6_.refs_7_), channel_id=1, source_target_pairs={{0,96},{32,0},{64,32},{96,64},{1,97},{33,1},{65,33},{97,65},{2,98}... | collective-permute-start | bytes 811016 | tf_op jit(solution)/shard_map/ppermute | solution.py:455
  39.9 44.3 %copy-start.7 = (s32[32]{0:T(128)S(1)}, s32[32]{0:T(128)}, u32[]{:S(2)}) copy-start(s32[32]{0:T(128)} %counts.3) | copy-start | bytes 388
  55.1 35.6 %collective-permute-start.13 = (bf16[16,576,128]{2,1,0:T(8,128)(2,1)S(1)}, bf16[16,576,128]{2,1,0:T(8,128)(2,1)S(1)}, u32[]{:S(2)}, u32[]{:S(2)}) collective-permute-start(bf16[16,576,128]{2,1,0:T(8,128)(2,1)S(1)} %dynamic-slice_bitcast_fusion.refs_0_), channel_id=1, source_target_pairs={{0,16},{16,0},{1,17},{17,1},{2,18},{18,2},{3,19},{19,3},{4,20},{20... | collective-permute-start | bytes 7077896 | tf_op jit(solution)/shard_map/ppermute | solution.py:494
  57.3 11.5 %collective-permute-start.7 = (bf16[8,176,128]{2,1,0:T(8,128)(2,1)}, bf16[8,176,128]{2,1,0:T(8,128)(2,1)S(1)}, u32[]{:S(2)}, u32[]{:S(2)}) collective-permute-start(bf16[8,176,128]{2,1,0:T(8,128)(2,1)} %get-tuple-element.24.own_low), channel_id=1, source_target_pairs={{0,32},{32,64},{64,96},{96,0},{1,33},{33,65},{65,97},{97,1},{2,34}... | collective-permute-start | bytes 1081352 | tf_op jit(solution)/shard_map/ppermute | solution.py:453
  58.6 10.2 %collective-permute-start.10 = (bf16[8,176,128]{2,1,0:T(8,128)(2,1)}, bf16[8,176,128]{2,1,0:T(8,128)(2,1)S(1)}, u32[]{:S(2)}, u32[]{:S(2)}) collective-permute-start(bf16[8,176,128]{2,1,0:T(8,128)(2,1)} %get-tuple-element.25.own_high), channel_id=1, source_target_pairs={{0,96},{32,0},{64,32},{96,64},{1,97},{33,1},{65,33},{97,65},{2,98}... | collective-permute-start | bytes 1081352 | tf_op jit(solution)/shard_map/ppermute | solution.py:453
  60.0 16.6 %collective-permute-start.8 = (bf16[8,176,128]{2,1,0:T(8,128)(2,1)}, bf16[8,176,128]{2,1,0:T(8,128)(2,1)S(1)}, u32[]{:S(2)}, u32[]{:S(2)}) collective-permute-start(bf16[8,176,128]{2,1,0:T(8,128)(2,1)} %get-tuple-element.25.own_high), channel_id=1, source_target_pairs={{0,32},{32,64},{64,96},{96,0},{1,33},{33,65},{65,97},{97,1},{2,34}... | collective-permute-start | bytes 1081352 | tf_op jit(solution)/shard_map/ppermute | solution.py:454
  60.1 16.6 %collective-permute-start.12 = (bf16[8,176,128]{2,1,0:T(8,128)(2,1)}, bf16[8,176,128]{2,1,0:T(8,128)(2,1)S(1)}, u32[]{:S(2)}, u32[]{:S(2)}) collective-permute-start(bf16[8,176,128]{2,1,0:T(8,128)(2,1)} %get-tuple-element.24.own_low), channel_id=1, source_target_pairs={{0,96},{32,0},{64,32},{96,64},{1,97},{33,1},{65,33},{97,65},{2,98}... | collective-permute-start | bytes 1081352 | tf_op jit(solution)/shard_map/ppermute | solution.py:454
  68.8 15.4 %collective-permute-start.9 = (bf16[8,176,128]{2,1,0:T(8,128)(2,1)S(1)}, bf16[8,176,128]{2,1,0:T(8,128)(2,1)S(1)}, u32[]{:S(2)}, u32[]{:S(2)}) collective-permute-start(bf16[8,176,128]{2,1,0:T(8,128)(2,1)S(1)} %collective-permute-done.7.a1), channel_id=1, source_target_pairs={{0,32},{32,64},{64,96},{96,0},{1,33},{33,65},{65,97},{97,1},{2,34}... | collective-permute-start | bytes 1081352 | tf_op jit(solution)/shard_map/ppermute | solution.py:455
  68.8 15.4 %collective-permute-start.11 = (bf16[8,176,128]{2,1,0:T(8,128)(2,1)S(1)}, bf16[8,176,128]{2,1,0:T(8,128)(2,1)S(1)}, u32[]{:S(2)}, u32[]{:S(2)}) collective-permute-start(bf16[8,176,128]{2,1,0:T(8,128)(2,1)S(1)} %collective-permute-done.10.b3), channel_id=1, source_target_pairs={{0,96},{32,0},{64,32},{96,64},{1,97},{33,1},{65,33},{97,65},{2,98}... | collective-permute-start | bytes 1081352 | tf_op jit(solution)/shard_map/ppermute | solution.py:455
  111.8 5.6 %collective-permute-start.14 = (bf16[528,128]{1,0:T(8,128)(2,1)S(1)}, bf16[528,128]{1,0:T(8,128)(2,1)S(1)}, u32[]{:S(2)}, u32[]{:S(2)}) collective-permute-start(bf16[528,128]{1,0:T(8,128)(2,1)S(1)} %get-tuple-element.29), channel_id=1, source_target_pairs={{0,32},{32,64},{64,96},{96,0},{1,33},{33,65},{65,97},{97,1},{2,34}... | collective-permute-start | bytes 405512 | tf_op jit(solution)/shard_map/ppermute | solution.py:550
  112.8 7.7 %collective-permute-start.15 = (bf16[528,128]{1,0:T(8,128)(2,1)S(1)}, bf16[528,128]{1,0:T(8,128)(2,1)S(1)}, u32[]{:S(2)}, u32[]{:S(2)}) collective-permute-start(bf16[528,128]{1,0:T(8,128)(2,1)S(1)} %get-tuple-element.30), channel_id=1, source_target_pairs={{0,64},{32,96},{64,0},{96,32},{1,65},{33,97},{65,1},{97,33},{2,66}... | collective-permute-start | bytes 405512 | tf_op jit(solution)/shard_map/ppermute | solution.py:550
  115.4 5.6 %collective-permute-start.16 = (bf16[528,128]{1,0:T(8,128)(2,1)S(1)}, bf16[528,128]{1,0:T(8,128)(2,1)S(1)}, u32[]{:S(2)}, u32[]{:S(2)}) collective-permute-start(bf16[528,128]{1,0:T(8,128)(2,1)S(1)} %get-tuple-element.31), channel_id=1, source_target_pairs={{0,96},{32,0},{64,32},{96,64},{1,97},{33,1},{65,33},{97,65},{2,98}... | collective-permute-start | bytes 405512 | tf_op jit(solution)/shard_map/ppermute | solution.py:550
  121.2 31.5 %collective-permute-start.20 = (bf16[4096,768]{1,0:T(8,128)(2,1)}, bf16[4096,768]{1,0:T(8,128)(2,1)S(1)}, u32[]{:S(2)}, u32[]{:S(2)}) collective-permute-start(bf16[4096,768]{1,0:T(8,128)(2,1)} %all-gather.2.cloned.1.call-done.xa), channel_id=1, source_target_pairs={{0,16},{16,0},{1,17},{17,1},{2,18},{18,2},{3,19},{19,3},{4,20},{20... | collective-permute-start | bytes 18874376 | tf_op jit(solution)/shard_map/ppermute | solution.py:560
  123.1 6.4 %collective-permute-start.17 = (bf16[528,128]{1,0:T(8,128)(2,1)S(1)}, bf16[528,128]{1,0:T(8,128)(2,1)S(1)}, u32[]{:S(2)}, u32[]{:S(2)}) collective-permute-start(bf16[528,128]{1,0:T(8,128)(2,1)S(1)} %loss.1.g0), channel_id=1, source_target_pairs={{0,32},{32,64},{64,96},{96,0},{1,33},{33,65},{65,97},{97,1},{2,34}... | collective-permute-start | bytes 405512 | tf_op jit(solution)/shard_map/ppermute | solution.py:460
  124.3 8.7 %collective-permute-start.18 = (bf16[528,128]{1,0:T(8,128)(2,1)S(1)}, bf16[528,128]{1,0:T(8,128)(2,1)S(1)}, u32[]{:S(2)}, u32[]{:S(2)}) collective-permute-start(bf16[528,128]{1,0:T(8,128)(2,1)S(1)} %loss.1.g0), channel_id=1, source_target_pairs={{0,64},{32,96},{64,0},{96,32},{1,65},{33,97},{65,1},{97,33},{2,66}... | collective-permute-start | bytes 405512 | tf_op jit(solution)/shard_map/ppermute | solution.py:460
  126.4 6.6 %collective-permute-start.19 = (bf16[528,128]{1,0:T(8,128)(2,1)S(1)}, bf16[528,128]{1,0:T(8,128)(2,1)S(1)}, u32[]{:S(2)}, u32[]{:S(2)}) collective-permute-start(bf16[528,128]{1,0:T(8,128)(2,1)S(1)} %loss.1.g0), channel_id=1, source_target_pairs={{0,96},{32,0},{64,32},{96,64},{1,97},{33,1},{65,33},{97,65},{2,98}... | collective-permute-start | bytes 405512 | tf_op jit(solution)/shard_map/ppermute | solution.py:460
  157.9 9.7 %collective-permute-start.21 = (bf16[64,1536]{1,0:T(8,128)(2,1)S(1)}, bf16[64,1536]{1,0:T(8,128)(2,1)S(1)}, u32[]{:S(2)}, u32[]{:S(2)}) collective-permute-start(bf16[64,1536]{1,0:T(8,128)(2,1)S(1)} %weight_piece.1.p0), channel_id=1, source_target_pairs={{0,9},{1,10},{2,11},{3,8},{4,13},{5,14},{6,15},{7,12},{8,1},{9,2},... | collective-permute-start | bytes 589832 | tf_op jit(solution)/shard_map/ppermute | solution.py:594
  159.3 9.9 %collective-permute-start.22 = (bf16[64,1536]{1,0:T(8,128)(2,1)S(1)}, bf16[64,1536]{1,0:T(8,128)(2,1)S(1)}, u32[]{:S(2)}, u32[]{:S(2)}) collective-permute-start(bf16[64,1536]{1,0:T(8,128)(2,1)S(1)} %weight_piece.1.p0), channel_id=1, source_target_pairs={{0,2},{1,3},{2,0},{3,1},{4,6},{5,7},{6,4},{7,5},{8,10},{9,11},{10,... | collective-permute-start | bytes 589832 | tf_op jit(solution)/shard_map/ppermute | solution.py:594
  160.4 11.7 %collective-permute-start.23 = (bf16[64,1536]{1,0:T(8,128)(2,1)S(1)}, bf16[64,1536]{1,0:T(8,128)(2,1)S(1)}, u32[]{:S(2)}, u32[]{:S(2)}) collective-permute-start(bf16[64,1536]{1,0:T(8,128)(2,1)S(1)} %weight_piece.1.p0), channel_id=1, source_target_pairs={{0,11},{1,8},{2,9},{3,10},{4,15},{5,12},{6,13},{7,14},{8,3},{9,0},... | collective-permute-start | bytes 589832 | tf_op jit(solution)/shard_map/ppermute | solution.py:594
  172.4 20.7 %collective-permute-start.26 = (bf16[1536,256]{1,0:T(8,128)(2,1)S(1)}, bf16[1536,256]{1,0:T(8,128)(2,1)S(1)}, u32[]{:S(2)}, u32[]{:S(2)}) collective-permute-start(bf16[1536,256]{1,0:T(8,128)(2,1)S(1)} %get-tuple-element.38.refs_0_), channel_id=1, source_target_pairs={{0,4},{1,5},{2,6},{3,7},{4,8},{5,9},{6,10},{7,11},{8,12},{9,13},{1... | collective-permute-start | bytes 2359304 | tf_op jit(solution)/shard_map/ppermute | solution.py:603
  173.5 19.6 %collective-permute-start.27 = (bf16[1536,256]{1,0:T(8,128)(2,1)S(1)}, bf16[1536,256]{1,0:T(8,128)(2,1)S(1)}, u32[]{:S(2)}, u32[]{:S(2)}) collective-permute-start(bf16[1536,256]{1,0:T(8,128)(2,1)S(1)} %get-tuple-element.38.refs_0_), channel_id=1, source_target_pairs={{0,12},{1,13},{2,14},{3,15},{4,0},{5,1},{6,2},{7,3},{8,4},{9,5},{1... | collective-permute-start | bytes 2359304 | tf_op jit(solution)/shard_map/ppermute | solution.py:604
  175.2 4.5 %collective-permute-start.28 = (f32[8,128]{1,0:T(8,128)S(1)}, f32[8,128]{1,0:T(8,128)S(1)}, u32[]{:S(2)}, u32[]{:S(2)}) collective-permute-start(f32[8,128]{1,0:T(8,128)S(1)} %get-tuple-element.41), channel_id=1, source_target_pairs={{0,16},{16,0},{1,17},{17,1},{2,18},{18,2},{3,19},{19,3},{4,20},{20... | collective-permute-start | bytes 12296 | tf_op jit(solution)/shard_map/ppermute | solution.py:571
  177.5 10.7 %collective-permute-start.24 = (bf16[768,256]{1,0:T(8,128)(2,1)S(1)}, bf16[768,256]{1,0:T(8,128)(2,1)S(1)}, u32[]{:S(2)}, u32[]{:S(2)}) collective-permute-start(bf16[768,256]{1,0:T(8,128)(2,1)S(1)} %get-tuple-element.39), channel_id=1, source_target_pairs={{0,3},{1,0},{2,1},{3,2},{4,7},{5,4},{6,5},{7,6},{8,11},{9,8},{10,9... | collective-permute-start | bytes 1179656 | tf_op jit(solution)/shard_map/ppermute | solution.py:605
  179.7 11.6 %collective-permute-start.25 = (bf16[768,256]{1,0:T(8,128)(2,1)S(1)}, bf16[768,256]{1,0:T(8,128)(2,1)S(1)}, u32[]{:S(2)}, u32[]{:S(2)}) collective-permute-start(bf16[768,256]{1,0:T(8,128)(2,1)S(1)} %get-tuple-element.40), channel_id=1, source_target_pairs={{0,1},{1,2},{2,3},{3,0},{4,5},{5,6},{6,7},{7,4},{8,9},{9,10},{10,1... | collective-permute-start | bytes 1179656 | tf_op jit(solution)/shard_map/ppermute | solution.py:606
  (7 other events, 142.7 us)
Sparse Core Ops, SparseCore 0:
  55.2 61.0 all-gather.1
